TPU v7x, 32 devices: a whole 2x2x4 slice. The times are simulated.
32 devices in a mesh: seq: 4 (over y, x), fsdp: 8 (over z, core).
Axes of the slice: x: 2, y: 2, z: 4, core: 2. Of those that a mesh axis runs over, the one named last changes fastest.
Arguments:
- resid_in: float32 [16, 1024, 2048], P('fsdp', 'seq'), may hold values from -6 to 6
- qkv_weight: float32 [6144, 2048], P('fsdp'), may hold values from -0.125 to 0.125
- qkv_bias: float32 [6144], P('fsdp'), may hold values from -2 to 2
- out_weight: float32 [2048, 2048], P('fsdp'), may hold values from -1 to 1
- out_bias: float32 [2048], P('fsdp'), may hold values from -2 to 2
- up_weight: float32 [8192, 2048], P('fsdp'), may hold values from -0.125 to 0.125
- up_bias: float32 [8192], P('fsdp'), may hold values from -3 to 3
- down_weight: float32 [8192, 2048], P('fsdp'), may hold values from -0.0625 to 0.0625
- down_bias: float32 [2048], P('fsdp'), may hold values from -2 to 2
- attn_gain: float32 [2048], P('fsdp'), may hold values from 0.5 to 1.5
- attn_shift: float32 [2048], P('fsdp'), may hold values from -1.2 to 1.2
- mlp_gain: float32 [2048], P('fsdp'), may hold values from 0.5 to 1.5
- mlp_shift: float32 [2048], P('fsdp'), may hold values from -1.2 to 1.2
- block_ids: int32 [16, 1024], P('fsdp'), may hold values from 0 to 7, never falling along the last dimension, each value on 1 to 256 neighbouring positions
- offsets: int32 [16, 8], P('fsdp'), may hold values from 0 to 4095
- grad_out: float32 [16, 1024, 2048], P('fsdp', 'seq'), may hold values from -6 to 6
Outputs:
- resid_out: float32 [16, 1024, 2048], P('fsdp', 'seq')
- grad_in: float32 [16, 1024, 2048], P('fsdp', 'seq')
- qkv_weight_grad: float32 [6144, 2048], P('fsdp')
- qkv_bias_grad: float32 [4096], P('fsdp')
- value_bias_grad: float32 [2048], P('fsdp')
- out_weight_grad: float32 [2048, 2048], P('fsdp')
- out_bias_grad: float32 [2048], P('fsdp')
- up_weight_grad: float32 [8192, 2048], P('fsdp')
- up_bias_grad: float32 [8192], P('fsdp')
- down_weight_grad: float32 [8192, 2048], P('fsdp')
- down_bias_grad: float32 [2048], P('fsdp')
- attn_gain_grad: float32 [2048], P('fsdp')
- attn_shift_grad: float32 [2048], P('fsdp')
- mlp_gain_grad: float32 [2048], P('fsdp')
- mlp_shift_grad: float32 [2048], P('fsdp')
Inputs may be any that keep to these rules, and one draw needn't show every extreme that they name: `block_ids`: along each sequence the block numbers never fall; every block holds 1 to 256 tokens and one block exactly 256.
All inputs are finite; a program needn't handle non-finite values.
Results may differ from a plain program's by a relative error of at most 0.012.
The roundings to bfloat16 on the way count: a program that leaves them out, or rounds other values in their place, can miss the bound.
Values may be sent and summed in bfloat16 or wider, within the bound.
A program may use at most 576 MiB of HBM per device.

v0:
```python
import math

import jax
import jax.numpy as jnp
from jax import lax
from jax.sharding import PartitionSpec as P

HEADS = 8
HEAD_DIM = 256
ROT_DIM = 64


EPS = 1e-05
NEG_FILL = -1e30


def layer_norm(values, gain, shift):
    center = values - jnp.mean(values, axis=-1, keepdims=True)
    spread = jnp.mean(center * center, axis=-1, keepdims=True)
    return center * lax.rsqrt(spread + EPS) * gain + shift


def rotary_tables(positions):
    half = ROT_DIM // 2
    inverse = jnp.exp(jnp.arange(half, dtype=jnp.float32) * (-2.0 * math.log(10000.0) / ROT_DIM))
    angles = positions.astype(jnp.float32)[..., None] * inverse
    return (jnp.cos(angles), jnp.sin(angles))


def block_offset(ids, starts):
    numbers = jnp.arange(starts.shape[1], dtype=jnp.int32)
    match = (ids[:, :, None] == numbers[None, None, :]).astype(jnp.int32)
    return jnp.sum(match * starts[:, None, :], axis=-1)


def rotate(values, cosine, sine):
    half = ROT_DIM // 2
    cosine = cosine[..., None, :]
    sine = sine[..., None, :]
    first = values[..., :half]
    second = values[..., half:ROT_DIM]
    return jnp.concatenate(
        [first * cosine - second * sine, second * cosine + first * sine, values[..., ROT_DIM:]],
        axis=-1,
    )


def gelu_exact(values):
    return jax.nn.gelu(values, approximate=False)


def contract_lead(left, right):
    return lax.dot_general(
        left, right, (((0,), (0,)), ((), ())), preferred_element_type=jnp.float32
    )


def contract_last(left, right):
    return lax.dot_general(
        left, right, (((1,), (1,)), ((), ())), preferred_element_type=jnp.float32
    )


def attend_forward(items):
    query, keys, values, ids = items
    allowed = ids[None, :] <= ids[:, None]
    scores = jnp.where(allowed, contract_last(query, keys) * HEAD_DIM ** (-0.5), NEG_FILL)
    top = jnp.max(scores, axis=1, keepdims=True)
    weights = jnp.exp(scores - top)
    total = jnp.sum(weights, axis=1, keepdims=True)
    probs = (weights / total).astype(jnp.bfloat16)
    mixed = jnp.dot(probs, values, preferred_element_type=jnp.float32).astype(jnp.bfloat16)
    return (mixed, (top + jnp.log(total))[:, 0])


def attend_backward(items):
    query, keys, values, ids, lse_row, grad_mix = items
    scale = HEAD_DIM ** (-0.5)
    allowed = ids[None, :] <= ids[:, None]
    scores = contract_last(query, keys) * scale
    probs = jnp.where(allowed, jnp.exp(scores - lse_row[:, None]), 0.0)
    grad_probs = contract_last(grad_mix, values)
    inner = jnp.sum(probs * grad_probs, axis=1, keepdims=True)
    grad_scores = (probs * (grad_probs - inner)).astype(jnp.bfloat16)
    grad_query = (jnp.dot(grad_scores, keys, preferred_element_type=jnp.float32) * scale).astype(
        jnp.bfloat16
    )
    grad_keys = (contract_lead(grad_scores, query) * scale).astype(jnp.bfloat16)
    grad_values = contract_lead(probs.astype(jnp.bfloat16), grad_mix).astype(jnp.bfloat16)
    return (grad_query, grad_keys, grad_values)


def body(
    resid_in,
    qkv_weight,
    qkv_bias,
    out_weight,
    out_bias,
    up_weight,
    up_bias,
    down_weight,
    down_bias,
    attn_gain,
    attn_shift,
    mlp_gain,
    mlp_shift,
    block_ids,
    offsets,
    grad_out,
):
    groups, piece, width = resid_in.shape
    tokens = groups * piece
    pieces = lax.axis_size("seq")
    length = piece * pieces
    rank = lax.axis_index("fsdp")
    heads_here = HEADS // pieces
    pairs = groups * heads_here
    flat = resid_in.reshape(tokens, width)
    gain_a, shift_a, gain_m, shift_m, proj_bias, attn_bias, hidden_bias, mlp_bias = (
        lax.all_gather(attn_gain, "fsdp", axis=0, tiled=True),
        lax.all_gather(attn_shift, "fsdp", axis=0, tiled=True),
        lax.all_gather(mlp_gain, "fsdp", axis=0, tiled=True),
        lax.all_gather(mlp_shift, "fsdp", axis=0, tiled=True),
        lax.all_gather(qkv_bias, "fsdp", axis=0, tiled=True),
        lax.all_gather(out_bias, "fsdp", axis=0, tiled=True),
        lax.all_gather(up_bias, "fsdp", axis=0, tiled=True),
        lax.all_gather(down_bias, "fsdp", axis=0, tiled=True),
    )
    qkv_low = qkv_weight.astype(jnp.bfloat16)
    out_low = out_weight.astype(jnp.bfloat16)
    up_low = up_weight.astype(jnp.bfloat16)
    down_low = down_weight.astype(jnp.bfloat16)
    qkv_full, out_full = (
        lax.all_gather(qkv_low, "fsdp", axis=0, tiled=True),
        lax.all_gather(out_low, "fsdp", axis=0, tiled=True),
    )
    normed_a32, norm_back_a = jax.vjp(layer_norm, flat, gain_a, shift_a)
    normed_m32, norm_back_m = jax.vjp(layer_norm, flat, gain_m, shift_m)
    normed_attn = normed_a32.astype(jnp.bfloat16)
    normed_mlp = normed_m32.astype(jnp.bfloat16)
    projected = (contract_last(normed_attn, qkv_full) + proj_bias).reshape(
        groups, piece, 3, HEADS, HEAD_DIM
    )
    first_pos = lax.axis_index("seq") * piece
    ids_piece = lax.dynamic_slice_in_dim(block_ids, first_pos, piece, 1)
    positions = (
        block_offset(ids_piece, offsets) + first_pos + jnp.arange(piece, dtype=jnp.int32)[None, :]
    )
    cosine, sine = rotary_tables(positions)
    query = rotate(projected[:, :, 0], cosine, sine)
    keys = rotate(projected[:, :, 1], cosine, sine)
    packed = jnp.stack([query, keys, projected[:, :, 2]], axis=2).astype(jnp.bfloat16)
    heads = lax.all_to_all(packed, "seq", split_axis=3, concat_axis=1, tiled=True)
    stacked = heads.transpose(2, 0, 3, 1, 4).reshape(3, pairs, length, HEAD_DIM)
    ids_pairs = jnp.repeat(block_ids, heads_here, axis=0)
    mixed_pairs, lse_pairs = lax.map(
        attend_forward, (stacked[0], stacked[1], stacked[2], ids_pairs)
    )
    back_heads = mixed_pairs.reshape(groups, heads_here, length, HEAD_DIM).transpose(0, 2, 1, 3)
    mixed_tok = lax.all_to_all(back_heads, "seq", split_axis=1, concat_axis=2, tiled=True).reshape(
        tokens, width
    )
    attn_part = jnp.dot(mixed_tok, out_full, preferred_element_type=jnp.float32) + attn_bias
    units_here = up_weight.shape[0]
    group_rows = lax.all_gather(normed_mlp, "fsdp", axis=0, tiled=True)
    local_bias = lax.dynamic_slice_in_dim(hidden_bias, rank * units_here, units_here)
    hidden = contract_last(group_rows, up_low) + local_bias
    active, gelu_back = jax.vjp(gelu_exact, hidden)
    active_low = active.astype(jnp.bfloat16)
    branch = (
        lax.psum_scatter(
            jnp.dot(active_low, down_low, preferred_element_type=jnp.float32).astype(jnp.bfloat16),
            "fsdp",
            scatter_dimension=0,
            tiled=True,
        ).astype(jnp.float32)
        + mlp_bias
    )
    result = flat + attn_part + branch
    grad_flat = grad_out.reshape(tokens, width)
    grad_low = grad_flat.astype(jnp.bfloat16)
    bias_sum = jnp.sum(grad_flat, axis=0)
    group_grad = lax.all_gather(grad_low, "fsdp", axis=0, tiled=True)
    grad_active = contract_last(group_grad, down_low).astype(jnp.bfloat16)
    grad_hidden = gelu_back(grad_active.astype(jnp.float32))[0]
    grad_hidden_low = grad_hidden.astype(jnp.bfloat16)
    grad_normed_m = lax.psum_scatter(
        jnp.dot(grad_hidden_low, up_low, preferred_element_type=jnp.float32),
        "fsdp",
        scatter_dimension=0,
        tiled=True,
    )
    up_grad_shard = contract_lead(grad_hidden_low, group_rows)
    down_grad_shard = contract_lead(active_low, group_grad)
    local_sum = jnp.sum(grad_hidden, axis=0)
    up_bias_term = lax.dynamic_update_slice_in_dim(
        jnp.zeros((hidden_bias.shape[0],), jnp.float32), local_sum, rank * units_here, 0
    )
    grad_mixed = contract_last(grad_low, out_full).astype(jnp.bfloat16)
    grad_heads = lax.all_to_all(
        grad_mixed.reshape(groups, piece, HEADS, HEAD_DIM),
        "seq",
        split_axis=2,
        concat_axis=1,
        tiled=True,
    )
    grad_pairs = grad_heads.transpose(0, 2, 1, 3).reshape(pairs, length, HEAD_DIM)
    grad_query, grad_keys, grad_values = lax.map(
        attend_backward, (stacked[0], stacked[1], stacked[2], ids_pairs, lse_pairs, grad_pairs)
    )
    grads_stack = (
        jnp.stack([grad_query, grad_keys, grad_values], axis=0)
        .reshape(3, groups, heads_here, length, HEAD_DIM)
        .transpose(1, 3, 0, 2, 4)
    )
    returned = lax.all_to_all(grads_stack, "seq", split_axis=1, concat_axis=3, tiled=True).astype(
        jnp.float32
    )
    grad_projected = jnp.stack(
        [
            rotate(returned[:, :, 0], cosine, -sine),
            rotate(returned[:, :, 1], cosine, -sine),
            returned[:, :, 2],
        ],
        axis=2,
    ).reshape(tokens, 3 * width)
    grad_projected_low = grad_projected.astype(jnp.bfloat16)
    proj_bias_term = jnp.sum(grad_projected, axis=0)
    qk_bias_term = proj_bias_term[: 2 * width]
    value_bias_term = proj_bias_term[2 * width :]
    grad_normed_a = jnp.dot(grad_projected_low, qkv_full, preferred_element_type=jnp.float32)
    grad_from_a, gain_a_term, shift_a_term = norm_back_a(grad_normed_a)
    grad_from_m, gain_m_term, shift_m_term = norm_back_m(grad_normed_m)
    grad_input = grad_flat + grad_from_a + grad_from_m
    qkv_term = contract_lead(grad_projected_low, normed_attn)
    out_term = contract_lead(mixed_tok, grad_low)
    (
        qkv_shard,
        out_shard,
        qk_bias_shard,
        value_bias_shard,
        bias_shard,
        up_bias_shard,
        gain_a_shard,
        shift_a_shard,
        gain_m_shard,
        shift_m_shard,
    ) = (
        lax.psum_scatter(qkv_term, "fsdp", scatter_dimension=0, tiled=True),
        lax.psum_scatter(out_term, "fsdp", scatter_dimension=0, tiled=True),
        lax.psum_scatter(qk_bias_term, "fsdp", scatter_dimension=0, tiled=True),
        lax.psum_scatter(value_bias_term, "fsdp", scatter_dimension=0, tiled=True),
        lax.psum_scatter(bias_sum, "fsdp", scatter_dimension=0, tiled=True),
        lax.psum_scatter(up_bias_term, "fsdp", scatter_dimension=0, tiled=True),
        lax.psum_scatter(gain_a_term, "fsdp", scatter_dimension=0, tiled=True),
        lax.psum_scatter(shift_a_term, "fsdp", scatter_dimension=0, tiled=True),
        lax.psum_scatter(gain_m_term, "fsdp", scatter_dimension=0, tiled=True),
        lax.psum_scatter(shift_m_term, "fsdp", scatter_dimension=0, tiled=True),
    )
    totals = lax.psum(
        (
            qkv_shard,
            out_shard,
            up_grad_shard,
            down_grad_shard,
            qk_bias_shard,
            value_bias_shard,
            bias_shard,
            up_bias_shard,
            gain_a_shard,
            shift_a_shard,
            gain_m_shard,
            shift_m_shard,
        ),
        "seq",
    )
    return (
        result.reshape(groups, piece, width),
        grad_input.reshape(groups, piece, width),
        totals[0],
        totals[4],
        totals[5],
        totals[1],
        totals[6],
        totals[2],
        totals[7],
        totals[3],
        totals[6],
        totals[8],
        totals[9],
        totals[10],
        totals[11],
    )


def solution(mesh):
    placed = (
        P("fsdp", "seq", None),
        P("fsdp", None),
        P("fsdp"),
        P("fsdp", None),
        P("fsdp"),
        P("fsdp", None),
        P("fsdp"),
        P("fsdp", None),
        P("fsdp"),
        P("fsdp"),
        P("fsdp"),
        P("fsdp"),
        P("fsdp"),
        P("fsdp", None),
        P("fsdp", None),
        P("fsdp", "seq", None),
    )
    return jax.shard_map(
        body,
        mesh=mesh,
        in_specs=placed,
        out_specs=(
            P("fsdp", "seq", None),
            P("fsdp", "seq", None),
            P("fsdp", None),
            P("fsdp"),
            P("fsdp"),
            P("fsdp", None),
            P("fsdp"),
            P("fsdp", None),
            P("fsdp"),
            P("fsdp", None),
            P("fsdp"),
            P("fsdp"),
            P("fsdp"),
            P("fsdp"),
            P("fsdp"),
        ),
        check_vma=False,
    )
```

profile of v0, /device:TPU:0, one launch (start us, length us, event | category | flops | bytes accessed | tf_op | source)
XLA Modules:
  0.0 2343.4 jit_solution(12414266780866556832)
XLA Ops:
  86.3 122.4 %all-gather.16.cloned.1.call-done = bf16[4096,2048]{1,0:T(8,128)(2,1)} async-done(((bf16[512,2048]{1,0:T(8,128)(2,1)}), bf16[4096,2048]{1,0:T(8,128)(2,1)}) %all-gather.16.cloned.1.call-update) | async-done | bytes 16777232 | tf_op jit(solution)/shard_map/all_gather | solution.py:165
  208.7 59.7 %multiply_convert_fusion.1 = (bf16[4096,1024]{1,0:T(8,128)(2,1)}, f32[4096,1024]{1,0:T(8,128)}, f32[4096,1024]{1,0:T(8,128)}) fusion(f32[1024]{0:T(1024)S(1)} %dynamic_slice.40, bf16[4096,2048]{1,0:T(8,128)(2,1)} %all-gather.16.cloned.1.call-done, f32[1024,2048]{1,0:T(8,128)} %param.25), kind=kOutput, calls=%fused_computation.70 | convolution fusion | flops 17458790400 | bytes 67112960 | tf_op jit(solution)/shard_map/dot_general | solution.py:59
  268.4 91.2 %all-gather.18.cloned.1.call-done = bf16[4096,2048]{1,0:T(8,128)(2,1)} async-done(((bf16[512,2048]{1,0:T(8,128)(2,1)}), bf16[4096,2048]{1,0:T(8,128)(2,1)}) %all-gather.18.cloned.1.call-update) | async-done | bytes 16777232 | tf_op jit(solution)/shard_map/all_gather | solution.py:183
  359.7 34.2 %fusion.89 = (f32[1024]{0:T(1024)}, bf16[4096,1024]{1,0:T(8,128)(2,1)}) fusion(f32[4096,1024]{1,0:T(8,128)} %get-tuple-element.179, bf16[4096,2048]{1,0:T(8,128)(2,1)} %all-gather.18.cloned.1.call-done, f32[1024,2048]{1,0:T(8,128)} %param.27, f32[4096,1024]{1,0:T(8,128)} %get-tuple-element.220, f32[1024]{0:T(1024)S(1)} %dynamic_slice.40), kind=kOutput, calls=%fused_computation.162 | convolution fusion | flops 17257463808 | bytes 67117056 | tf_op jit(solution)/shard_map/dot_general | solution.py:59
  393.9 26.9 %fusion.72 = f32[4096,2048]{1,0:T(8,128)} fusion(bf16[4096,1024]{1,0:T(8,128)(2,1)} %get-tuple-element.223, f32[1024,2048]{1,0:T(8,128)} %param.25), kind=kOutput, calls=%fused_computation.114 | convolution fusion | flops 17181966336 | bytes 50331648 | tf_op jit(solution)/shard_map/dot_general | solution.py:188
  421.5 22.4 all-gather.2
  445.8 134.4 %all-gather.12.cloned.1.call-done = bf16[6144,2048]{1,0:T(8,128)(2,1)} async-done(((bf16[768,2048]{1,0:T(8,128)(2,1)}), bf16[6144,2048]{1,0:T(8,128)(2,1)}) %all-gather.12.cloned.1.call-update) | async-done | bytes 25165840 | tf_op jit(solution)/shard_map/all_gather | solution.py:134
  580.2 19.6 convolution_add_fusion
  640.1 70.4 %all-to-all-done = bf16[2,256,3,8,256]{4,1,0,2,3:T(8,128)(2,1)} async-done(((bf16[2,256,3,8,256]{4,1,0,2,3:T(8,128)(2,1)}), bf16[2,256,3,8,256]{4,1,0,2,3:T(8,128)(2,1)}, u32[]{:S(2)}, u32[]{:S(2)}) %all-to-all-start) | async-done | bytes 6291488 | tf_op jit(solution)/shard_map/all_to_all | solution.py:153
  717.6 22.1 while.26
  744.2 28.2 %all_to_all.60 = bf16[2,1024,2,256]{3,2,0,1:T(2,128)(2,1)S(1)} all-to-all(bf16[2,1024,2,256]{3,2,0,1:T(2,128)(2,1)S(1)} %bitcast.248), channel_id=1, replica_groups=mesh['seq'=4,'fsdp'=8] {'seq'}, dimensions={1} | all-to-all | bytes 4194304 | tf_op jit(solution)/shard_map/all_to_all | solution.py:160
  801.2 26.8 %all_to_all.61 = bf16[2,256,8,256]{3,1,0,2:T(8,128)(2,1)S(1)} all-to-all(bf16[2,256,8,256]{3,1,0,2:T(8,128)(2,1)S(1)} %copy.108), channel_id=1, replica_groups=mesh['seq'=4,'fsdp'=8] {'seq'}, dimensions={2} | all-to-all | bytes 4194304 | tf_op jit(solution)/shard_map/all_to_all | solution.py:200
  832.6 38.6 %while.27 = (s32[]{:T(128)}, bf16[4,1024,256]{2,1,0:T(8,128)(2,1)}, bf16[4,1024,256]{2,1,0:T(8,128)(2,1)}, bf16[4,1024,256]{2,1,0:T(8,128)(2,1)}, s32[4,1024]{1,...) while((s32[]{:T(128)}, bf16[4,1024,256]{2,1,0:T(8,128)(2,1)}, ...), condition=%wide.region_10.11_spmd, body=%wide.region_8.10_spmd.sunk | while | flops 2696150016 | bytes 53519540 | solution.py:208
  899.5 62.7 %all-to-all-done.3 = bf16[2,1024,3,2,256]{4,3,0,2,1:T(2,128)(2,1)} async-done(((bf16[2,1024,3,2,256]{4,3,0,2,1:T(2,128)(2,1)}), bf16[2,1024,3,2,256]{4,3,0,2,1:T(2,128)(2,1)}, u32[]{:S(2)}, u32[]{:S(2)}) %all-to-all-start.3) | async-done | bytes 6291488 | tf_op jit(solution)/shard_map/all_to_all | solution.py:216
  1024.6 22.8 fusion.90
  1047.5 24.8 %convolution_convert_fusion = bf16[4096,2048]{1,0:T(8,128)(2,1)} fusion(bf16[4096,1024]{1,0:T(8,128)(2,1)} %get-tuple-element.178, f32[1024,2048]{1,0:T(8,128)} %param.27), kind=kOutput, calls=%fused_computation.84 | convolution fusion | flops 17190354944 | bytes 33554432 | tf_op jit(solution)/shard_map/dot_general | solution.py:172
  1073.5 24.6 %fusion.92 = f32[1024,2048]{1,0:T(8,128)} fusion(bf16[4096,1024]{1,0:T(8,128)(2,1)} %get-tuple-element.178, bf16[4096,2048]{1,0:T(8,128)(2,1)} %all-gather.18.cloned.1.call-done), kind=kOutput, calls=%fused_computation.165 | convolution fusion | flops 17179869184 | bytes 33554432 | tf_op jit(solution)/shard_map/dot_general | solution.py:53
  1100.5 25.0 %multiply_reduce_fusion.1 = (f32[2048]{0:T(1024)}, f32[512]{0:T(512)S(1)}, f32[512]{0:T(512)S(1)}, f32[2048]{0:T(1024)}, f32[2048]{0:T(1024)}, /*index=5*/f32[2048]{0:T(1024)}, f32[512,2048]{1,0:T(8,128)}) fusion(f32[512,2048]{1,0:T(8,128)} %reduce-scatter.7.cloned.1.call-done, f32[2,256,2048]{2,1,0:T(8,128)} %param.20, f32[512]{0:T(512)S(1)} %copy-done.40, ...), kind=kOutput, calls=%fused_computation.108 | convolution fusion | flops 12899573760 | bytes 44097536 | tf_op jit(solution)/shard_map/dot_general | solution.py:231
  1125.6 24.5 %fusion.70 = f32[1024,2048]{1,0:T(8,128)} fusion(bf16[4096,2048]{1,0:T(8,128)(2,1)} %all-gather.16.cloned.1.call-done, bf16[4096,1024]{1,0:T(8,128)(2,1)} %get-tuple-element.223), kind=kOutput, calls=%fused_computation.112 | convolution fusion | flops 17179869184 | bytes 33554432 | tf_op jit(solution)/shard_map/dot_general | solution.py:53
  1157.2 484.0 %reduce-scatter.9.cloned.1.call-done = f32[768,2048]{1,0:T(8,128)} async-done(((f32[6144,2048]{1,0:T(8,128)}), f32[768,2048]{1,0:T(8,128)}) %reduce-scatter.9.cloned.1.call-update) | async-done | bytes 6291472 | tf_op jit(solution)/shard_map/reduce_scatter | solution.py:249
  1663.2 147.1 %reduce-scatter.5.cloned.1.call-done = bf16[512,2048]{1,0:T(8,128)(2,1)} async-done(((bf16[4096,2048]{1,0:T(8,128)(2,1)}), bf16[512,2048]{1,0:T(8,128)(2,1)}) %reduce-scatter.5.cloned.1.call-update) | async-done | bytes 2097168 | tf_op jit(solution)/shard_map/reduce_scatter | solution.py:171
  1826.7 37.5 %all-reduce.14.cloned.1.call-done = (f32[4096]{0:T(1024)}, f32[2048]{0:T(1024)}, f32[2048]{0:T(1024)}, f32[8192]{0:T(1024)}, f32[2048]{0:T(1024)}, /*index=5*/f32[2048]{0:T(1024)}, f32[2048]{0:T(1024)}, f32[2048]{0:T(1024)}) async-done(((f32[4096]{0:T(1024)}, f32[2048]{0:T(1024)}, f32[2048]{0:T(1024)}, f32[8192]{0:T(1024)}, f32[2048]{0:T(1024)}, /*index=5*/f32[2048]{0:T(1024)}, f32[2048]{0:T(1024)}, ...) | async-done | bytes 98320
  1870.1 16.9 all-reduce.9
  1887.1 430.8 %all-reduce.16.cloned.1.call-done = (f32[768,2048]{1,0:T(8,128)}, f32[256,2048]{1,0:T(8,128)}, f32[1024,2048]{1,0:T(8,128)}, f32[1024,2048]{1,0:T(8,128)}) async-done(((f32[768,2048]{1,0:T(8,128)}, f32[256,2048]{1,0:T(8,128)}, f32[1024,2048]{1,0:T(8,128)}, f32[1024,2048]{1,0:T(8,128)}), (f32[768,2048]{1,0:T(8,128)}, f32[256,2048]{1,0:T(8,128)}, f32[1024,2048]{1,0:T(8,128)}, ...) | async-done | bytes 25165840 | tf_op jit(solution)/shard_map/psum | solution.py:260
  (304 shorter events, 388.5 us)
Async XLA Ops:
  7.2 38.3 %copy-start.49 = (f32[256]{0:T(256)S(1)}, f32[256]{0:T(256)}, u32[]{:S(2)}) copy-start(f32[256]{0:T(256)} %param.32) | copy-start | bytes 3076
  7.2 201.5 %all-gather.16.cloned.1.call-start = ((), (), s32[]{:S(2)}) async-start(), calls=%async_computation.10 | async-start | bytes 18874368 | tf_op jit(solution)/shard_map/all_gather | solution.py:165
  9.7 44.5 %copy-start = (f32[2,256,2048]{2,1,0:T(8,128)S(1)}, f32[2,256,2048]{2,1,0:T(8,128)}, u32[]{:S(2)}) copy-start(f32[2,256,2048]{2,1,0:T(8,128)} %param.20) | copy-start | bytes 12582916
  9.8 35.8 %copy-start.33 = (f32[2,256]{1,0:T(2,128)}, f32[2,256]{1,0:T(2,128)S(1)}, u32[]{:S(2)}) copy-start(f32[2,256]{1,0:T(2,128)S(1)} %get-tuple-element.219) | copy-start | bytes 6148
  9.8 48.0 %copy-start.37 = (f32[1,2,2,128]{3,1,2,0:T(2,128)}, f32[1,2,2,128]{3,1,2,0:T(2,128)S(1)}, u32[]{:S(2)}) copy-start(f32[1,2,2,128]{3,1,2,0:T(2,128)S(1)} %copy.125) | copy-start | bytes 6148
  13.3 32.3 %copy-start.35 = (f32[1,2,2,128]{3,1,2,0:T(2,128)}, f32[1,2,2,128]{3,1,2,0:T(2,128)S(1)}, u32[]{:S(2)}) copy-start(f32[1,2,2,128]{3,1,2,0:T(2,128)S(1)} %copy.126) | copy-start | bytes 6148
  13.3 44.5 %copy-start.39 = (f32[512]{0:T(512)}, f32[512]{0:T(512)S(1)}, u32[]{:S(2)}) copy-start(f32[512]{0:T(512)S(1)} %rsqrt.16) | copy-start | bytes 6148
  26.7 31.1 %copy-start.27 = (f32[8,1,256]{2,1,0:T(1,128)}, f32[8,1,256]{2,1,0:T(1,128)S(1)}, u32[]{:S(2)}) copy-start(f32[8,1,256]{2,1,0:T(1,128)S(1)} %all-gather) | copy-start | bytes 24580
  57.9 301.8 %all-gather.18.cloned.1.call-start = ((), (), s32[]{:S(2)}) async-start(), calls=%async_computation.12 | async-start | bytes 18874368 | tf_op jit(solution)/shard_map/all_gather | solution.py:183
  64.8 515.4 %all-gather.12.cloned.1.call-start = ((), (), s32[]{:S(2)}) async-start(), calls=%async_computation.8 | async-start | bytes 28311552 | tf_op jit(solution)/shard_map/all_gather | solution.py:134
  70.8 719.5 %all-gather.14.cloned.1.call-start = ((), (), s32[]{:S(2)}) async-start(), calls=%async_computation.9 | async-start | bytes 9437184 | tf_op jit(solution)/shard_map/all_gather | solution.py:135
  72.0 1028.5 %reduce-scatter.7.cloned.1.call-start = ((), (), s32[]{:S(2)}) async-start(), calls=%async_computation.13 | async-start | bytes 37748736 | tf_op jit(solution)/shard_map/reduce_scatter | solution.py:187
  420.8 159.4 %copy-start.23 = (bf16[512,2048]{1,0:T(8,128)(2,1)S(1)}, bf16[512,2048]{1,0:T(8,128)(2,1)}, u32[]{:S(2)}) copy-start(bf16[512,2048]{1,0:T(8,128)(2,1)} %get-tuple-element.202) | copy-start | bytes 6291460
  445.8 180.2 %copy-start.16 = (f32[2,256,32]{2,1,0:T(8,128)}, f32[2,256,32]{2,1,0:T(8,128)S(1)}, u32[]{:S(2)}) copy-start(f32[2,256,32]{2,1,0:T(8,128)S(1)} %get-tuple-element.213) | copy-start | bytes 196612
  634.7 75.8 %all-to-all-start = ((bf16[2,256,3,8,256]{4,1,0,2,3:T(8,128)(2,1)}), bf16[2,256,3,8,256]{4,1,0,2,3:T(8,128)(2,1)}, u32[]{:S(2)}, u32[]{:S(2)}) async-start(bf16[2,256,3,8,256]{4,1,0,2,3:T(8,128)(2,1)} %pad_maximum_fusion.1), calls=%async_computation | async-start | bytes 12582912 | tf_op jit(solution)/shard_map/all_to_all | solution.py:153
  640.0 517.3 %reduce-scatter.11.cloned.1.call-start = ((), (), s32[]{:S(2)}) async-start(), calls=%async_computation.15 | async-start | bytes 18874368 | tf_op jit(solution)/shard_map/reduce_scatter | solution.py:250
  739.7 32.8 %copy-start.8 = (bf16[4,1024,256]{2,1,0:T(8,128)(2,1)}, bf16[4,1024,256]{2,1,0:T(8,128)(2,1)S(1)}, u32[]{:S(2)}) copy-start(bf16[4,1024,256]{2,1,0:T(8,128)(2,1)S(1)} %get-tuple-element.491) | copy-start | bytes 6291460
  889.3 72.9 %all-to-all-start.3 = ((bf16[2,1024,3,2,256]{4,3,0,2,1:T(2,128)(2,1)}), bf16[2,1024,3,2,256]{4,3,0,2,1:T(2,128)(2,1)}, u32[]{:S(2)}, u32[]{:S(2)}) async-start(bf16[2,1024,3,2,256]{4,3,0,2,1:T(2,128)(2,1)} %maximum_bitcast_fusion), calls=%async_computation.4 | async-start | bytes 12582912 | tf_op jit(solution)/shard_map/all_to_all | solution.py:216
  894.7 746.5 %reduce-scatter.9.cloned.1.call-start = ((), (), s32[]{:S(2)}) async-start(), calls=%async_computation.14 | async-start | bytes 56623104 | tf_op jit(solution)/shard_map/reduce_scatter | solution.py:249
  1047.4 762.9 %reduce-scatter.5.cloned.1.call-start = ((), (), s32[]{:S(2)}) async-start(), calls=%async_computation.11 | async-start | bytes 18874368 | tf_op jit(solution)/shard_map/reduce_scatter | solution.py:171
  1072.3 791.9 %all-reduce.14.cloned.1.call-start = ((), (), s32[]{:S(2)}) async-start(), calls=%async_computation.16 | async-start | bytes 196608
  1125.6 1192.3 %all-reduce.16.cloned.1.call-start = ((), (), s32[]{:S(2)}) async-start(), calls=%async_computation.17 | async-start | bytes 50331648 | tf_op jit(solution)/shard_map/psum | solution.py:260
  1641.2 169.1 %copy-start.19 = (bf16[512,2048]{1,0:T(8,128)(2,1)S(1)}, bf16[512,2048]{1,0:T(8,128)(2,1)}, u32[]{:S(2)}) copy-start(bf16[512,2048]{1,0:T(8,128)(2,1)} %reshape.239) | copy-start | bytes 6291460
  1887.1 438.3 %copy-start.53 = (f32[256]{0:T(256)}, f32[256]{0:T(256)S(1)}, u32[]{:S(2)}) copy-start(f32[256]{0:T(256)S(1)} %get-tuple-element.436) | copy-start | bytes 3076
  (51 other events, 415.4 us)
Sparse Core Ops, SparseCore 0:
  58.0 150.7 all-gather.15
  210.3 149.3 all-gather.17
  361.9 218.2 all-gather.11
  581.7 80.2 all-gather.13
  664.2 324.0 reduce-scatter.6
  990.6 166.5 reduce-scatter.10
  1159.7 481.4 reduce-scatter.8
  1643.6 166.6 reduce-scatter.4
  1813.2 50.9 all-reduce.13
  1869.1 448.6 all-reduce.15
where the time goes:
time: 2350 us; the launch traced here: 2340 us
  waiting for transfers between devices  1590 us (68%)
  matrix products  343 us (15%)
  blocking collectives  168 us (7%)
  local copies, waits for them, and re-layouts  131 us (6%)
  other arithmetic  84.3 us (4%)
    reduce_scatter x1, waiting for transfers between devices, body(): lax.psum_scatter(qkv_term, 'fsdp', scatter_dimension=0, tiled=True)  484 us
    psum x1, waiting for transfers between devices, body(): lax.psum((qkv_shard, out_shard, up_grad_shard, down_grad_shard, qk_bias_s...  431 us
    reduce_scatter x1, waiting for transfers between devices, body(): lax.psum_scatter(jnp.dot(active_low, down_low, preferred_element_type=jnp...  147 us
    dot_general x16, matrix products, contract_last(): lax.dot_general(left, right, (((1,), (1,)), ((), ())), preferred_element_...  143 us
    all_gather x1, waiting for transfers between devices, body(): lax.all_gather(qkv_low, 'fsdp', axis=0, tiled=True)  134 us
    all_gather x1, waiting for transfers between devices, body(): group_rows = lax.all_gather(normed_mlp, 'fsdp', axis=0, tiled=True)  122 us
    dot_general x12, matrix products, contract_lead(): lax.dot_general(left, right, (((0,), (0,)), ((), ())), preferred_element_...  96.7 us
    all_gather x1, waiting for transfers between devices, body(): group_grad = lax.all_gather(grad_low, 'fsdp', axis=0, tiled=True)  91.2 us
  transfers between devices with their start and end apart: 12, of which 10 were waited for; matrix products, arithmetic and copies ran while one was open for 22% of the time, Pallas kernels for 0%

commit v1 on v0

--- a/solution.py
+++ b/solution.py
@@ -293,6 +293,320 @@
     )
 
 
+LANES = 128
+
+
+def pick(slices, which):
+    return lax.dynamic_index_in_dim(slices, which, 0, keepdims=False)
+
+
+def swap_core(value):
+    return lax.ppermute(value, "fsdp", [(i, i ^ 1) for i in range(8)])
+
+
+def along_z(value, pairs):
+    return lax.ppermute(value, "fsdp", [(2 * a + c, 2 * b + c) for a, b in pairs for c in range(2)])
+
+
+def spread_pairs(step):
+    pairs = []
+    for source in range(4):
+        part = (step + source) % 4
+        for rank in range(8):
+            pairs.append((source * 8 + rank, (2 * (rank % 2) + part // 2) * 8 + rank - rank % 2 + part % 2))
+    return pairs
+
+
+def gather_z(own, z):
+    low_half = z < 2
+    edge = (z == 0) | (z == 3)
+    above = along_z(own, [(1, 0), (2, 1), (3, 2)])
+    below = along_z(own, [(0, 1), (1, 2), (2, 3)])
+    first = jnp.where(low_half, above, below)
+    outer = jnp.where(low_half, below, above)
+    inner = along_z(first, [(1, 0), (2, 3)])
+    cross = along_z(outer, [(1, 2), (2, 1)])
+    second = jnp.where(edge, inner, outer)
+    third = jnp.where(edge, along_z(cross, [(1, 0), (2, 3)]), cross)
+    return [own, first, second, third]
+
+
+def scatter_z(parts, z):
+    low = jnp.bfloat16
+    low_half = z < 2
+    far = along_z(parts[3].astype(low), [(0, 1), (3, 2)])
+    cross = along_z((parts[3] + far.astype(jnp.float32)).astype(low), [(1, 2), (2, 1)])
+    near = along_z(parts[2].astype(low), [(0, 1), (3, 2)])
+    one = parts[1] + near.astype(jnp.float32)
+    two = parts[2] + cross.astype(jnp.float32)
+    up = jnp.where(low_half, one, two).astype(low)
+    down = jnp.where(low_half, two, one).astype(low)
+    from_below = along_z(up, [(0, 1), (1, 2), (2, 3)])
+    from_above = along_z(down, [(1, 0), (2, 1), (3, 2)])
+    return parts[0] + from_below.astype(jnp.float32) + from_above.astype(jnp.float32)
+
+
+def swap_seq(value, bit):
+    return lax.ppermute(value, "seq", [(i, i ^ bit) for i in range(4)])
+
+
+def sum_seq(part, x, y):
+    rows, columns = part.shape
+    halves = part.reshape(2, 2, 2, rows // 8, columns)
+    low = jnp.bfloat16
+    outs = []
+    for half, (bit_a, at_a), (bit_b, at_b) in ((0, (1, x), (2, y)), (1, (2, y), (1, x))):
+        mine = halves[half]
+        sent = swap_seq(pick(mine, 1 - at_a).astype(low), bit_a)
+        kept = pick(mine, at_a) + sent.astype(jnp.float32)
+        sent = swap_seq(pick(kept, 1 - at_b).astype(low), bit_b)
+        outs.append((pick(kept, at_b) + sent.astype(jnp.float32)).astype(low))
+    return outs
+
+
+def spread_seq(pieces, x, y):
+    outs = []
+    for piece, (bit_a, at_a), (bit_b, at_b) in ((pieces[0], (1, x), (2, y)), (pieces[1], (2, y), (1, x))):
+        other = swap_seq(piece, bit_b)
+        both = jnp.where(at_b == 0, jnp.stack([piece, other]), jnp.stack([other, piece]))
+        other = swap_seq(both, bit_a)
+        outs.append(jnp.where(at_a == 0, jnp.stack([both, other]), jnp.stack([other, both])))
+    rows, columns = pieces[0].shape
+    return jnp.stack(outs).reshape(8 * rows, columns).astype(jnp.float32)
+
+
+def split_body(
+    resid_in,
+    qkv_weight,
+    qkv_bias,
+    out_weight,
+    out_bias,
+    up_weight,
+    up_bias,
+    down_weight,
+    down_bias,
+    attn_gain,
+    attn_shift,
+    mlp_gain,
+    mlp_shift,
+    block_ids,
+    offsets,
+    grad_out,
+):
+    low = jnp.bfloat16
+    f32 = jnp.float32
+    groups, piece, width = resid_in.shape
+    tokens = groups * piece
+    s = lax.axis_index("seq")
+    f = lax.axis_index("fsdp")
+    z, c = f // 2, f % 2
+    x, y = s % 2, s // 2
+    both_axes = ("seq", "fsdp")
+    units = up_weight.shape[0]
+
+    packed = jnp.concatenate(
+        [attn_gain, attn_shift, mlp_gain, mlp_shift, out_bias + down_bias, qkv_bias]
+    )
+    small = lax.all_gather(packed, "fsdp", axis=0)
+    gain_a, shift_a, gain_m, shift_m, bias_out = (
+        small[:, i * 256 : (i + 1) * 256].reshape(width) for i in range(5)
+    )
+    head_bias = small[:, 5 * 256 :].reshape(3, HEADS, HEAD_DIM)
+    head_bias = lax.dynamic_index_in_dim(head_bias, f, 1, keepdims=False).reshape(3 * HEAD_DIM)
+    ids_starts = lax.all_gather(
+        jnp.concatenate([block_ids, offsets], axis=1), "fsdp", axis=0, tiled=True
+    )
+    ids_all = ids_starts[:, : block_ids.shape[1]]
+    starts_all = ids_starts[:, block_ids.shape[1] :]
+
+    flat = resid_in.reshape(tokens, width)
+    center = flat - jnp.mean(flat, axis=-1, keepdims=True)
+    inv = lax.rsqrt(jnp.mean(center * center, axis=-1, keepdims=True) + EPS)
+    normal = center * inv
+    grad_flat = grad_out.reshape(tokens, width)
+
+    def plane_out(value):
+        parts = value.reshape(4, tokens // 4, width)
+        got = [
+            lax.ppermute(pick(parts, (k + s) % 4), both_axes, spread_pairs(k)) for k in range(4)
+        ]
+        return jnp.concatenate(got, axis=0)
+
+    def plane_back(value):
+        parts = value.reshape(4, tokens // 4, width)
+        got = jnp.stack(
+            [
+                lax.ppermute(parts[k], both_axes, [(b, a) for a, b in spread_pairs(k)])
+                for k in range(4)
+            ]
+        )
+        return jnp.concatenate([pick(got, (j - s + 4) % 4) for j in range(4)], axis=0)
+
+    own_n = plane_out(normal.astype(low))
+    own_g = plane_out(grad_flat.astype(low))
+
+    quarter = HEAD_DIM // 4
+    qkv_low = lax.dynamic_slice_in_dim(
+        qkv_weight.reshape(3, HEAD_DIM, width), s * quarter, quarter, 1
+    ).astype(low)
+    came = jnp.stack(
+        [
+            lax.ppermute(qkv_low[i], "fsdp", [(r, (3 * r + i) % 8) for r in range(8)])
+            for i in range(3)
+        ]
+    )
+
+    def third_of(i):
+        return (3 * ((3 * (f - i + 8)) % 8) + i) // 8
+
+    slot_of = [
+        sum(jnp.where(third_of(i) == kind, i, 0) for i in range(3)) for kind in range(3)
+    ]
+    came = jnp.stack([pick(came, slot_of[kind]) for kind in range(3)])
+    head_w = lax.all_gather(came, "seq", axis=1, tiled=True).reshape(3 * HEAD_DIM, width)
+    up_low = up_weight.astype(low)
+    plain_w = jnp.concatenate([up_low, head_w], axis=0)
+    gains = jnp.concatenate(
+        [jnp.broadcast_to(gain_m, (units, width)), jnp.broadcast_to(gain_a, (768, width))], axis=0
+    )
+    shifts = jnp.concatenate(
+        [jnp.broadcast_to(shift_m, (units, width)), jnp.broadcast_to(shift_a, (768, width))],
+        axis=0,
+    )
+    w_in = (plain_w.astype(f32) * gains).astype(low)
+    bias_in = jnp.concatenate([up_bias, head_bias]) + jnp.sum(
+        plain_w.astype(f32) * shifts, axis=1
+    )
+    w_out = jnp.concatenate([down_weight, out_weight], axis=0).astype(low)
+
+    halves = [(2 * (s % 2) + c, c), (2 * (s % 2) + 1 - c, 1 - c)]
+    rows_at = [((part - k + 4) % 4) * 2 + core for part, core in halves for k in range(4)]
+    blocks = [
+        z,
+        jnp.where(z % 2 == 0, 1, 2),
+        jnp.where(z == 0, 2, jnp.where(z == 1, 0, jnp.where(z == 2, 3, 1))),
+        jnp.where(z < 2, 3, 0),
+    ]
+    ids_rows = ids_all.reshape(16, 8, LANES)
+    ids_slots = [pick(ids_rows, block * 4 + s) for block in blocks]
+    ids_here = jnp.stack(
+        [jnp.concatenate([pick(row, at) for at in rows_at]) for row in ids_slots]
+    )
+    starts_here = jnp.stack([pick(starts_all, block * 4 + s) for block in blocks])
+    pos = (jnp.stack(rows_at)[:, None] * LANES + jnp.arange(LANES)[None, :]).reshape(1024)
+    positions = block_offset(ids_here, starts_here) + pos[None, :]
+    cosine, sine = rotary_tables(positions)
+
+    slots_n = gather_z(own_n, z)
+    own_g, _ = lax.optimization_barrier((own_g, slots_n[3]))
+    slots_g = gather_z(own_g, z)
+
+    full_n, kept_act, kept_slope, heads, outs = [], [], [], [], []
+    parts = []
+    for t in range(4):
+        n_t = jnp.concatenate([slots_n[t], swap_core(slots_n[t])], axis=0)
+        full_n.append(n_t)
+        projected = contract_last(n_t, w_in) + bias_in
+        hidden = projected[:, :units]
+        cdf = 0.5 * (1.0 + lax.erf(hidden * (0.5**0.5)))
+        act = (hidden * cdf).astype(low)
+        slope = (cdf + hidden * jnp.exp(-0.5 * hidden * hidden) * (1.0 / math.sqrt(2.0 * math.pi))).astype(low)
+        qkv = projected[:, units:].reshape(1024, 3, HEAD_DIM)
+        query = rotate(qkv[:, None, 0], cosine[t], sine[t])[:, 0].astype(low)
+        keys = rotate(qkv[:, None, 1], cosine[t], sine[t])[:, 0].astype(low)
+        values = qkv[:, 2].astype(low)
+        mixed, lse = attend_forward((query, keys, values, ids_here[t]))
+        heads.append((query, keys, values, lse))
+        a_t = jnp.concatenate([act, mixed], axis=1)
+        outs.append(a_t)
+        kept_slope.append(slope)
+        p_own = jnp.dot(a_t[:512], w_out, preferred_element_type=f32)
+        p_sib = jnp.dot(a_t[512:], w_out, preferred_element_type=f32).astype(low)
+        parts.append(p_own + swap_core(p_sib).astype(f32))
+    branch = plane_back(scatter_z(parts, z).astype(low))
+    result = flat + branch.astype(f32) + bias_out
+
+    full_g, backs, parts = [], [], []
+    for t in range(4):
+        g_t = jnp.concatenate([slots_g[t], swap_core(slots_g[t])], axis=0)
+        full_g.append(g_t)
+        grad_a = contract_last(g_t, w_out).astype(low)
+        gh = (grad_a[:, :units].astype(f32) * kept_slope[t].astype(f32)).astype(low)
+        query, keys, values, lse = heads[t]
+        gq, gk, gv = attend_backward((query, keys, values, ids_here[t], lse, grad_a[:, units:]))
+        gq = rotate(gq.astype(f32)[:, None], cosine[t], -sine[t])[:, 0].astype(low)
+        gk = rotate(gk.astype(f32)[:, None], cosine[t], -sine[t])[:, 0].astype(low)
+        b_t = jnp.concatenate([gh, gq, gk, gv], axis=1)
+        backs.append(b_t)
+        u_own = jnp.dot(b_t[:512], w_in, preferred_element_type=f32)
+        u_sib = jnp.dot(b_t[512:], w_in, preferred_element_type=f32).astype(low)
+        parts.append(u_own + swap_core(u_sib).astype(f32))
+    u = plane_back(scatter_z(parts, z).astype(low)).astype(f32)
+    grad_input = grad_flat + inv * (
+        u - jnp.mean(u, axis=-1, keepdims=True) - normal * jnp.mean(u * normal, axis=-1, keepdims=True)
+    )
+
+    all_n, all_g = jnp.concatenate(full_n), jnp.concatenate(full_g)
+    all_a, all_b = jnp.concatenate(outs), jnp.concatenate(backs)
+    term_out = contract_lead(all_a, all_g)
+    raw_in = contract_lead(all_b, all_n)
+    sums = jnp.sum(all_b.astype(f32), axis=0)
+    term_in = raw_in * gains + sums[:, None] * shifts
+    gain_terms = raw_in * plain_w.astype(f32)
+    shift_terms = sums[:, None] * plain_w.astype(f32)
+
+    down_out = spread_seq(sum_seq(term_out, x, y), x, y)
+    up_out = spread_seq(sum_seq(term_in[:units], x, y), x, y)
+    qkv_quarter = sum_seq(term_in[units:].reshape(3, 2, 4, 32, width).transpose(1, 2, 0, 3, 4).reshape(768, width), x, y)
+    qkv_quarter = jnp.stack(qkv_quarter).reshape(2, 3, 32, width)
+    kinds = jnp.stack([pick(qkv_quarter.transpose(1, 0, 2, 3), third_of(i)) for i in range(3)])
+    qkv_back = [
+        lax.ppermute(kinds[i], "fsdp", [((3 * r + i) % 8, r) for r in range(8)]) for i in range(3)
+    ]
+    qkv_back = jnp.stack(qkv_back).transpose(1, 0, 2, 3).reshape(2, 96, width)
+    qkv_out = spread_seq([qkv_back[0], qkv_back[1]], x, y)
+    qkv_out = qkv_out.reshape(2, 4, 3, 32, width).transpose(2, 0, 1, 3, 4).reshape(768, width)
+
+    slots = jnp.zeros((16, HEAD_DIM), f32)
+    slots = lax.dynamic_update_slice(slots, sums[units : units + 256][None], (f, 0))
+    slots = lax.dynamic_update_slice(slots, sums[units + 256 : units + 512][None], (8 + f, 0))
+    spread = jnp.stack(
+        [
+            jnp.sum(gain_terms[units:], axis=0),
+            jnp.sum(shift_terms[units:], axis=0),
+            jnp.sum(gain_terms[:units], axis=0),
+            jnp.sum(shift_terms[:units], axis=0),
+            jnp.sum(grad_flat, axis=0),
+        ]
+    )
+    wide = jnp.concatenate(
+        [spread.reshape(5, 8, 256).transpose(1, 0, 2).reshape(8, 5 * 256), slots.reshape(8, 512)], axis=1
+    )
+    mine = lax.psum_scatter(wide, "fsdp", scatter_dimension=0, tiled=True)[0]
+    mine = lax.psum(jnp.concatenate([mine, sums[:units], sums[units + 512 :]]), "seq")
+    vectors = [mine[i * 256 : (i + 1) * 256] for i in range(5)]
+    qk_grad = mine[1280:1792]
+    up_bias_grad = mine[1792 : 1792 + units]
+    value_grad = mine[1792 + units :]
+    return (
+        result.reshape(groups, piece, width),
+        grad_input.reshape(groups, piece, width),
+        qkv_out,
+        qk_grad,
+        value_grad,
+        down_out[units:],
+        vectors[4],
+        up_out,
+        up_bias_grad,
+        down_out[:units],
+        vectors[4],
+        vectors[0],
+        vectors[1],
+        vectors[2],
+        vectors[3],
+    )
+
+
 def solution(mesh):
     placed = (
         P("fsdp", "seq", None),
@@ -313,7 +627,7 @@
         P("fsdp", "seq", None),
     )
     return jax.shard_map(
-        body,
+        split_body if mesh.shape["fsdp"] == HEADS and mesh.shape["seq"] == 4 else body,
         mesh=mesh,
         in_specs=placed,
         out_specs=(

time: 2350 us -> 1530 us (0.65)
  waiting for transfers between devices: 1590 us -> 404 us
  starting transfers between devices: 11.5 us -> 186 us
  other arithmetic: 84.3 us -> 240 us
  blocking collectives: 168 us -> 119 us
  matrix products: 343 us -> 389 us
  local copies, waits for them, and re-layouts: 131 us -> 158 us
    reduce_scatter x4 -> x0, waiting for transfers between devices: 638 us -> none  [the longest x1 484 us: body(): lax.psum_scatter(qkv_term, 'fsdp', scatter_dimension=0, tiled=True)]
    psum x1 -> x0, waiting for transfers between devices: 431 us -> none  [body(): lax.psum((qkv_shard, out_shard, up_grad_shard, down_grad_shard, qk_bias_s...]
    ppermute x0 -> x82, waiting for transfers between devices: none -> 404 us  [the longest x20 220 us: along_z(): lax.ppermute(value, 'fsdp', [(2 * a + c, 2 * b + c) for a, b in pairs for...]
    all_gather x4 -> x1, waiting for transfers between devices: 348 us -> 0.01 us  [split_body(): lax.all_gather(came, 'seq', axis=1, tiled=True).reshape(3 * HEAD_DIM, width)]
    ppermute x0 -> x82, starting transfers between devices: none -> 186 us  [the longest x20 61.4 us: along_z(): lax.ppermute(value, 'fsdp', [(2 * a + c, 2 * b + c) for a, b in pairs for...]
    all_to_all x2 -> x0, waiting for transfers between devices: 133 us -> none  [the longest x1 70.4 us: body(): lax.all_to_all(packed, 'seq', split_axis=3, concat_axis=1, tiled=True)]
    all_to_all x2 -> x0, blocking collectives: 55 us -> none  [the longest x1 28.2 us: body(): lax.all_to_all(back_heads, 'seq', split_axis=1, concat_axis=2, tiled=True)]
    convert_element_type x5 -> x29, other arithmetic: 22.6 us -> 70.1 us  [the longest x2 20.1 us: scatter_z(): up = jnp.where(low_half, one, two).astype(low)]
  transfers between devices with their start and end apart: 12 -> 83, of which waited for: 10 -> 23; matrix products, arithmetic and copies ran while one was open for 22% -> 48% of each run, Pallas kernels for 0% -> 0%
where the time goes in v1:
time: 1530 us; the launch traced here: 1510 us
  waiting for transfers between devices  404 us (26%)
  matrix products  389 us (25%)
  other arithmetic  240 us (16%)
  starting transfers between devices  186 us (12%)
  local copies, waits for them, and re-layouts  158 us (10%)
  blocking collectives  119 us (8%)
  between operations  18.2 us (1%)
    ppermute x20, waiting for transfers between devices, along_z(): lax.ppermute(value, 'fsdp', [(2 * a + c, 2 * b + c) for a, b in pairs for...  220 us
    ppermute x24, waiting for transfers between devices, swap_seq(): return lax.ppermute(value, 'seq', [(i, i ^ bit) for i in range(4)])  173 us
    dot_general x16, matrix products, contract_last(): lax.dot_general(left, right, (((1,), (1,)), ((), ())), preferred_element_...  128 us
    dot_general x10, matrix products, contract_lead(): lax.dot_general(left, right, (((0,), (0,)), ((), ())), preferred_element_...  110 us
    ppermute x20, starting transfers between devices, along_z(): lax.ppermute(value, 'fsdp', [(2 * a + c, 2 * b + c) for a, b in pairs for...  61.4 us
    all_gather x1, blocking collectives, split_body(): small = lax.all_gather(packed, 'fsdp', axis=0)  60.7 us
    ppermute x8, starting transfers between devices, plane_out(): lax.ppermute(pick(parts, (k + s) % 4), both_axes, spread_pairs(k))  56.8 us
    unnamed x426, local copies, waits for them, and re-layouts  52.8 us
  transfers between devices with their start and end apart: 83, of which 23 were waited for; matrix products, arithmetic and copies ran while one was open for 48% of the time, Pallas kernels for 0%

profile of v1, /device:TPU:0, one launch (start us, length us, event | category | flops | bytes accessed | tf_op | source)
XLA Modules:
  0.0 1514.3 jit_solution(5642502531882120179)
XLA Ops:
  34.2 15.5 %all-gather.1 = s32[8,2,1032]{2,1,0:T(2,128)S(1)} all-gather(s32[1,2,1032]{2,1,0:T(2,128)S(1)} %add_bitcast_fusion), channel_id=1, replica_groups=mesh['seq'=4,'fsdp'=8] {'fsdp'}, dimensions={0}, use_global_device_ids=true | all-gather | bytes 74304 | tf_op jit(solution)/shard_map/all_gather | solution.py:416
  85.6 39.2 %collective-permute-start.30 = (bf16[128,2048]{1,0:T(8,128)(2,1)S(1)}, bf16[128,2048]{1,0:T(8,128)(2,1)}, u32[]{:S(2)}, u32[]{:S(2)}) collective-permute-start(bf16[128,2048]{1,0:T(8,128)(2,1)S(1)} %get-tuple-element.109), channel_id=1, source_target_pairs={{0,1},{1,17},{2,3},{3,19},{4,5},{5,21},{6,7},{7,23},{8,8},{9,24},{... | collective-permute-start | bytes 1572872 | tf_op jit(solution)/shard_map/ppermute | solution.py:431
  133.6 60.7 %all-gather = f32[16384]{0:T(1024)S(1)} all-gather(f32[2048]{0:T(1024)} %copy-done.163), channel_id=2, replica_groups=mesh['seq'=4,'fsdp'=8] {'fsdp'}, dimensions={0}, use_global_device_ids=true | all-gather | bytes 73728 | tf_op jit(solution)/shard_map/all_gather | solution.py:410
  250.3 18.4 %fusion.76 = f32[1024,1792]{1,0:T(8,128)} fusion(bf16[512,2048]{1,0:T(8,128)(2,1)} %collective-permute-done.11, bf16[512,2048]{1,0:T(8,128)(2,1)} %get-tuple-element.32, f32[1792]{0:T(1024)S(1)} %maximum_add_fusion, f32[768,2048]{1,0:T(8,128)} %broadcast_in_dim.120, f32[1024,2048]{1,0:T(8,128)} %broadcast_in_dim.119, bf16[768,2048]{1,0:T(8,128)(2,1)S(1)} %bitcast.716, ...), kind=kOutput, calls=%fused_computation.153 | convolution fusion | flops 7552106496 | bytes 33561600 | tf_op jit(solution)/shard_map/dot_general | solution.py:59
  275.4 19.4 %convolution_add_fusion = f32[1024,1792]{1,0:T(8,128)} fusion(bf16[1024,2048]{1,0:T(8,128)(2,1)} %get-tuple-element.118, f32[1792]{0:T(1024)S(1)} %maximum_add_fusion, f32[768,2048]{1,0:T(8,128)} %broadcast_in_dim.120, f32[1024,2048]{1,0:T(8,128)} %broadcast_in_dim.119, bf16[768,2048]{1,0:T(8,128)(2,1)} %bitcast.706, ...), kind=kOutput, calls=%fused_computation.154 | convolution fusion | flops 7543717888 | bytes 33561600 | tf_op jit(solution)/shard_map/dot_general | solution.py:59
  319.3 18.4 %fusion.73 = f32[1024,1792]{1,0:T(8,128)} fusion(bf16[512,2048]{1,0:T(8,128)(2,1)} %collective-permute-done.14, bf16[512,2048]{1,0:T(8,128)(2,1)} %get-tuple-element.29, f32[1792]{0:T(1024)S(1)} %copy-done.162, f32[768,2048]{1,0:T(8,128)} %broadcast_in_dim.120, f32[1024,2048]{1,0:T(8,128)} %broadcast_in_dim.119, bf16[768,2048]{1,0:T(8,128)(2,1)S(1)} %bitcast.717, ...), kind=kOutput, calls=%fused_computation.152 | convolution fusion | flops 7552106496 | bytes 33561600 | tf_op jit(solution)/shard_map/dot_general | solution.py:59
  346.8 20.6 %collective-permute-done.18 = bf16[512,2048]{1,0:T(8,128)(2,1)} collective-permute-done((bf16[512,2048]{1,0:T(8,128)(2,1)}, bf16[512,2048]{1,0:T(8,128)(2,1)}, u32[]{:S(2)}, u32[]{:S(2)}) %collective-permute-start.18) | collective-permute-done | bytes 2097184 | tf_op jit(solution)/shard_map/ppermute | solution.py:308
  385.0 37.3 %collective-permute-done.35 = bf16[512,2048]{1,0:T(8,128)(2,1)S(1)} collective-permute-done((bf16[512,2048]{1,0:T(8,128)(2,1)S(1)}, bf16[512,2048]{1,0:T(8,128)(2,1)S(1)}, u32[]{:S(2)}, u32[]{:S(2)}) %collective-permute-start.35) | collective-permute-done | bytes 2097184 | tf_op jit(solution)/shard_map/ppermute | solution.py:308
  432.8 18.3 %fusion.70 = f32[1024,1792]{1,0:T(8,128)} fusion(bf16[512,2048]{1,0:T(8,128)(2,1)} %collective-permute-done.19, bf16[512,2048]{1,0:T(8,128)(2,1)} %copy-done.68, f32[1792]{0:T(1024)S(1)} %copy-done.162, f32[768,2048]{1,0:T(8,128)} %broadcast_in_dim.120, f32[1024,2048]{1,0:T(8,128)} %broadcast_in_dim.119, bf16[768,2048]{1,0:T(8,128)(2,1)S(1)} %bitcast.718, ...), kind=kOutput, calls=%fused_computation.151 | convolution fusion | flops 7552106496 | bytes 33561600 | tf_op jit(solution)/shard_map/dot_general | solution.py:59
  630.3 28.5 %collective-permute-done.44 = bf16[512,2048]{1,0:T(8,128)(2,1)} collective-permute-done((bf16[512,2048]{1,0:T(8,128)(2,1)}, bf16[512,2048]{1,0:T(8,128)(2,1)}, u32[]{:S(2)}, u32[]{:S(2)}) %collective-permute-start.44) | collective-permute-done | bytes 2097184 | tf_op jit(solution)/shard_map/ppermute | solution.py:308
  758.1 34.5 %convert_reduce_fusion = (f32[1792]{0:T(1024)S(1)}, bf16[4096,1792]{1,0:T(8,128)(2,1)}) fusion(bf16[1024,256]{1,0:T(8,128)(2,1)} %fusion.158, bf16[1024,256]{1,0:T(8,128)(2,1)} %copy.368, bf16[1024,256]{1,0:T(8,128)(2,1)} %copy.367, bf16[1024,1024]{1,0:T(8,128)(2,1)} %get-tuple-element.46, bf16[1024,256]{1,0:T(8,128)(2,1)} %copy-done.59, ...), kind=kLoop, calls=%fused_computation | loop fusion | flops 249559296 | bytes 29367296 | tf_op jit(solution)/shard_map/reduce_sum | solution.py:553
  792.7 48.3 %convert_multiply_fusion.1 = (f32[1792,2048]{1,0:T(8,128)}, f32[1792,2048]{1,0:T(8,128)}, f32[1792,2048]{1,0:T(8,128)}) fusion(bf16[768,2048]{1,0:T(8,128)(2,1)} %bitcast.713, bf16[1024,2048]{1,0:T(8,128)(2,1)} %convert_element_type.586, f32[768,2048]{1,0:T(8,128)S(1)} %bitcast.647, f32[1024,2048]{1,0:T(8,128)} %copy-done.9, ...), kind=kOutput, calls=%fused_computation.2 | convolution fusion | flops 30105141248 | bytes 112204800 | tf_op jit(solution)/shard_map/dot_general | solution.py:53
  851.5 27.2 %all-reduce = f32[8,1792]{1,0:T(8,128)S(1)} all-reduce(f32[8,1792]{1,0:T(8,128)S(1)} %pad_maximum_fusion.24), channel_id=3, replica_groups=mesh['seq'=4,'fsdp'=8] {'fsdp'}, use_global_device_ids=true, to_apply=%region_24.25.clone | all-reduce | flops 14336 | bytes 114688
  879.4 15.8 %psum.7 = f32[3072]{0:T(1024)S(1)} all-reduce(f32[3072]{0:T(1024)S(1)} %pad_maximum_fusion.25), channel_id=1, replica_groups=mesh['seq'=4,'fsdp'=8] {'seq'}, use_global_device_ids=true, to_apply=%region_25.26 | all-reduce | flops 3072 | bytes 24576 | tf_op jit(solution)/shard_map/psum | solution.py:586
  931.2 45.6 %fusion.5 = f32[1280,2048]{1,0:T(8,128)} fusion(bf16[4096,2048]{1,0:T(8,128)(2,1)} %constant_dynamic-update-slice_fusion.30, bf16[1024,256]{1,0:T(8,128)(2,1)S(1)} %copy-done.177, bf16[1024,1024]{1,0:T(8,128)(2,1)} %get-tuple-element.47, bf16[1024,256]{1,0:T(8,128)(2,1)S(1)} %copy-done.179, bf16[1024,1024]{1,0:T(8,128)(2,1)} %get-tuple-element.51, ...), kind=kOutput, calls=%fused_computation.13 | convolution fusion | flops 21558722560 | bytes 37748736 | tf_op jit(solution)/shard_map/dot_general | solution.py:53
  1004.9 49.3 %collective-permute-done.78 = bf16[2,128,2048]{2,1,0:T(8,128)(2,1)S(1)} collective-permute-done((bf16[2,128,2048]{2,1,0:T(8,128)(2,1)S(1)}, bf16[2,128,2048]{2,1,0:T(8,128)(2,1)S(1)}, u32[]{:S(2)}, u32[]{:S(2)}) %collective-permute-start.78) | collective-permute-done | bytes 1048608 | tf_op jit(solution)/shard_map/ppermute | solution.py:350
  1067.2 25.8 %collective-permute-done.58 = bf16[96,2048]{1,0:T(8,128)(2,1)S(1)} collective-permute-done((bf16[96,2048]{1,0:T(8,128)(2,1)S(1)}, bf16[96,2048]{1,0:T(8,128)(2,1)S(1)}, u32[]{:S(2)}, u32[]{:S(2)}) %collective-permute-start.58) | collective-permute-done | bytes 393248 | tf_op jit(solution)/shard_map/ppermute | solution.py:350
  1125.2 22.4 %collective-permute-done.64 = bf16[96,2048]{1,0:T(8,128)(2,1)S(1)} collective-permute-done((bf16[96,2048]{1,0:T(8,128)(2,1)S(1)}, bf16[96,2048]{1,0:T(8,128)(2,1)S(1)}, u32[]{:S(2)}, u32[]{:S(2)}) %collective-permute-start.64) | collective-permute-done | bytes 393248 | tf_op jit(solution)/shard_map/ppermute | solution.py:350
  1222.9 13.8 collective-permute-done.81
  1254.4 41.8 %collective-permute-done.21 = bf16[512,2048]{1,0:T(8,128)(2,1)} collective-permute-done((bf16[512,2048]{1,0:T(8,128)(2,1)}, bf16[512,2048]{1,0:T(8,128)(2,1)}, u32[]{:S(2)}, u32[]{:S(2)}) %collective-permute-start.21) | collective-permute-done | bytes 2097184 | tf_op jit(solution)/shard_map/ppermute | solution.py:308
  1318.6 22.5 %collective-permute-done.42 = bf16[512,2048]{1,0:T(8,128)(2,1)S(1)} collective-permute-done((bf16[512,2048]{1,0:T(8,128)(2,1)}, bf16[512,2048]{1,0:T(8,128)(2,1)S(1)}, u32[]{:S(2)}, u32[]{:S(2)}) %collective-permute-start.42) | collective-permute-done | bytes 2097184 | tf_op jit(solution)/shard_map/ppermute | solution.py:308
  1356.2 24.8 %collective-permute-done.16 = bf16[512,2048]{1,0:T(8,128)(2,1)} collective-permute-done((bf16[512,2048]{1,0:T(8,128)(2,1)}, bf16[512,2048]{1,0:T(8,128)(2,1)}, u32[]{:S(2)}, u32[]{:S(2)}) %collective-permute-start.16) | collective-permute-done | bytes 2097184 | tf_op jit(solution)/shard_map/ppermute | solution.py:308
  1415.3 16.5 %collective-permute-done.49 = bf16[512,2048]{1,0:T(8,128)(2,1)} collective-permute-done((bf16[512,2048]{1,0:T(8,128)(2,1)}, bf16[512,2048]{1,0:T(8,128)(2,1)}, u32[]{:S(2)}, u32[]{:S(2)}) %collective-permute-start.49) | collective-permute-done | bytes 2097184 | tf_op jit(solution)/shard_map/ppermute | solution.py:308
  1454.3 14.9 collective-permute-done.23
  (857 shorter events, 816.3 us)
Async XLA Ops:
  7.2 224.2 %all-gather.4.cloned.1.call-start = ((), (), s32[]{:S(2)}) async-start(), calls=%async_computation | async-start | bytes 3932160 | tf_op jit(solution)/shard_map/all_gather | solution.py:466
  79.3 115.3 %collective-permute-start.32 = (bf16[128,2048]{1,0:T(8,128)(2,1)}, bf16[128,2048]{1,0:T(8,128)(2,1)}, u32[]{:S(2)}, u32[]{:S(2)}) collective-permute-start(bf16[128,2048]{1,0:T(8,128)(2,1)} %get-tuple-element.107), channel_id=1, source_target_pairs={{0,9},{1,25},{2,11},{3,27},{4,13},{5,29},{6,15},{7,31},{8,0},{9,16... | collective-permute-start | bytes 1572872 | tf_op jit(solution)/shard_map/ppermute | solution.py:431
  81.2 132.1 %collective-permute-start.31 = (bf16[128,2048]{1,0:T(8,128)(2,1)}, bf16[128,2048]{1,0:T(8,128)(2,1)}, u32[]{:S(2)}, u32[]{:S(2)}) collective-permute-start(bf16[128,2048]{1,0:T(8,128)(2,1)} %get-tuple-element.108), channel_id=1, source_target_pairs={{0,8},{1,24},{2,10},{3,26},{4,12},{5,28},{6,14},{7,30},{8,9},{9,25... | collective-permute-start | bytes 1572872 | tf_op jit(solution)/shard_map/ppermute | solution.py:431
  85.6 127.8 %collective-permute-start.30 = (bf16[128,2048]{1,0:T(8,128)(2,1)S(1)}, bf16[128,2048]{1,0:T(8,128)(2,1)}, u32[]{:S(2)}, u32[]{:S(2)}) collective-permute-start(bf16[128,2048]{1,0:T(8,128)(2,1)S(1)} %get-tuple-element.109), channel_id=1, source_target_pairs={{0,1},{1,17},{2,3},{3,19},{4,5},{5,21},{6,7},{7,23},{8,8},{9,24},{... | collective-permute-start | bytes 1572872 | tf_op jit(solution)/shard_map/ppermute | solution.py:431
  132.1 84.4 %collective-permute-start.11 = (bf16[512,2048]{1,0:T(8,128)(2,1)}, bf16[512,2048]{1,0:T(8,128)(2,1)}, u32[]{:S(2)}, u32[]{:S(2)}) collective-permute-start(bf16[512,2048]{1,0:T(8,128)(2,1)} %get-tuple-element.32), channel_id=1, source_target_pairs={{0,1},{1,0},{2,3},{3,2},{4,5},{5,4},{6,7},{7,6},{8,9},{9,8},{10,11... | collective-permute-start | bytes 6291464 | tf_op jit(solution)/shard_map/ppermute | solution.py:304
  132.2 87.5 %collective-permute-start.13 = (bf16[512,2048]{1,0:T(8,128)(2,1)}, bf16[512,2048]{1,0:T(8,128)(2,1)}, u32[]{:S(2)}, u32[]{:S(2)}) collective-permute-start(bf16[512,2048]{1,0:T(8,128)(2,1)} %get-tuple-element.32), channel_id=1, source_target_pairs={{2,0},{3,1},{4,6},{5,7},{10,8},{11,9},{12,14},{13,15},{18,16},{19,... | collective-permute-start | bytes 6291464 | tf_op jit(solution)/shard_map/ppermute | solution.py:308
  226.1 93.1 %collective-permute-start.14 = (bf16[512,2048]{1,0:T(8,128)(2,1)}, bf16[512,2048]{1,0:T(8,128)(2,1)}, u32[]{:S(2)}, u32[]{:S(2)}) collective-permute-start(bf16[512,2048]{1,0:T(8,128)(2,1)} %get-tuple-element.29), channel_id=1, source_target_pairs={{0,1},{1,0},{2,3},{3,2},{4,5},{5,4},{6,7},{7,6},{8,9},{9,8},{10,11... | collective-permute-start | bytes 6291464 | tf_op jit(solution)/shard_map/ppermute | solution.py:304
  229.4 88.3 %collective-permute-start.17 = (bf16[512,2048]{1,0:T(8,128)(2,1)}, bf16[512,2048]{1,0:T(8,128)(2,1)}, u32[]{:S(2)}, u32[]{:S(2)}) collective-permute-start(bf16[512,2048]{1,0:T(8,128)(2,1)} %get-tuple-element.30), channel_id=1, source_target_pairs={{2,4},{3,5},{4,2},{5,3},{10,12},{11,13},{12,10},{13,11},{18,20},{1... | collective-permute-start | bytes 6291464 | tf_op jit(solution)/shard_map/ppermute | solution.py:308
  431.5 70.1 %collective-permute-start.37 = (bf16[512,2048]{1,0:T(8,128)(2,1)}, bf16[512,2048]{1,0:T(8,128)(2,1)}, u32[]{:S(2)}, u32[]{:S(2)}) collective-permute-start(bf16[512,2048]{1,0:T(8,128)(2,1)} %get-tuple-element.23), channel_id=1, source_target_pairs={{0,1},{1,0},{2,3},{3,2},{4,5},{5,4},{6,7},{7,6},{8,9},{9,8},{10,11... | collective-permute-start | bytes 6291464 | tf_op jit(solution)/shard_map/ppermute | solution.py:304
  431.5 95.9 %collective-permute-start.39 = (bf16[512,2048]{1,0:T(8,128)(2,1)}, bf16[512,2048]{1,0:T(8,128)(2,1)}, u32[]{:S(2)}, u32[]{:S(2)}) collective-permute-start(bf16[512,2048]{1,0:T(8,128)(2,1)} %get-tuple-element.23), channel_id=1, source_target_pairs={{2,0},{3,1},{4,6},{5,7},{10,8},{11,9},{12,14},{13,15},{18,16},{19,... | collective-permute-start | bytes 6291464 | tf_op jit(solution)/shard_map/ppermute | solution.py:308
  535.5 70.4 %collective-permute-start.43 = (bf16[512,2048]{1,0:T(8,128)(2,1)}, bf16[512,2048]{1,0:T(8,128)(2,1)}, u32[]{:S(2)}, u32[]{:S(2)}) collective-permute-start(bf16[512,2048]{1,0:T(8,128)(2,1)} %get-tuple-element.21), channel_id=1, source_target_pairs={{2,4},{3,5},{4,2},{5,3},{10,12},{11,13},{12,10},{13,11},{18,20},{1... | collective-permute-start | bytes 6291464 | tf_op jit(solution)/shard_map/ppermute | solution.py:308
  599.1 84.1 %collective-permute-start.41 = (bf16[512,2048]{1,0:T(8,128)(2,1)}, bf16[512,2048]{1,0:T(8,128)(2,1)}, u32[]{:S(2)}, u32[]{:S(2)}) collective-permute-start(bf16[512,2048]{1,0:T(8,128)(2,1)} %convolution_convert_fusion.1), channel_id=1, source_target_pairs={{0,1},{1,0},{2,3},{3,2},{4,5},{5,4},{6,7},{7,6},{8,9},{9,8},{10,11... | collective-permute-start | bytes 6291464 | tf_op jit(solution)/shard_map/ppermute | solution.py:304
  673.5 628.1 %collective-permute-start.38 = (bf16[512,2048]{1,0:T(8,128)(2,1)}, bf16[512,2048]{1,0:T(8,128)(2,1)}, u32[]{:S(2)}, u32[]{:S(2)}) collective-permute-start(bf16[512,2048]{1,0:T(8,128)(2,1)} %convolution_convert_fusion.2), channel_id=1, source_target_pairs={{0,1},{1,0},{2,3},{3,2},{4,5},{5,4},{6,7},{7,6},{8,9},{9,8},{10,11... | collective-permute-start | bytes 6291464 | tf_op jit(solution)/shard_map/ppermute | solution.py:304
  918.6 254.7 %collective-permute-start.46 = (bf16[512,2048]{1,0:T(8,128)(2,1)}, bf16[512,2048]{1,0:T(8,128)(2,1)}, u32[]{:S(2)}, u32[]{:S(2)}) collective-permute-start(bf16[512,2048]{1,0:T(8,128)(2,1)} %convolution_convert_fusion), channel_id=1, source_target_pairs={{0,1},{1,0},{2,3},{3,2},{4,5},{5,4},{6,7},{7,6},{8,9},{9,8},{10,11... | collective-permute-start | bytes 6291464 | tf_op jit(solution)/shard_map/ppermute | solution.py:304
  920.1 67.7 %collective-permute-start.55 = (bf16[2,96,2048]{2,1,0:T(8,128)(2,1)S(1)}, bf16[2,96,2048]{2,1,0:T(8,128)(2,1)}, u32[]{:S(2)}, u32[]{:S(2)}) collective-permute-start(bf16[2,96,2048]{2,1,0:T(8,128)(2,1)S(1)} %fusion.187), channel_id=1, source_target_pairs={{0,8},{8,0},{16,24},{24,16},{1,9},{9,1},{17,25},{25,17},{2,10},{10... | collective-permute-start | bytes 2359304 | tf_op jit(solution)/shard_map/ppermute | solution.py:350
  986.5 108.6 %collective-permute-start.70 = (bf16[2,160,2048]{2,1,0:T(8,128)(2,1)S(1)}, bf16[2,160,2048]{2,1,0:T(8,128)(2,1)S(1)}, u32[]{:S(2)}, u32[]{:S(2)}) collective-permute-start(bf16[2,160,2048]{2,1,0:T(8,128)(2,1)S(1)} %fusion.128), channel_id=1, source_target_pairs={{0,16},{8,24},{16,0},{24,8},{1,17},{9,25},{17,1},{25,9},{2,18},{10... | collective-permute-start | bytes 3932168 | tf_op jit(solution)/shard_map/ppermute | solution.py:350
  987.9 66.3 %collective-permute-start.78 = (bf16[2,128,2048]{2,1,0:T(8,128)(2,1)S(1)}, bf16[2,128,2048]{2,1,0:T(8,128)(2,1)S(1)}, u32[]{:S(2)}, u32[]{:S(2)}) collective-permute-start(bf16[2,128,2048]{2,1,0:T(8,128)(2,1)S(1)} %fusion.182), channel_id=1, source_target_pairs={{0,16},{8,24},{16,0},{24,8},{1,17},{9,25},{17,1},{25,9},{2,18},{10... | collective-permute-start | bytes 3145736 | tf_op jit(solution)/shard_map/ppermute | solution.py:350
  1108.5 77.1 %collective-permute-start.20 = (bf16[512,2048]{1,0:T(8,128)(2,1)}, bf16[512,2048]{1,0:T(8,128)(2,1)}, u32[]{:S(2)}, u32[]{:S(2)}) collective-permute-start(bf16[512,2048]{1,0:T(8,128)(2,1)} %convolution_convert_fusion.4), channel_id=1, source_target_pairs={{0,1},{1,0},{2,3},{3,2},{4,5},{5,4},{6,7},{7,6},{8,9},{9,8},{10,11... | collective-permute-start | bytes 6291464 | tf_op jit(solution)/shard_map/ppermute | solution.py:304
  1218.7 77.4 %collective-permute-start.21 = (bf16[512,2048]{1,0:T(8,128)(2,1)}, bf16[512,2048]{1,0:T(8,128)(2,1)}, u32[]{:S(2)}, u32[]{:S(2)}) collective-permute-start(bf16[512,2048]{1,0:T(8,128)(2,1)} %get-tuple-element.245), channel_id=1, source_target_pairs={{0,2},{1,3},{6,4},{7,5},{8,10},{9,11},{14,12},{15,13},{16,18},{17,... | collective-permute-start | bytes 6291464 | tf_op jit(solution)/shard_map/ppermute | solution.py:308
  1236.7 104.4 %collective-permute-start.42 = (bf16[512,2048]{1,0:T(8,128)(2,1)}, bf16[512,2048]{1,0:T(8,128)(2,1)S(1)}, u32[]{:S(2)}, u32[]{:S(2)}) collective-permute-start(bf16[512,2048]{1,0:T(8,128)(2,1)} %get-tuple-element.223), channel_id=1, source_target_pairs={{0,2},{1,3},{6,4},{7,5},{8,10},{9,11},{14,12},{15,13},{16,18},{17,... | collective-permute-start | bytes 6291464 | tf_op jit(solution)/shard_map/ppermute | solution.py:308
  1301.6 79.5 %collective-permute-start.16 = (bf16[512,2048]{1,0:T(8,128)(2,1)}, bf16[512,2048]{1,0:T(8,128)(2,1)}, u32[]{:S(2)}, u32[]{:S(2)}) collective-permute-start(bf16[512,2048]{1,0:T(8,128)(2,1)} %get-tuple-element.243), channel_id=1, source_target_pairs={{0,2},{1,3},{6,4},{7,5},{8,10},{9,11},{14,12},{15,13},{16,18},{17,... | collective-permute-start | bytes 6291464 | tf_op jit(solution)/shard_map/ppermute | solution.py:308
  1310.9 76.1 %collective-permute-start.22 = (bf16[512,2048]{1,0:T(8,128)(2,1)}, bf16[512,2048]{1,0:T(8,128)(2,1)}, u32[]{:S(2)}, u32[]{:S(2)}) collective-permute-start(bf16[512,2048]{1,0:T(8,128)(2,1)} %add_convert_fusion.3), channel_id=1, source_target_pairs={{2,4},{3,5},{4,2},{5,3},{10,12},{11,13},{12,10},{13,11},{18,20},{1... | collective-permute-start | bytes 6291464 | tf_op jit(solution)/shard_map/ppermute | solution.py:308
  1342.9 96.9 %collective-permute-start.8 = (bf16[512,2048]{1,0:T(8,128)(2,1)}, bf16[512,2048]{1,0:T(8,128)(2,1)}, u32[]{:S(2)}, u32[]{:S(2)}) collective-permute-start(bf16[512,2048]{1,0:T(8,128)(2,1)} %convolution_convert_fusion.7), channel_id=1, source_target_pairs={{0,1},{1,0},{2,3},{3,2},{4,5},{5,4},{6,7},{7,6},{8,9},{9,8},{10,11... | collective-permute-start | bytes 6291464 | tf_op jit(solution)/shard_map/ppermute | solution.py:304
  1397.8 71.5 %collective-permute-start.23 = (bf16[512,2048]{1,0:T(8,128)(2,1)}, bf16[512,2048]{1,0:T(8,128)(2,1)S(1)}, u32[]{:S(2)}, u32[]{:S(2)}) collective-permute-start(bf16[512,2048]{1,0:T(8,128)(2,1)} %get-tuple-element.35), channel_id=1, source_target_pairs={{0,2},{1,3},{2,4},{3,5},{4,6},{5,7},{8,10},{9,11},{10,12},{11,13},... | collective-permute-start | bytes 6291464 | tf_op jit(solution)/shard_map/ppermute | solution.py:308
  (259 other events, 4063.1 us)
Sparse Core Ops, SparseCore 0:
  85.6 93.4 all-gather.3

commit v2 on v1

--- a/solution.py
+++ b/solution.py
@@ -1,8 +1,11 @@
+import functools
 import math
 
 import jax
 import jax.numpy as jnp
 from jax import lax
+from jax.experimental import pallas as pl
+from jax.experimental.pallas import tpu as pltpu
 from jax.sharding import PartitionSpec as P
 
 HEADS = 8
@@ -293,7 +296,975 @@
     )
 
 
+bf, f32 = jnp.bfloat16, jnp.float32
+TOK, HALF = 1024, 512
+VM = 56 * 1024 * 1024
+
+
+def nt(a, b):
+    return lax.dot_general(a, b, (((1,), (1,)), ((), ())), preferred_element_type=f32)
+
+
+def nn(a, b):
+    return lax.dot_general(a, b, (((1,), (0,)), ((), ())), preferred_element_type=f32)
+
+
+def tn(a, b):
+    return lax.dot_general(a, b, (((0,), (0,)), ((), ())), preferred_element_type=f32)
+
+
+def params(n=1, limit=VM):
+    return pltpu.CompilerParams(dimension_semantics=("arbitrary",) * n, vmem_limit_bytes=limit)
+
+
+def cost(flops, nbytes):
+    return pl.CostEstimate(flops=int(flops), bytes_accessed=int(nbytes), transcendentals=0)
+
+
+def turn(head, c, s):
+    first = head[:, :128]
+    lane = lax.broadcasted_iota(jnp.int32, first.shape, 1)
+    partner = jnp.where(lane < 32, pltpu.roll(first, 96, 1), pltpu.roll(first, 32, 1))
+    return jnp.concatenate([first * c + partner * s, head[:, 128:]], axis=1)
+
+
+def gelu_pair(h):
+    cdf = 0.5 * (1.0 + lax.erf(h * (0.5**0.5)))
+    pdf = jnp.exp(-0.5 * (h * h)) * (1.0 / math.sqrt(2.0 * math.pi))
+    return (h * cdf).astype(bf), (cdf + h * pdf).astype(bf)
+
+
+def h_body(units_tiles, n0, n1, w, b, c, s, act, slope, qkv, x):
+    j = pl.program_id(0)
+
+    @pl.when(j == 0)
+    def _():
+        x[:HALF] = n0[...]
+        x[HALF:] = n1[...]
+
+    @pl.when(j < units_tiles)
+    def _():
+        act[...], slope[...] = gelu_pair(nt(x[...], w[...]) + b[...])
+
+    @pl.when((j >= units_tiles) & (j < units_tiles + 2))
+    def _():
+        qkv[0] = turn(nt(x[...], w[...]) + b[...], c[0], s[0]).astype(bf)
+
+    @pl.when(j == units_tiles + 2)
+    def _():
+        qkv[0] = (nt(x[...], w[...]) + b[...]).astype(bf)
+
+
+def h_call(n0, n1, w, b, c, s, t):
+    width = n0.shape[1]
+    rows = w.shape[0]
+    tile = 256
+    units_tiles = (rows - 768) // tile
+    full = lambda *shape: pl.BlockSpec(shape, lambda j: (0,) * len(shape))
+    return pl.pallas_call(
+        functools.partial(h_body, units_tiles),
+        grid=(rows // tile,),
+        in_specs=[
+            full(HALF, width), full(HALF, width),
+            pl.BlockSpec((tile, width), lambda j: (j, 0)),
+            pl.BlockSpec((1, tile), lambda j: (0, j)),
+            pl.BlockSpec((1, TOK, 128), lambda j: (t, 0, 0)), pl.BlockSpec((1, TOK, 128), lambda j: (t, 0, 0)),
+        ],
+        out_specs=[
+            pl.BlockSpec((TOK, tile), lambda j: (0, jnp.minimum(j, units_tiles - 1))),
+            pl.BlockSpec((TOK, tile), lambda j: (0, jnp.minimum(j, units_tiles - 1))),
+            pl.BlockSpec((1, TOK, tile), lambda j: (jnp.maximum(j - units_tiles, 0), 0, 0)),
+        ],
+        out_shape=[
+            jax.ShapeDtypeStruct((TOK, rows - 768), bf),
+            jax.ShapeDtypeStruct((TOK, rows - 768), bf),
+            jax.ShapeDtypeStruct((3, TOK, 256), bf),
+        ],
+        scratch_shapes=[pltpu.VMEM((TOK, width), bf)],
+        compiler_params=params(),
+        cost_estimate=cost(2 * TOK * width * rows, 24e6),
+        name="project",
+    )(n0, n1, w, b, c, s)
+
+
+def attn_body(q, k, v, idq, idk, mixed, lse):
+    scores = nt(q[0], k[0]) * (256 ** -0.5)
+    allowed = idk[0] <= idq[0]
+    scores = jnp.where(allowed, scores, -1e30)
+    top = jnp.max(scores, axis=1, keepdims=True)
+    weights = jnp.exp(scores - top)
+    total = jnp.sum(weights, axis=1, keepdims=True)
+    probs = (weights / total).astype(bf)
+    mixed[...] = nn(probs, v[0]).astype(bf)
+    lse[...] = top + jnp.log(total)
+
+
+def attn_call(qkv, ids_col, ids_row, t):
+    tile = 256
+    return pl.pallas_call(
+        attn_body,
+        grid=(TOK // tile,),
+        in_specs=[
+            pl.BlockSpec((1, tile, 256), lambda i: (0, i, 0)),
+            pl.BlockSpec((1, TOK, 256), lambda i: (1, 0, 0)),
+            pl.BlockSpec((1, TOK, 256), lambda i: (2, 0, 0)),
+            pl.BlockSpec((1, tile, 1), lambda i: (t, i, 0)),
+            pl.BlockSpec((1, 1, TOK), lambda i: (t, 0, 0)),
+        ],
+        out_specs=[
+            pl.BlockSpec((tile, 256), lambda i: (i, 0)),
+            pl.BlockSpec((tile, 1), lambda i: (i, 0)),
+        ],
+        out_shape=[jax.ShapeDtypeStruct((TOK, 256), bf), jax.ShapeDtypeStruct((TOK, 1), f32)],
+        compiler_params=params(),
+        cost_estimate=cost(4 * TOK * TOK * 256, 4e6),
+        name="attend",
+    )(qkv, qkv, qkv, ids_col, ids_row)
+
+
+def attn_back_body(q, k, v, g, idq, idk, lse, cq, sq, ck, sk, out_q, out_kv, sums, acc_k, acc_v, acc_s):
+    i = pl.program_id(0)
+    last = pl.num_programs(0) - 1
+    scale = 256 ** -0.5
+
+    @pl.when(i == 0)
+    def _():
+        acc_k[...] = jnp.zeros_like(acc_k)
+        acc_v[...] = jnp.zeros_like(acc_v)
+        acc_s[...] = jnp.zeros_like(acc_s)
+
+    scores = nt(q[0], k[0]) * scale
+    allowed = idk[0] <= idq[0]
+    probs = jnp.where(allowed, jnp.exp(scores - lse[...]), 0.0)
+    grad_probs = nt(g[...], v[0])
+    inner = jnp.sum(probs * grad_probs, axis=1, keepdims=True)
+    gs = (probs * (grad_probs - inner)).astype(bf)
+    gq = (nn(gs, k[0]) * scale).astype(bf).astype(f32)
+    gq = turn(gq, cq[0], -sq[0])
+    acc_s[0:1, :] += jnp.sum(gq, axis=0, keepdims=True)
+    out_q[0] = gq.astype(bf)
+    acc_k[...] += tn(gs, q[0])
+    acc_v[...] += tn(probs.astype(bf), g[...])
+
+    @pl.when(i == last)
+    def _():
+        gk = (acc_k[...] * scale).astype(bf).astype(f32)
+        gk = turn(gk, ck[0], -sk[0])
+        out_kv[0] = gk.astype(bf)
+        gv = acc_v[...].astype(bf)
+        out_kv[1] = gv
+        acc_s[1:2, :] = jnp.sum(gk, axis=0, keepdims=True)
+        acc_s[2:3, :] = jnp.sum(gv.astype(f32), axis=0, keepdims=True)
+        sums[...] = acc_s[...]
+
+
+def attn_back_call(qkv, gmix, ids_col, ids_row, lse, c, s, t):
+    tile = 256
+    return pl.pallas_call(
+        attn_back_body,
+        grid=(TOK // tile,),
+        in_specs=[
+            pl.BlockSpec((1, tile, 256), lambda i: (0, i, 0)),
+            pl.BlockSpec((1, TOK, 256), lambda i: (1, 0, 0)),
+            pl.BlockSpec((1, TOK, 256), lambda i: (2, 0, 0)),
+            pl.BlockSpec((tile, 256), lambda i: (i, 0)),
+            pl.BlockSpec((1, tile, 1), lambda i: (t, i, 0)),
+            pl.BlockSpec((1, 1, TOK), lambda i: (t, 0, 0)),
+            pl.BlockSpec((tile, 1), lambda i: (i, 0)),
+            pl.BlockSpec((1, tile, 128), lambda i: (t, i, 0)),
+            pl.BlockSpec((1, tile, 128), lambda i: (t, i, 0)),
+            pl.BlockSpec((1, TOK, 128), lambda i: (t, 0, 0)),
+            pl.BlockSpec((1, TOK, 128), lambda i: (t, 0, 0)),
+        ],
+        out_specs=[
+            pl.BlockSpec((1, tile, 256), lambda i: (0, i, 0)),
+            pl.BlockSpec((2, TOK, 256), lambda i: (0, 0, 0)),
+            pl.BlockSpec((8, 256), lambda i: (0, 0)),
+        ],
+        out_shape=[
+            jax.ShapeDtypeStruct((1, TOK, 256), bf),
+            jax.ShapeDtypeStruct((2, TOK, 256), bf),
+            jax.ShapeDtypeStruct((8, 256), f32),
+        ],
+        scratch_shapes=[pltpu.VMEM((TOK, 256), f32), pltpu.VMEM((TOK, 256), f32), pltpu.VMEM((8, 256), f32)],
+        compiler_params=params(),
+        cost_estimate=cost(10 * TOK * TOK * 256, 6e6),
+        name="attend_back",
+    )(qkv, qkv, qkv, gmix, ids_col, ids_row, lse, c, s, c, s)
+
+
+def p_body(act, mixed, wd, wo, own, sib):
+    out = nn(act[...], wd[...]) + nn(mixed[...], wo[...])
+    own[...] = out[:HALF]
+    sib[...] = out[HALF:].astype(bf)
+
+
+def p_call(act, mixed, w):
+    units, width = act.shape[1], w.shape[1]
+    tile = 256
+    full = lambda *shape: pl.BlockSpec(shape, lambda j: (0,) * len(shape))
+    return pl.pallas_call(
+        p_body,
+        grid=(width // tile,),
+        in_specs=[
+            full(TOK, units), full(TOK, 256),
+            pl.BlockSpec((units, tile), lambda j: (0, j)),
+            pl.BlockSpec((256, tile), lambda j: (units // 256, j)),
+        ],
+        out_specs=[pl.BlockSpec((HALF, tile), lambda j: (0, j))] * 2,
+        out_shape=[jax.ShapeDtypeStruct((HALF, width), f32), jax.ShapeDtypeStruct((HALF, width), bf)],
+        compiler_params=params(),
+        cost_estimate=cost(2 * TOK * width * (units + 256), 16e6),
+        name="combine",
+    )(act, mixed, w, w)
+
+
+def ga_body(units_tiles, g0, g1, w, slope, gh, gmix, x):
+    j = pl.program_id(0)
+
+    @pl.when(j == 0)
+    def _():
+        x[:HALF] = g0[...]
+        x[HALF:] = g1[...]
+
+    ga = nt(x[...], w[...]).astype(bf)
+
+    @pl.when(j < units_tiles)
+    def _():
+        gh[...] = (ga.astype(f32) * slope[...].astype(f32)).astype(bf)
+
+    @pl.when(j == units_tiles)
+    def _():
+        gmix[...] = ga
+
+
+def ga_call(g0, g1, w, slope):
+    width, rows = w.shape[1], w.shape[0]
+    tile = 256
+    units_tiles = rows // tile - 1
+    full = lambda *shape: pl.BlockSpec(shape, lambda j: (0,) * len(shape))
+    return pl.pallas_call(
+        functools.partial(ga_body, units_tiles),
+        grid=(rows // tile,),
+        in_specs=[
+            full(HALF, width), full(HALF, width),
+            pl.BlockSpec((tile, width), lambda j: (j, 0)),
+            pl.BlockSpec((TOK, tile), lambda j: (0, jnp.minimum(j, units_tiles - 1))),
+        ],
+        out_specs=[
+            pl.BlockSpec((TOK, tile), lambda j: (0, jnp.minimum(j, units_tiles - 1))),
+            full(TOK, 256),
+        ],
+        out_shape=[jax.ShapeDtypeStruct((TOK, rows - 256), bf), jax.ShapeDtypeStruct((TOK, 256), bf)],
+        scratch_shapes=[pltpu.VMEM((TOK, width), bf)],
+        compiler_params=params(),
+        cost_estimate=cost(2 * TOK * width * rows, 16e6),
+        name="pull",
+    )(g0, g1, w, slope)
+
+
+def u_body(gh, gq, gkv, wu, wq, own, sib):
+    out = nn(gh[...], wu[...]) + nn(gq[0], wq[0:256]) + nn(gkv[0], wq[256:512]) + nn(gkv[1], wq[512:768])
+    own[...] = out[:HALF]
+    sib[...] = out[HALF:].astype(bf)
+
+
+def u_call(gh, gq, gkv, w_up, w_qkv):
+    units, width = gh.shape[1], w_up.shape[1]
+    tile = 256
+    full = lambda *shape: pl.BlockSpec(shape, lambda j: (0,) * len(shape))
+    return pl.pallas_call(
+        u_body,
+        grid=(width // tile,),
+        in_specs=[
+            full(TOK, units), full(1, TOK, 256), full(2, TOK, 256),
+            pl.BlockSpec((units, tile), lambda j: (0, j)),
+            pl.BlockSpec((768, tile), lambda j: (0, j)),
+        ],
+        out_specs=[pl.BlockSpec((HALF, tile), lambda j: (0, j))] * 2,
+        out_shape=[jax.ShapeDtypeStruct((HALF, width), f32), jax.ShapeDtypeStruct((HALF, width), bf)],
+        compiler_params=params(),
+        cost_estimate=cost(2 * TOK * width * (units + 768), 20e6),
+        name="push",
+    )(gh, gq, gkv, w_up, w_qkv)
+
+
+def g2_body(acts, mixes, rights, term, acc, left, right, out, sems):
+    units = acts.shape[2]
+    rows = units + 256
+
+    def copies(k):
+        slot = k % 2
+        pairs = [
+            (acts.at[k], left.at[slot, :, pl.ds(0, units)]),
+            (mixes.at[k], left.at[slot, :, pl.ds(units, 256)]),
+            (rights.at[k], right.at[slot]),
+        ]
+        return [pltpu.make_async_copy(a, b, sems.at[slot, i]) for i, (a, b) in enumerate(pairs)]
+
+    for cp in copies(0):
+        cp.start()
+    for k in range(4):
+        if k < 3:
+            for cp in copies(k + 1):
+                cp.start()
+        for cp in copies(k):
+            cp.wait()
+        slot = k % 2
+
+        @pl.loop(0, rows // 256)
+        def _(m):
+            cols = pl.ds(pl.multiple_of(m * 256, 256), 256)
+            part = tn(left[slot, :, cols], right[slot])
+            if k == 0:
+                acc[cols, :] = part
+            elif k < 3:
+                acc[cols, :] += part
+            else:
+                out[cols, :] = (acc[cols, :] + part).astype(bf)
+    done = pltpu.make_async_copy(out, term, sems.at[0, 0])
+    done.start()
+    done.wait()
+
+
+def g2_call(acts, mixes, rights):
+    units, width = acts.shape[2], rights.shape[2]
+    rows = units + 256
+    return pl.pallas_call(
+        g2_body,
+        in_specs=[pl.BlockSpec(memory_space=pl.ANY)] * 3,
+        out_specs=pl.BlockSpec(memory_space=pl.ANY),
+        out_shape=jax.ShapeDtypeStruct((rows, width), bf),
+        scratch_shapes=[
+            pltpu.VMEM((rows, width), f32),
+            pltpu.VMEM((2, TOK, rows), bf),
+            pltpu.VMEM((2, TOK, width), bf),
+            pltpu.VMEM((rows, width), bf),
+            pltpu.SemaphoreType.DMA((2, 4)),
+        ],
+        compiler_params=pltpu.CompilerParams(vmem_limit_bytes=VM),
+        cost_estimate=cost(2 * 4096 * width * rows, 40e6),
+        name="grad_out_weights",
+    )(acts, mixes, rights)
+
+
+def g1_body(
+    ghs, gps, rights, plain, gain, shift, term, sides, sums, acc, acc_s, left, right, out, w, sems, sem_w
+):
+    units = ghs.shape[2]
+    rows = units + 768
+    tiles = rows // 256
+
+    def copies(k):
+        slot = k % 2
+        pairs = [(ghs.at[k], left.at[slot, :, pl.ds(0, units)])]
+        pairs += [(gps.at[k, i], left.at[slot, :, pl.ds(units + 256 * i, 256)]) for i in range(3)]
+        pairs += [(rights.at[k], right.at[slot])]
+        return [pltpu.make_async_copy(a, b, sems.at[slot, i]) for i, (a, b) in enumerate(pairs)]
+
+    weights = pltpu.make_async_copy(plain, w, sem_w)
+    weights.start()
+    for cp in copies(0):
+        cp.start()
+    ones = jnp.ones((TOK, 128), bf)
+    sides[...] = jnp.zeros_like(sides)
+    for k in range(4):
+        if k < 3:
+            for cp in copies(k + 1):
+                cp.start()
+        for cp in copies(k):
+            cp.wait()
+        slot = k % 2
+        if k == 3:
+            weights.wait()
+
+        @pl.loop(0, tiles)
+        def _(m):
+            cols = pl.ds(pl.multiple_of(m * 256, 256), 256)
+            piece = left[slot, :, cols]
+            part = tn(piece, right[slot])
+            part_s = tn(piece, ones)
+            if k == 0:
+                acc[cols, :] = part
+                acc_s[cols, :] = part_s
+            elif k < 3:
+                acc[cols, :] += part
+                acc_s[cols, :] += part_s
+            else:
+                raw = acc[cols, :] + part
+                total = acc_s[cols, :] + part_s
+                acc_s[cols, :] = total
+                total = total[:, 0:1]
+                which = (m >= units // 256).astype(jnp.int32)
+                g = jnp.where(which == 0, gain[0:1, :], gain[1:2, :])
+                s = jnp.where(which == 0, shift[0:1, :], shift[1:2, :])
+                out[cols, :] = (raw * g + total * s).astype(bf)
+                wt = w[cols, :].astype(f32)
+                one = jnp.sum(wt * raw, axis=0, keepdims=True)
+                two = jnp.sum(wt * total, axis=0, keepdims=True)
+
+                @pl.when(which == 0)
+                def _():
+                    sides[0:1, :] += one
+                    sides[1:2, :] += two
+
+                @pl.when(which == 1)
+                def _():
+                    sides[2:3, :] += one
+                    sides[3:4, :] += two
+
+    done = pltpu.make_async_copy(out, term, sem_w)
+    done.start()
+    sums[...] = acc_s[...]
+    done.wait()
+
+
+def g1_call(ghs, gps, rights, plain, gain, shift):
+    units, width = ghs.shape[2], rights.shape[2]
+    rows = units + 768
+    anys = pl.BlockSpec(memory_space=pl.ANY)
+    vmem = pl.BlockSpec(memory_space=pltpu.VMEM)
+    return pl.pallas_call(
+        g1_body,
+        in_specs=[anys] * 4 + [vmem] * 2,
+        out_specs=[anys, vmem, vmem],
+        out_shape=[
+            jax.ShapeDtypeStruct((rows, width), bf),
+            jax.ShapeDtypeStruct((8, width), f32),
+            jax.ShapeDtypeStruct((rows, 128), f32),
+        ],
+        scratch_shapes=[
+            pltpu.VMEM((rows, width), f32),
+            pltpu.VMEM((rows, 128), f32),
+            pltpu.VMEM((2, TOK, rows), bf),
+            pltpu.VMEM((2, TOK, width), bf),
+            pltpu.VMEM((rows, width), bf),
+            pltpu.VMEM((rows, width), bf),
+            pltpu.SemaphoreType.DMA((2, 6)),
+            pltpu.SemaphoreType.DMA,
+        ],
+        compiler_params=pltpu.CompilerParams(vmem_limit_bytes=VM),
+        cost_estimate=cost(2 * 4096 * width * rows, 50e6),
+        name="grad_in_weights",
+    )(ghs, gps, rights, plain, gain, shift)
+
+
 LANES = 128
+
+
+MESH = pl.DeviceIdType.MESH
+
+
+def line_order(z, t):
+    near = jnp.where(z < 2, z + 1, z - 1)
+    mid = jnp.where(z == 0, 2, jnp.where(z == 1, 0, jnp.where(z == 2, 3, 1)))
+    far = jnp.where(z < 2, 3, 0)
+    return jnp.where(t == 0, z, jnp.where(t == 1, near, jnp.where(t == 2, mid, far)))
+
+
+def remote(src, dst, send, recv, s, f):
+    return pltpu.make_async_remote_copy(
+        src_ref=src, dst_ref=dst, send_sem=send, recv_sem=recv, device_id=(s, f), device_id_type=MESH
+    )
+
+
+def line_barrier(s, f, z):
+    barrier = pltpu.get_barrier_semaphore()
+
+    @pl.when(z < 3)
+    def _():
+        pl.semaphore_signal(barrier, inc=1, device_id=(s, f + 2), device_id_type=MESH)
+
+    @pl.when(z > 0)
+    def _():
+        pl.semaphore_signal(barrier, inc=1, device_id=(s, f - 2), device_id_type=MESH)
+
+    pl.semaphore_signal(barrier, inc=1, device_id=(s, f + 1 - 2 * (f % 2)), device_id_type=MESH)
+
+    @pl.when((z == 0) | (z == 3))
+    def _():
+        pl.semaphore_wait(barrier, 2)
+
+    @pl.when((z == 1) | (z == 2))
+    def _():
+        pl.semaphore_wait(barrier, 3)
+
+
+def line_step(buf, k, z, s, f, sems, held=None):
+    send_up, recv_up, send_dn, recv_dn = sems
+    own = pl.ds(0, HALF)
+
+    @pl.when((z - k >= 0) & (z < 3))
+    def _():
+        ref = buf.at[z - k, own]
+        remote(ref if held is None else held, ref, send_up.at[k], recv_up.at[k], s, f + 2).start()
+
+    @pl.when((z + k <= 3) & (z > 0))
+    def _():
+        ref = buf.at[z + k, own]
+        remote(ref if held is None else held, ref, send_dn.at[k], recv_dn.at[k], s, f - 2).start()
+
+
+def line_arrive(buf, k, z, s, f, sems):
+    send_up, recv_up, send_dn, recv_dn = sems
+    own = pl.ds(0, HALF)
+
+    @pl.when(z - 1 - k >= 0)
+    def _():
+        ref = buf.at[z - 1 - k, own]
+        remote(ref, ref, send_up.at[k], recv_up.at[k], s, f - 2).wait_recv()
+
+    @pl.when(z + 1 + k <= 3)
+    def _():
+        ref = buf.at[z + 1 + k, own]
+        remote(ref, ref, send_dn.at[k], recv_dn.at[k], s, f + 2).wait_recv()
+
+
+def line_sent(buf, k, z, s, f, sems):
+    send_up, recv_up, send_dn, recv_dn = sems
+    own = pl.ds(0, HALF)
+
+    @pl.when((z - k >= 0) & (z < 3))
+    def _():
+        ref = buf.at[z - k, own]
+        remote(ref, ref, send_up.at[k], recv_up.at[k], s, f + 2).wait_send()
+
+    @pl.when((z + k <= 3) & (z > 0))
+    def _():
+        ref = buf.at[z + k, own]
+        remote(ref, ref, send_dn.at[k], recv_dn.at[k], s, f - 2).wait_send()
+
+
+def core_copy(buf, b, s, f, sems, held=None):
+    send, recv = sems
+    return remote(
+        buf.at[b, pl.ds(0, HALF)] if held is None else held, buf.at[b, pl.ds(HALF, HALF)], send.at[b], recv.at[b], s, f + 1 - 2 * (f % 2)
+    )
+
+
+def new_blocks(k, z, act):
+    if k == 0:
+        act(z)
+        return
+
+    @pl.when(z - k >= 0)
+    def _():
+        act(z - k)
+
+    @pl.when(z + k <= 3)
+    def _():
+        act(z + k)
+
+
+def forward_body(
+    own_n, own_g, w_in_h, w_out_h, bias, cos, sin, idc, idr,
+    n_all, g_all, act_o, slope_o, qkv_o, mixed_o, lse_o, own_o, sib_o,
+    w_in, w_out, x, act, slope, qkv, mixed, lse, p_own, p_sib,
+    load, line_n0, line_n1, line_n2, line_n3, line_g0, line_g1, line_g2, line_g3,
+    core_n0, core_n1, core_p0, core_p1, out_sems,
+):
+    s, f = lax.axis_index("seq"), lax.axis_index("fsdp")
+    z = f // 2
+    line_n, line_g = (line_n0, line_n1, line_n2, line_n3), (line_g0, line_g1, line_g2, line_g3)
+    core_n, core_p = (core_n0, core_n1), (core_p0, core_p1)
+    own, other = pl.ds(0, HALF), pl.ds(HALF, HALF)
+    units = act.shape[1]
+    first = [
+        pltpu.make_async_copy(own_n, x.at[own], load.at[0]),
+        pltpu.make_async_copy(own_g, p_sib, load.at[3]),
+        pltpu.make_async_copy(w_in_h, w_in, load.at[1]),
+        pltpu.make_async_copy(w_out_h, w_out, load.at[2]),
+    ]
+    keep = [
+        pltpu.make_async_copy(x.at[own], n_all.at[z, own], load.at[0]),
+        pltpu.make_async_copy(p_sib, g_all.at[z, own], load.at[3]),
+    ]
+    for copy in first:
+        copy.start()
+    line_barrier(s, f, z)
+
+    def outs(b):
+        return [
+            pltpu.make_async_copy(src, dst.at[b], out_sems.at[i])
+            for i, (src, dst) in enumerate(
+                [(act, act_o), (slope, slope_o), (qkv, qkv_o), (mixed, mixed_o), (lse, lse_o), (p_own, own_o)]
+            )
+        ]
+
+    def send_sib(b):
+        return remote(p_sib, sib_o.at[b], core_p[0].at[b], core_p[1].at[b], s, f + 1 - 2 * (f % 2))
+
+    for t in range(4):
+        b = line_order(z, t)
+        top = pltpu.make_async_copy(n_all.at[b, own], x.at[own], load.at[0])
+        low_half = pltpu.make_async_copy(n_all.at[b, other], x.at[other], load.at[4])
+        if t == 0:
+            line_step(n_all, 0, z, s, f, line_n, own_n)
+            core_copy(n_all, z, s, f, core_n, own_n).start()
+            for copy, then in zip(first[:2], keep):
+                copy.wait()
+                then.start()
+        else:
+            line_arrive(n_all, t - 1, z, s, f, line_n)
+            if t < 3:
+                line_step(n_all, t, z, s, f, line_n)
+            else:
+                line_step(g_all, 0, z, s, f, line_g, own_g)
+            new_blocks(t, z, lambda v: core_copy(n_all, v, s, f, core_n).start())
+            top.start()
+        core_copy(n_all, b, s, f, core_n).wait_recv()
+        low_half.start()
+        if t == 0:
+            for copy in first[2:] + keep:
+                copy.wait()
+        else:
+            top.wait()
+            before = line_order(z, t - 1)
+            for copy in outs(before):
+                copy.wait()
+            send_sib(before).wait_send()
+        low_half.wait()
+
+        @pl.loop(0, units // 256)
+        def _(j):
+            at = pl.ds(pl.multiple_of(j * 256, 256), 256)
+            h = nt(x[...], w_in[at, :]) + bias[:, at]
+            act[:, at], slope[:, at] = gelu_pair(h)
+
+        @pl.loop(0, 2)
+        def _(j):
+            at = pl.ds(pl.multiple_of(units + j * 256, 256), 256)
+            h = nt(x[...], w_in[at, :]) + bias[:, at]
+            qkv[j] = turn(h, cos[b], sin[b]).astype(bf)
+
+        at = pl.ds(units + 512, 256)
+        qkv[2] = (nt(x[...], w_in[at, :]) + bias[:, at]).astype(bf)
+
+        @pl.loop(0, TOK // 256)
+        def _(i):
+            rows = pl.ds(pl.multiple_of(i * 256, 256), 256)
+            scores = nt(qkv[0, rows, :], qkv[1]) * (256 ** -0.5)
+            scores = jnp.where(idr[b] <= idc[b, rows, :], scores, -1e30)
+            top_score = jnp.max(scores, axis=1, keepdims=True)
+            weights = jnp.exp(scores - top_score)
+            total = jnp.sum(weights, axis=1, keepdims=True)
+            probs = (weights / total).astype(bf)
+            mixed[rows, :] = nn(probs, qkv[2]).astype(bf)
+            lse[rows, :] = jnp.broadcast_to(top_score + jnp.log(total), (256, LANES))
+
+        @pl.loop(0, p_own.shape[1] // 256)
+        def _(j):
+            at = pl.ds(pl.multiple_of(j * 256, 256), 256)
+            out = nn(act[...], w_out[pl.ds(0, units), at]) + nn(mixed[...], w_out[pl.ds(units, 256), at])
+            p_own[:, at] = out[:HALF].astype(bf)
+            p_sib[:, at] = out[HALF:].astype(bf)
+
+        for copy in outs(b):
+            copy.start()
+        send_sib(b).start()
+
+    last = line_order(z, 3)
+    for copy in outs(last):
+        copy.wait()
+    send_sib(last).wait_send()
+    for b in range(4):
+        core_copy(n_all, b, s, f, core_n).wait_send()
+        send_sib(b).wait_recv()
+    for k in range(3):
+        line_sent(n_all, k, z, s, f, line_n)
+    line_arrive(g_all, 0, z, s, f, line_g)
+    line_sent(g_all, 0, z, s, f, line_g)
+
+
+def forward_call(own_n, own_g, w_in, w_out, bias, cos, sin, ids_col, ids_row):
+    width = own_n.shape[1]
+    units = w_in.shape[0] - 768
+    anys = pl.BlockSpec(memory_space=pl.ANY)
+    vmem = pl.BlockSpec(memory_space=pltpu.VMEM)
+    shape = jax.ShapeDtypeStruct
+    dma = lambda n: pltpu.SemaphoreType.DMA((n,))
+    return pl.pallas_call(
+        forward_body,
+        in_specs=[anys] * 4 + [vmem] * 5,
+        out_specs=[anys] * 9,
+        out_shape=[
+            shape((4, TOK, width), bf), shape((4, TOK, width), bf),
+            shape((4, TOK, units), bf), shape((4, TOK, units), bf), shape((4, 3, TOK, 256), bf),
+            shape((4, TOK, 256), bf), shape((4, TOK, LANES), f32),
+            shape((4, HALF, width), bf), shape((4, HALF, width), bf),
+        ],
+        scratch_shapes=[
+            pltpu.VMEM(w_in.shape, bf), pltpu.VMEM(w_out.shape, bf), pltpu.VMEM((TOK, width), bf),
+            pltpu.VMEM((TOK, units), bf), pltpu.VMEM((TOK, units), bf), pltpu.VMEM((3, TOK, 256), bf),
+            pltpu.VMEM((TOK, 256), bf), pltpu.VMEM((TOK, LANES), f32),
+            pltpu.VMEM((HALF, width), bf), pltpu.VMEM((HALF, width), bf),
+            dma(5), dma(3), dma(3), dma(3), dma(3), dma(3), dma(3), dma(3), dma(3),
+            dma(4), dma(4), dma(4), dma(4), dma(6),
+        ],
+        compiler_params=pltpu.CompilerParams(
+            vmem_limit_bytes=60 * 1024 * 1024, collective_id=0, has_side_effects=True
+        ),
+        cost_estimate=cost(8 * TOK * width * (w_in.shape[0] + w_out.shape[0]), 200e6),
+        name="forward",
+    )(own_n, own_g, w_in, w_out, bias, cos, sin, ids_col, ids_row)
+
+
+def sum_add(dst, parts):
+    @pl.loop(0, HALF // 64)
+    def _(i):
+        rows = pl.ds(pl.multiple_of(i * 64, 64), 64)
+        total = parts[0][rows, :].astype(f32)
+        for part in parts[1:]:
+            total = total + part[rows, :].astype(f32)
+        dst[rows, :] = total.astype(bf)
+
+
+def line_sum_step(k, z, s, f, own, sib, land, stage, out, loads, sends, recvs):
+    for way in range(2):
+        d = z - 3 + k if way == 0 else z + 3 - k
+        valid = d >= 0 if way == 0 else d <= 3
+        to = f - 2 if way == 0 else f + 2
+        inner = z < 3 if way == 0 else z > 0
+        was = z - 4 + k >= 0 if way == 0 else z + 4 - k <= 3
+
+        @pl.when(valid)
+        def _():
+            terms = [
+                pltpu.make_async_copy(own.at[d], stage.at[0], loads.at[0]),
+                pltpu.make_async_copy(sib.at[d], stage.at[1], loads.at[1]),
+            ]
+            for copy in terms:
+                copy.start()
+            if k > 0:
+
+                @pl.when(was)
+                def _():
+                    remote(out.at[way], land.at[way, k - 1], sends.at[way, k - 1], recvs.at[way, k - 1], s, to).wait_send()
+
+                @pl.when(inner)
+                def _():
+                    remote(out.at[way], land.at[way, k - 1], sends.at[way, k - 1], recvs.at[way, k - 1], s, to).wait_recv()
+                    came = pltpu.make_async_copy(land.at[way, k - 1], stage.at[2], loads.at[2])
+                    came.start()
+                    came.wait()
+
+            for copy in terms:
+                copy.wait()
+            if k > 0:
+
+                @pl.when(inner)
+                def _():
+                    sum_add(out.at[way], [stage.at[0], stage.at[1], stage.at[2]])
+
+                @pl.when(jnp.logical_not(inner))
+                def _():
+                    sum_add(out.at[way], [stage.at[0], stage.at[1]])
+            else:
+                sum_add(out.at[way], [stage.at[0], stage.at[1]])
+            remote(out.at[way], land.at[way, k], sends.at[way, k], recvs.at[way, k], s, to).start()
+
+
+def line_sum_end(z, s, f, own, sib, land, stage, out, loads, sends, recvs, result):
+    terms = [
+        pltpu.make_async_copy(own.at[z], stage.at[0], loads.at[0]),
+        pltpu.make_async_copy(sib.at[z], stage.at[1], loads.at[1]),
+    ]
+    for copy in terms:
+        copy.start()
+    for copy in terms:
+        copy.wait()
+
+    for way in range(2):
+        to = f - 2 if way == 0 else f + 2
+        sent = z > 0 if way == 0 else z < 3
+        got = z < 3 if way == 0 else z > 0
+
+        @pl.when(sent)
+        def _():
+            remote(out.at[way], land.at[way, 2], sends.at[way, 2], recvs.at[way, 2], s, to).wait_send()
+
+        @pl.when(got)
+        def _():
+            remote(out.at[way], land.at[way, 2], sends.at[way, 2], recvs.at[way, 2], s, to).wait_recv()
+            came = pltpu.make_async_copy(land.at[way, 2], stage.at[2], loads.at[2])
+            came.start()
+            came.wait()
+            sum_add(stage.at[0], [stage.at[0], stage.at[2]])
+
+    sum_add(stage.at[0], [stage.at[0], stage.at[1]])
+    copy = pltpu.make_async_copy(stage.at[0], result, loads.at[0])
+    copy.start()
+    copy.wait()
+
+
+def backward_body(
+    g_part, w_in_h, w_out_h, slope_h, qkv_h, lse_h, p_own, p_sib, cos, sin, idc, idr,
+    g_all, gh_o, gp_o, own_o, sib_o, branch, land, sums,
+    w_in, w_out, x, slope, qkv, lse, gh, gmix, gp, acc_k, acc_v, u_own, u_sib, stage, rs_out,
+    load, l0, l1, l2, l3, core_0, core_1, core_u0, core_u1, out_sems, rs_send, rs_recv,
+):
+    s, f = lax.axis_index("seq"), lax.axis_index("fsdp")
+    z = f // 2
+    line = (l0, l1, l2, l3)
+    core = (core_0, core_1)
+    own, other = pl.ds(0, HALF), pl.ds(HALF, HALF)
+    units = gh.shape[1]
+    scale = 256 ** -0.5
+    first = [
+        pltpu.make_async_copy(w_in_h, w_in, load.at[0]),
+        pltpu.make_async_copy(w_out_h, w_out, load.at[1]),
+    ]
+    for copy in first:
+        copy.start()
+    line_barrier(s, f, z)
+    swap = lambda b: core_copy(g_all, b, s, f, core)
+    new_blocks(0, z, lambda b: swap(b).start())
+    line_step(g_all, 1, z, s, f, line)
+    new_blocks(1, z, lambda b: swap(b).start())
+    reduce_args = (z, s, f, p_own, p_sib, land, stage, rs_out, load.at[pl.ds(8, 3)], rs_send, rs_recv)
+    line_sum_step(0, *reduce_args)
+    sums[...] = jnp.zeros_like(sums)
+
+    def ins(b):
+        return [
+            pltpu.make_async_copy(src.at[b], dst, load.at[2 + i])
+            for i, (src, dst) in enumerate([(slope_h, slope), (qkv_h, qkv), (lse_h, lse)])
+        ]
+
+    def outs(b):
+        return [
+            pltpu.make_async_copy(src, dst.at[b], out_sems.at[i])
+            for i, (src, dst) in enumerate([(gh, gh_o), (gp, gp_o), (u_own, own_o)])
+        ]
+
+    def send_sib(b):
+        return remote(u_sib, sib_o.at[b], core_u0.at[b], core_u1.at[b], s, f + 1 - 2 * (f % 2))
+
+    for t in range(4):
+        b = line_order(z, t)
+        for copy in ins(b):
+            copy.start()
+        if t == 3:
+            line_arrive(g_all, 2, z, s, f, line)
+            new_blocks(3, z, lambda v: swap(v).start())
+        top = pltpu.make_async_copy(g_all.at[b, own], x.at[own], load.at[5])
+        top.start()
+        swap(b).wait_recv()
+        low_half = pltpu.make_async_copy(g_all.at[b, other], x.at[other], load.at[6])
+        low_half.start()
+        if t == 0:
+            for copy in first:
+                copy.wait()
+        else:
+            before = line_order(z, t - 1)
+            for copy in outs(before):
+                copy.wait()
+            send_sib(before).wait_send()
+        for copy in ins(b):
+            copy.wait()
+        top.wait()
+        low_half.wait()
+
+        @pl.loop(0, units // 256)
+        def _(j):
+            at = pl.ds(pl.multiple_of(j * 256, 256), 256)
+            ga = nt(x[...], w_out[at, :]).astype(bf)
+            gh[:, at] = (ga.astype(f32) * slope[:, at].astype(f32)).astype(bf)
+
+        gmix[...] = nt(x[...], w_out[pl.ds(units, 256), :]).astype(bf)
+        acc_k[...] = jnp.zeros_like(acc_k)
+        acc_v[...] = jnp.zeros_like(acc_v)
+
+        @pl.loop(0, TOK // 256)
+        def _(i):
+            rows = pl.ds(pl.multiple_of(i * 256, 256), 256)
+            q, g = qkv[0, rows, :], gmix[rows, :]
+            scores = nt(q, qkv[1]) * scale
+            allowed = idr[b] <= idc[b, rows, :]
+            probs = jnp.where(allowed, jnp.exp(scores - lse[rows, 0:1]), 0.0)
+            grad_probs = nt(g, qkv[2])
+            inner = jnp.sum(probs * grad_probs, axis=1, keepdims=True)
+            gs = (probs * (grad_probs - inner)).astype(bf)
+            gq = (nn(gs, qkv[1]) * scale).astype(bf).astype(f32)
+            gq = turn(gq, cos[b, rows, :], -sin[b, rows, :])
+            sums[0:1, :] += jnp.sum(gq, axis=0, keepdims=True)
+            gp[0, rows, :] = gq.astype(bf)
+            acc_k[...] += tn(gs, q)
+            acc_v[...] += tn(probs.astype(bf), g)
+
+        gk = (acc_k[...] * scale).astype(bf).astype(f32)
+        gk = turn(gk, cos[b], -sin[b])
+        sums[1:2, :] += jnp.sum(gk, axis=0, keepdims=True)
+        gp[1] = gk.astype(bf)
+        gv = acc_v[...].astype(bf)
+        sums[2:3, :] += jnp.sum(gv.astype(f32), axis=0, keepdims=True)
+        gp[2] = gv
+        if t == 1:
+            line_arrive(g_all, 1, z, s, f, line)
+            line_step(g_all, 2, z, s, f, line)
+            new_blocks(2, z, lambda v: swap(v).start())
+            line_sum_step(1, *reduce_args)
+        if t == 3:
+            line_sum_step(2, *reduce_args)
+
+        @pl.loop(0, u_own.shape[1] // 256)
+        def _(j):
+            at = pl.ds(pl.multiple_of(j * 256, 256), 256)
+            out = nn(gh[...], w_in[pl.ds(0, units), at])
+            for i in range(3):
+                out = out + nn(gp[i], w_in[pl.ds(units + 256 * i, 256), at])
+            u_own[:, at] = out[:HALF].astype(bf)
+            u_sib[:, at] = out[HALF:].astype(bf)
+
+        for copy in outs(b):
+            copy.start()
+        send_sib(b).start()
+
+    line_sum_end(*reduce_args, branch)
+    last = line_order(z, 3)
+    for copy in outs(last):
+        copy.wait()
+    send_sib(last).wait_send()
+    for b in range(4):
+        swap(b).wait_send()
+        send_sib(b).wait_recv()
+    for k in (1, 2):
+        line_sent(g_all, k, z, s, f, line)
+
+
+def backward_call(g_part, w_in, w_out, slope, qkv, lse, p_own, p_sib, cos, sin, ids_col, ids_row):
+    width = w_in.shape[1]
+    units = w_in.shape[0] - 768
+    anys = pl.BlockSpec(memory_space=pl.ANY)
+    vmem = pl.BlockSpec(memory_space=pltpu.VMEM)
+    shape = jax.ShapeDtypeStruct
+    dma = lambda *n: pltpu.SemaphoreType.DMA(n)
+    return pl.pallas_call(
+        backward_body,
+        in_specs=[anys] * 8 + [vmem] * 4,
+        out_specs=[anys] * 7 + [vmem],
+        out_shape=[
+            shape((4, TOK, width), bf), shape((4, TOK, units), bf), shape((4, 3, TOK, 256), bf),
+            shape((4, HALF, width), bf), shape((4, HALF, width), bf), shape((HALF, width), bf),
+            shape((2, 3, HALF, width), bf), shape((8, 256), f32),
+        ],
+        input_output_aliases={0: 0},
+        scratch_shapes=[
+            pltpu.VMEM(w_in.shape, bf), pltpu.VMEM(w_out.shape, bf), pltpu.VMEM((TOK, width), bf),
+            pltpu.VMEM((TOK, units), bf), pltpu.VMEM((3, TOK, 256), bf), pltpu.VMEM((TOK, LANES), f32),
+            pltpu.VMEM((TOK, units), bf), pltpu.VMEM((TOK, 256), bf), pltpu.VMEM((3, TOK, 256), bf),
+            pltpu.VMEM((TOK, 256), f32), pltpu.VMEM((TOK, 256), f32),
+            pltpu.VMEM((HALF, width), bf), pltpu.VMEM((HALF, width), bf),
+            pltpu.VMEM((3, HALF, width), bf), pltpu.VMEM((2, HALF, width), bf),
+            dma(11), dma(3), dma(3), dma(3), dma(3), dma(4), dma(4), dma(4), dma(4), dma(3),
+            dma(2, 3), dma(2, 3),
+        ],
+        compiler_params=pltpu.CompilerParams(
+            vmem_limit_bytes=62 * 1024 * 1024, collective_id=1, has_side_effects=True
+        ),
+        cost_estimate=cost(8 * TOK * width * (w_in.shape[0] + w_out.shape[0]), 200e6),
+        name="backward",
+    )(g_part, w_in, w_out, slope, qkv, lse, p_own, p_sib, cos, sin, ids_col, ids_row)
 
 
 def pick(slices, which):
@@ -348,6 +1319,37 @@
 
 def swap_seq(value, bit):
     return lax.ppermute(value, "seq", [(i, i ^ bit) for i in range(4)])
+
+
+def gather_small(value, f):
+    gathered = value[None]
+    for bit in (1, 2, 4):
+        other = lax.ppermute(gathered, "fsdp", [(i, i ^ bit) for i in range(8)])
+        low_side = (f // bit) % 2 == 0
+        gathered = jnp.concatenate(
+            [jnp.where(low_side, gathered, other), jnp.where(low_side, other, gathered)]
+        )
+    return gathered
+
+
+def scatter_small(value, f):
+    for bit in (4, 2, 1):
+        half = value.shape[0] // 2
+        low_side = (f // bit) % 2 == 0
+        sent = jnp.where(low_side, value[half:], value[:half])
+        kept = jnp.where(low_side, value[:half], value[half:])
+        value = kept + lax.ppermute(sent, "fsdp", [(i, i ^ bit) for i in range(8)])
+    return value[0]
+
+
+def sum_small(value):
+    for bit in (1, 2):
+        value = value + swap_seq(value, bit)
+    return value
+
+
+def after(value, other):
+    return lax.optimization_barrier((value, other))[0]
 
 
 def sum_seq(part, x, y):
@@ -404,26 +1406,24 @@
     both_axes = ("seq", "fsdp")
     units = up_weight.shape[0]
 
+    length = block_ids.shape[1]
+    own_small = [attn_gain, attn_shift, mlp_gain, mlp_shift, out_bias + down_bias, qkv_bias]
     packed = jnp.concatenate(
-        [attn_gain, attn_shift, mlp_gain, mlp_shift, out_bias + down_bias, qkv_bias]
-    )
-    small = lax.all_gather(packed, "fsdp", axis=0)
-    gain_a, shift_a, gain_m, shift_m, bias_out = (
-        small[:, i * 256 : (i + 1) * 256].reshape(width) for i in range(5)
-    )
-    head_bias = small[:, 5 * 256 :].reshape(3, HEADS, HEAD_DIM)
-    head_bias = lax.dynamic_index_in_dim(head_bias, f, 1, keepdims=False).reshape(3 * HEAD_DIM)
-    ids_starts = lax.all_gather(
-        jnp.concatenate([block_ids, offsets], axis=1), "fsdp", axis=0, tiled=True
-    )
-    ids_all = ids_starts[:, : block_ids.shape[1]]
-    starts_all = ids_starts[:, block_ids.shape[1] :]
-
+        own_small + [block_ids.reshape(-1).astype(f32), offsets.reshape(-1).astype(f32)]
+    )
     flat = resid_in.reshape(tokens, width)
     center = flat - jnp.mean(flat, axis=-1, keepdims=True)
     inv = lax.rsqrt(jnp.mean(center * center, axis=-1, keepdims=True) + EPS)
     normal = center * inv
     grad_flat = grad_out.reshape(tokens, width)
+    small = gather_small(packed, f)
+    gain_a, shift_a, gain_m, shift_m, bias_out = (
+        small[:, i * 256 : (i + 1) * 256].reshape(width) for i in range(5)
+    )
+    head_bias = small[:, 1280:2048].reshape(3, HEADS, HEAD_DIM)
+    head_bias = lax.dynamic_index_in_dim(head_bias, f, 1, keepdims=False).reshape(3 * HEAD_DIM)
+    ids_all = small[:, 2048 : 2048 + groups * length].astype(jnp.int32).reshape(-1, 8, LANES)
+    starts_all = small[:, 2048 + groups * length :].astype(jnp.int32).reshape(-1, offsets.shape[1])
 
     def plane_out(value):
         parts = value.reshape(4, tokens // 4, width)
@@ -443,7 +1443,7 @@
         return jnp.concatenate([pick(got, (j - s + 4) % 4) for j in range(4)], axis=0)
 
     own_n = plane_out(normal.astype(low))
-    own_g = plane_out(grad_flat.astype(low))
+    own_g = plane_out(after(grad_flat.astype(low), own_n))
 
     quarter = HEAD_DIM // 4
     qkv_low = lax.dynamic_slice_in_dim(
@@ -463,127 +1463,76 @@
         sum(jnp.where(third_of(i) == kind, i, 0) for i in range(3)) for kind in range(3)
     ]
     came = jnp.stack([pick(came, slot_of[kind]) for kind in range(3)])
-    head_w = lax.all_gather(came, "seq", axis=1, tiled=True).reshape(3 * HEAD_DIM, width)
-    up_low = up_weight.astype(low)
-    plain_w = jnp.concatenate([up_low, head_w], axis=0)
-    gains = jnp.concatenate(
-        [jnp.broadcast_to(gain_m, (units, width)), jnp.broadcast_to(gain_a, (768, width))], axis=0
-    )
-    shifts = jnp.concatenate(
-        [jnp.broadcast_to(shift_m, (units, width)), jnp.broadcast_to(shift_a, (768, width))],
-        axis=0,
-    )
-    w_in = (plain_w.astype(f32) * gains).astype(low)
-    bias_in = jnp.concatenate([up_bias, head_bias]) + jnp.sum(
-        plain_w.astype(f32) * shifts, axis=1
-    )
-    w_out = jnp.concatenate([down_weight, out_weight], axis=0).astype(low)
+    got = jnp.stack([came] + [swap_seq(came, bit) for bit in (1, 2, 3)])
+    head_w = jnp.stack([pick(got, s ^ q) for q in range(4)], axis=1).reshape(3 * HEAD_DIM, width)
+    gain = jnp.stack([gain_m, gain_a])
+    shift = jnp.stack([shift_m, shift_a])
+    up_low = up_weight.astype(low).astype(f32)
+    head32 = head_w.astype(f32)
+    plain_w = jnp.concatenate([up_low, head32], axis=0).astype(low)
+    w_up = (up_low * gain_m).astype(low)
+    w_head = (head32 * gain_a).astype(low)
+    w_in = jnp.concatenate([w_up, w_head], axis=0)
+    bias_in = jnp.concatenate(
+        [
+            up_bias + jnp.sum(up_low * shift_m, axis=1),
+            head_bias + jnp.sum(head32 * shift_a, axis=1),
+        ]
+    )[None]
+    w_out = jnp.concatenate([down_weight.astype(low), out_weight.astype(low)], axis=0)
 
     halves = [(2 * (s % 2) + c, c), (2 * (s % 2) + 1 - c, 1 - c)]
     rows_at = [((part - k + 4) % 4) * 2 + core for part, core in halves for k in range(4)]
-    blocks = [
-        z,
-        jnp.where(z % 2 == 0, 1, 2),
-        jnp.where(z == 0, 2, jnp.where(z == 1, 0, jnp.where(z == 2, 3, 1))),
-        jnp.where(z < 2, 3, 0),
-    ]
-    ids_rows = ids_all.reshape(16, 8, LANES)
-    ids_slots = [pick(ids_rows, block * 4 + s) for block in blocks]
+    ids_slots = [pick(ids_all, block * 4 + s) for block in range(4)]
     ids_here = jnp.stack(
         [jnp.concatenate([pick(row, at) for at in rows_at]) for row in ids_slots]
-    )
-    starts_here = jnp.stack([pick(starts_all, block * 4 + s) for block in blocks])
+    ).reshape(4, 1024)
+    starts_here = jnp.stack([pick(starts_all, block * 4 + s) for block in range(4)])
     pos = (jnp.stack(rows_at)[:, None] * LANES + jnp.arange(LANES)[None, :]).reshape(1024)
     positions = block_offset(ids_here, starts_here) + pos[None, :]
-    cosine, sine = rotary_tables(positions)
-
-    slots_n = gather_z(own_n, z)
-    own_g, _ = lax.optimization_barrier((own_g, slots_n[3]))
-    slots_g = gather_z(own_g, z)
-
-    full_n, kept_act, kept_slope, heads, outs = [], [], [], [], []
-    parts = []
-    for t in range(4):
-        n_t = jnp.concatenate([slots_n[t], swap_core(slots_n[t])], axis=0)
-        full_n.append(n_t)
-        projected = contract_last(n_t, w_in) + bias_in
-        hidden = projected[:, :units]
-        cdf = 0.5 * (1.0 + lax.erf(hidden * (0.5**0.5)))
-        act = (hidden * cdf).astype(low)
-        slope = (cdf + hidden * jnp.exp(-0.5 * hidden * hidden) * (1.0 / math.sqrt(2.0 * math.pi))).astype(low)
-        qkv = projected[:, units:].reshape(1024, 3, HEAD_DIM)
-        query = rotate(qkv[:, None, 0], cosine[t], sine[t])[:, 0].astype(low)
-        keys = rotate(qkv[:, None, 1], cosine[t], sine[t])[:, 0].astype(low)
-        values = qkv[:, 2].astype(low)
-        mixed, lse = attend_forward((query, keys, values, ids_here[t]))
-        heads.append((query, keys, values, lse))
-        a_t = jnp.concatenate([act, mixed], axis=1)
-        outs.append(a_t)
-        kept_slope.append(slope)
-        p_own = jnp.dot(a_t[:512], w_out, preferred_element_type=f32)
-        p_sib = jnp.dot(a_t[512:], w_out, preferred_element_type=f32).astype(low)
-        parts.append(p_own + swap_core(p_sib).astype(f32))
-    branch = plane_back(scatter_z(parts, z).astype(low))
-    result = flat + branch.astype(f32) + bias_out
-
-    full_g, backs, parts = [], [], []
-    for t in range(4):
-        g_t = jnp.concatenate([slots_g[t], swap_core(slots_g[t])], axis=0)
-        full_g.append(g_t)
-        grad_a = contract_last(g_t, w_out).astype(low)
-        gh = (grad_a[:, :units].astype(f32) * kept_slope[t].astype(f32)).astype(low)
-        query, keys, values, lse = heads[t]
-        gq, gk, gv = attend_backward((query, keys, values, ids_here[t], lse, grad_a[:, units:]))
-        gq = rotate(gq.astype(f32)[:, None], cosine[t], -sine[t])[:, 0].astype(low)
-        gk = rotate(gk.astype(f32)[:, None], cosine[t], -sine[t])[:, 0].astype(low)
-        b_t = jnp.concatenate([gh, gq, gk, gv], axis=1)
-        backs.append(b_t)
-        u_own = jnp.dot(b_t[:512], w_in, preferred_element_type=f32)
-        u_sib = jnp.dot(b_t[512:], w_in, preferred_element_type=f32).astype(low)
-        parts.append(u_own + swap_core(u_sib).astype(f32))
-    u = plane_back(scatter_z(parts, z).astype(low)).astype(f32)
+    lane = jnp.arange(LANES)
+    inverse = jnp.exp(
+        (lane % 32).astype(f32) * (-2.0 * math.log(10000.0) / ROT_DIM)
+    )
+    angles = jnp.where(lane < ROT_DIM, positions.astype(f32)[..., None] * inverse, 0.0)
+    cosine = jnp.cos(angles)
+    sine = jnp.sin(angles) * jnp.where(lane < ROT_DIM // 2, -1.0, 1.0)
+    ids_col, ids_row = ids_here[:, :, None], ids_here[:, None, :]
+
+    n_all, g_part, act_all, slope_all, qkv_all, mixed_all, lse_all, p_own, p_sib = forward_call(
+        own_n, own_g, w_in, w_out, bias_in, cosine, sine, ids_col, ids_row
+    )
+    g_all, gh_all, gp_all, u_own, u_sib, branch, _, col_sums = backward_call(
+        g_part, w_in, w_out, slope_all, qkv_all, lse_all, p_own, p_sib, cosine, sine, ids_col, ids_row
+    )
+    result = flat + plane_back(branch).astype(f32) + bias_out
+    term_out = g2_call(act_all, mixed_all, g_all)
+    down_out = lax.psum(term_out, "seq").astype(f32)
+    blk = [line_order(z, t) for t in range(4)]
+    parts = [pick(u_own, q).astype(f32) + pick(u_sib, q).astype(f32) for q in blk]
+    u_sum = scatter_z(parts, z).astype(low)
+    u = plane_back(u_sum).astype(f32)
     grad_input = grad_flat + inv * (
         u - jnp.mean(u, axis=-1, keepdims=True) - normal * jnp.mean(u * normal, axis=-1, keepdims=True)
     )
-
-    all_n, all_g = jnp.concatenate(full_n), jnp.concatenate(full_g)
-    all_a, all_b = jnp.concatenate(outs), jnp.concatenate(backs)
-    term_out = contract_lead(all_a, all_g)
-    raw_in = contract_lead(all_b, all_n)
-    sums = jnp.sum(all_b.astype(f32), axis=0)
-    term_in = raw_in * gains + sums[:, None] * shifts
-    gain_terms = raw_in * plain_w.astype(f32)
-    shift_terms = sums[:, None] * plain_w.astype(f32)
-
-    down_out = spread_seq(sum_seq(term_out, x, y), x, y)
-    up_out = spread_seq(sum_seq(term_in[:units], x, y), x, y)
-    qkv_quarter = sum_seq(term_in[units:].reshape(3, 2, 4, 32, width).transpose(1, 2, 0, 3, 4).reshape(768, width), x, y)
-    qkv_quarter = jnp.stack(qkv_quarter).reshape(2, 3, 32, width)
-    kinds = jnp.stack([pick(qkv_quarter.transpose(1, 0, 2, 3), third_of(i)) for i in range(3)])
+    term_in, sides, sums = g1_call(gh_all, gp_all, n_all, plain_w, gain, shift)
+    qkv_sum = lax.psum(term_in[units:], "seq").reshape(3, HEAD_DIM, width)
+    up_out = lax.psum(term_in[:units], "seq").astype(f32)
+    kinds = [pick(qkv_sum, third_of(i)) for i in range(3)]
     qkv_back = [
         lax.ppermute(kinds[i], "fsdp", [((3 * r + i) % 8, r) for r in range(8)]) for i in range(3)
     ]
-    qkv_back = jnp.stack(qkv_back).transpose(1, 0, 2, 3).reshape(2, 96, width)
-    qkv_out = spread_seq([qkv_back[0], qkv_back[1]], x, y)
-    qkv_out = qkv_out.reshape(2, 4, 3, 32, width).transpose(2, 0, 1, 3, 4).reshape(768, width)
+    qkv_out = jnp.concatenate(qkv_back).astype(f32)
 
     slots = jnp.zeros((16, HEAD_DIM), f32)
-    slots = lax.dynamic_update_slice(slots, sums[units : units + 256][None], (f, 0))
-    slots = lax.dynamic_update_slice(slots, sums[units + 256 : units + 512][None], (8 + f, 0))
-    spread = jnp.stack(
-        [
-            jnp.sum(gain_terms[units:], axis=0),
-            jnp.sum(shift_terms[units:], axis=0),
-            jnp.sum(gain_terms[:units], axis=0),
-            jnp.sum(shift_terms[:units], axis=0),
-            jnp.sum(grad_flat, axis=0),
-        ]
-    )
+    slots = lax.dynamic_update_slice(slots, col_sums[0:1], (f, 0))
+    slots = lax.dynamic_update_slice(slots, col_sums[1:2], (8 + f, 0))
+    spread = jnp.concatenate([sides[:4], jnp.sum(grad_flat, axis=0)[None]])
     wide = jnp.concatenate(
         [spread.reshape(5, 8, 256).transpose(1, 0, 2).reshape(8, 5 * 256), slots.reshape(8, 512)], axis=1
     )
-    mine = lax.psum_scatter(wide, "fsdp", scatter_dimension=0, tiled=True)[0]
-    mine = lax.psum(jnp.concatenate([mine, sums[:units], sums[units + 512 :]]), "seq")
+    wide = after(wide, u_sum)
+    mine = sum_small(jnp.concatenate([scatter_small(wide, f), sums[:units, 0], col_sums[2]]))
     vectors = [mine[i * 256 : (i + 1) * 256] for i in range(5)]
     qk_grad = mine[1280:1792]
     up_bias_grad = mine[1792 : 1792 + units]
@@ -600,10 +1549,10 @@
         up_bias_grad,
         down_out[:units],
         vectors[4],
+        vectors[2],
+        vectors[3],
         vectors[0],
         vectors[1],
-        vectors[2],
-        vectors[3],
     )
 
 

time: 1530 us -> 988 us (0.65)
  Pallas kernels: 0 us -> 434 us
  matrix products: 389 us -> 0 us
  other arithmetic: 240 us -> 107 us
  waiting for transfers between devices: 404 us -> 275 us
  blocking collectives: 119 us -> 0 us
  local copies, waits for them, and re-layouts: 158 us -> 40.4 us
  starting transfers between devices: 186 us -> 104 us
    pallas_call x0 -> x4, Pallas kernels: none -> 434 us  [the longest x1 190 us: forward_call(): pl.pallas_call(forward_body, in_specs=[anys] * 4 + [vmem] * 5, out_specs=...]
    dot_general x50 -> x0, matrix products: 389 us -> none  [the longest x16 128 us: contract_last(): lax.dot_general(left, right, (((1,), (1,)), ((), ())), preferred_element_...]
    ppermute x20 -> x5, waiting for transfers between devices: 220 us -> 92.8 us  [along_z(): lax.ppermute(value, 'fsdp', [(2 * a + c, 2 * b + c) for a, b in pairs for...]
    ppermute x24 -> x5, waiting for transfers between devices: 173 us -> 49.4 us  [swap_seq(): return lax.ppermute(value, 'seq', [(i, i ^ bit) for i in range(4)])]
    all_gather x2 -> x0, blocking collectives: 76.2 us -> none  [the longest x1 60.7 us: split_body(): small = lax.all_gather(packed, 'fsdp', axis=0)]
    ppermute x8, waiting for transfers between devices: 0.02 us -> 47.7 us  [plane_back(): lax.ppermute(parts[k], both_axes, [(b, a) for a, b in spread_pairs(k)])]
    reduce_sum x11 -> x3, other arithmetic: 54.7 us -> 9.53 us  [the longest x1 4.58 us: split_body(): spread = jnp.concatenate([sides[:4], jnp.sum(grad_flat, axis=0)[None]])]
    unnamed x426 -> x73, local copies, waits for them, and re-layouts: 52.8 us -> 8.55 us
  transfers between devices with their start and end apart: 83 -> 39, of which waited for: 23 -> 20; matrix products, arithmetic and copies ran while one was open for 48% -> 12% of each run, Pallas kernels for 0% -> 3%
where the time goes in v2:
time: 988 us; the launch traced here: 976 us
  Pallas kernels  434 us (44%)
  waiting for transfers between devices  275 us (28%)
  other arithmetic  107 us (11%)
  starting transfers between devices  104 us (11%)
  local copies, waits for them, and re-layouts  40.4 us (4%)
  between operations  16.1 us (2%)
    pallas_call x1, Pallas kernels, forward_call(): pl.pallas_call(forward_body, in_specs=[anys] * 4 + [vmem] * 5, out_specs=...  190 us
    pallas_call x1, Pallas kernels, backward_call(): pl.pallas_call(backward_body, in_specs=[anys] * 8 + [vmem] * 4, out_specs...  162 us
    ppermute x5, waiting for transfers between devices, along_z(): lax.ppermute(value, 'fsdp', [(2 * a + c, 2 * b + c) for a, b in pairs for...  92.8 us
    pallas_call x1, Pallas kernels, g1_call(): pl.pallas_call(g1_body, in_specs=[anys] * 4 + [vmem] * 2, out_specs=[anys...  51.1 us
    ppermute x5, waiting for transfers between devices, swap_seq(): return lax.ppermute(value, 'seq', [(i, i ^ bit) for i in range(4)])  49.4 us
    ppermute x8, waiting for transfers between devices, plane_back(): lax.ppermute(parts[k], both_axes, [(b, a) for a, b in spread_pairs(k)])  47.7 us
    psum x1, waiting for transfers between devices, split_body(): qkv_sum = lax.psum(term_in[units:], 'seq').reshape(3, HEAD_DIM, width)  40.7 us
    ppermute x5, starting transfers between devices, along_z(): lax.ppermute(value, 'fsdp', [(2 * a + c, 2 * b + c) for a, b in pairs for...  33.8 us
  transfers between devices with their start and end apart: 39, of which 20 were waited for; matrix products, arithmetic and copies ran while one was open for 12% of the time, Pallas kernels for 3%

profile of v2, /device:TPU:0, one launch (start us, length us, event | category | flops | bytes accessed | tf_op | source)
XLA Modules:
  0.0 976.4 jit_solution(17040645673735068043)
XLA Ops:
  52.7 6.6 collective-permute-done.10
  70.1 8.9 sine_multiply_fusion
  92.7 7.1 collective-permute-done.2
  123.4 18.1 %collective-permute-done.15 = bf16[3,64,2048]{2,1,0:T(8,128)(2,1)S(1)} collective-permute-done((bf16[3,64,2048]{2,1,0:T(8,128)(2,1)S(1)}, bf16[3,64,2048]{2,1,0:T(8,128)(2,1)S(1)}, u32[]{:S(2)}, u32[]{:S(2)}) %collective-permute-start.15) | collective-permute-done | bytes 786464 | tf_op jit(solution)/shard_map/ppermute | solution.py:1321
  149.0 6.4 pad_maximum_fusion.1.plain
  155.5 7.6 pad_maximum_fusion.w_in_h
  166.2 190.0 %forward.1 = (bf16[4,1024,2048]{2,1,0:T(8,128)(2,1)}, bf16[4,1024,2048]{2,1,0:T(8,128)(2,1)}, bf16[4,1024,1024]{2,1,0:T(8,128)(2,1)}, bf16[4,1024,1024]{2,1,0:T(...) custom-call(bf16[512,2048]{1,0:T(8,128)(2,1)} %copy-done.11, ...), custom_call_target="tpu_custom_call" | custom-call | flops 51539607552 | bytes 200000000 | tf_op jit(solution)/shard_map/forward/pallas_call | solution.py:986
  356.2 162.0 %backward.1 = (bf16[4,1024,2048]{2,1,0:T(8,128)(2,1)}, bf16[4,1024,1024]{2,1,0:T(8,128)(2,1)}, bf16[4,3,1024,256]{3,2,1,0:T(8,128)(2,1)}, bf16[4,512,2048]{2,1,0...) custom-call(bf16[4,1024,2048]{2,1,0:T(8,128)(2,1)} %get-tuple-elemen, ...), custom_call_target="tpu_custom_call", output_to_operand_aliasing={{0}: (0, {})} | custom-call | flops 51539607552 | bytes 200000000 | tf_op jit(solution)/shard_map/backward/pallas_call | solution.py:1242
  518.2 51.1 %grad_in_weights.1 = (bf16[1792,2048]{1,0:T(8,128)(2,1)}, f32[8,2048]{1,0:T(8,128)}, f32[1792,128]{1,0:T(8,128)}) custom-call(bf16[4,1024,1024]{2,1,0:T(8,128)(2,1)} %get-tuple-element.46.ghs, bf16[4,3,1024,256]{3,2,1,0:T(8,128)(2,1)} %get-tuple-element.47.gps, bf16[4,1024,2048]{2,1,0:T(8,128)(2,1)} %get-tuple-element.48.rights, ...), custom_call_target="tpu_custom_call" | custom-call | flops 30064771072 | bytes 50000000 | tf_op jit(solution)/shard_map/grad_in_weights/pallas_call | solution.py:727
  584.2 8.0 collective-permute-start.22
  592.1 31.3 %grad_out_weights.1 = bf16[1280,2048]{1,0:T(8,128)(2,1)} custom-call(bf16[4,1024,1024]{2,1,0:T(8,128)(2,1)} %get-tuple-element.54.acts, bf16[4,1024,256]{2,1,0:T(8,128)(2,1)} %get-tuple-element.55.mixes, bf16[4,1024,2048]{2,1,0:T(8,128)(2,1)} %get-tuple-element.56.rights), custom_call_target="tpu_custom_call" | custom-call | flops 21474836480 | bytes 40000000 | tf_op jit(solution)/shard_map/grad_out_weights/pallas_call | solution.py:633
  626.2 10.3 %collective-permute-done.22 = bf16[512,2048]{1,0:T(8,128)(2,1)} collective-permute-done((bf16[512,2048]{1,0:T(8,128)(2,1)}, bf16[512,2048]{1,0:T(8,128)(2,1)}, u32[]{:S(2)}, u32[]{:S(2)}) %collective-permute-start.22) | collective-permute-done | bytes 2097184 | tf_op jit(solution)/shard_map/ppermute | solution.py:1279
  644.0 37.3 %collective-permute-done.21 = bf16[512,2048]{1,0:T(8,128)(2,1)} collective-permute-done((bf16[512,2048]{1,0:T(8,128)(2,1)S(1)}, bf16[512,2048]{1,0:T(8,128)(2,1)}, u32[]{:S(2)}, u32[]{:S(2)}) %collective-permute-start.21) | collective-permute-done | bytes 2097184 | tf_op jit(solution)/shard_map/ppermute | solution.py:1279
  681.3 9.5 select_convert_fusion.1
  690.8 19.9 %collective-permute-start.24 = (bf16[512,2048]{1,0:T(8,128)(2,1)}, bf16[512,2048]{1,0:T(8,128)(2,1)}, u32[]{:S(2)}, u32[]{:S(2)}) collective-permute-start(bf16[512,2048]{1,0:T(8,128)(2,1)} %get-tuple-element.64), channel_id=1, source_target_pairs={{0,2},{1,3},{2,4},{3,5},{4,6},{5,7},{8,10},{9,11},{10,12},{11,13},... | collective-permute-start | bytes 6291464 | tf_op jit(solution)/shard_map/ppermute | solution.py:1279
  714.8 40.0 %collective-permute-done.24 = bf16[512,2048]{1,0:T(8,128)(2,1)} collective-permute-done((bf16[512,2048]{1,0:T(8,128)(2,1)}, bf16[512,2048]{1,0:T(8,128)(2,1)}, u32[]{:S(2)}, u32[]{:S(2)}) %collective-permute-start.24) | collective-permute-done | bytes 2097184 | tf_op jit(solution)/shard_map/ppermute | solution.py:1279
  766.8 6.7 collective-permute-start.18
  777.6 19.4 %collective-permute-done.18 = bf16[128,2048]{1,0:T(8,128)(2,1)S(1)} collective-permute-done((bf16[128,2048]{1,0:T(8,128)(2,1)S(1)}, bf16[128,2048]{1,0:T(8,128)(2,1)S(1)}, u32[]{:S(2)}, u32[]{:S(2)}) %collective-permute-start.18) | collective-permute-done | bytes 524320 | tf_op jit(solution)/shard_map/ppermute | solution.py:1439
  797.0 16.6 %collective-permute-done.19 = bf16[128,2048]{1,0:T(8,128)(2,1)S(1)} collective-permute-done((bf16[128,2048]{1,0:T(8,128)(2,1)S(1)}, bf16[128,2048]{1,0:T(8,128)(2,1)S(1)}, u32[]{:S(2)}, u32[]{:S(2)}) %collective-permute-start.19) | collective-permute-done | bytes 524320 | tf_op jit(solution)/shard_map/ppermute | solution.py:1439
  828.0 28.0 %collective-permute-done.37 = f32[3072]{0:T(1024)S(1)} collective-permute-done((f32[3072]{0:T(1024)S(1)}, f32[3072]{0:T(1024)S(1)}, u32[]{:S(2)}, u32[]{:S(2)}) %collective-permute-start.37) | collective-permute-done | bytes 12320 | tf_op jit(solution)/shard_map/ppermute | solution.py:1321
  862.4 5.9 collective-permute-done.29
  873.2 40.7 %all-reduce.3.cloned.1.call-done = (bf16[3,256,2048]{2,1,0:T(8,128)(2,1)}, bf16[1280,2048]{1,0:T(8,128)(2,1)}, bf16[1024,2048]{1,0:T(8,128)(2,1)}) async-done(((bf16[3,256,2048]{2,1,0:T(8,128)(2,1)}, bf16[1280,2048]{1,0:T(8,128)(2,1)}, bf16[1024,2048]{1,0:T(8,128)(2,1)}), (bf16[3,256,2048]{2,1,0:T(8,128)(2,1)}, bf16[1280,2048]{1,0:T(8,128)(2,1)}, bf16[1024,2048]{1,0:T(8,128)(2,1)})) %all-reduce.3.cloned.1.call-update) | async-done | bytes 12582928 | tf_op jit(solution)/shard_map/psum | solution.py:1519
  924.6 6.5 multiply_add_fusion
  945.4 19.5 %collective-permute-done.32 = bf16[256,2048]{1,0:T(8,128)(2,1)S(1)} collective-permute-done((bf16[256,2048]{1,0:T(8,128)(2,1)S(1)}, bf16[256,2048]{1,0:T(8,128)(2,1)S(1)}, u32[]{:S(2)}, u32[]{:S(2)}) %collective-permute-start.32) | collective-permute-done | bytes 1048608 | tf_op jit(solution)/shard_map/ppermute | solution.py:1523
  (253 shorter events, 202.9 us)
Async XLA Ops:
  7.2 906.7 %all-reduce.3.cloned.1.call-start = ((), (), s32[]{:S(2)}) async-start(), calls=%async_computation | async-start | bytes 25165824 | tf_op jit(solution)/shard_map/psum | solution.py:1519
  12.9 35.4 %collective-permute-start.8 = (f32[1,4112]{1,0:T(1,128)S(1)}, f32[1,4112]{1,0:T(1,128)S(1)}, u32[]{:S(2)}, u32[]{:S(2)}) collective-permute-start(f32[1,4112]{1,0:T(1,128)S(1)} %broadcast_in_dim.44), channel_id=1, source_target_pairs={{0,1},{1,0},{2,3},{3,2},{4,5},{5,4},{6,7},{7,6},{8,9},{9,8},{10,11... | collective-permute-start | bytes 49352 | tf_op jit(solution)/shard_map/ppermute | solution.py:1327
  15.8 66.6 %collective-permute-start.11 = (bf16[64,2048]{1,0:T(8,128)(2,1)}, bf16[64,2048]{1,0:T(8,128)(2,1)}, u32[]{:S(2)}, u32[]{:S(2)}) collective-permute-start(bf16[64,2048]{1,0:T(8,128)(2,1)} %get-tuple-element.108), channel_id=1, source_target_pairs={{0,0},{1,3},{2,6},{3,1},{4,4},{5,7},{6,2},{7,5},{8,8},{9,11},{10,1... | collective-permute-start | bytes 786440 | tf_op jit(solution)/shard_map/ppermute | solution.py:1454
  19.4 63.1 %collective-permute-start.12 = (bf16[64,2048]{1,0:T(8,128)(2,1)}, bf16[64,2048]{1,0:T(8,128)(2,1)}, u32[]{:S(2)}, u32[]{:S(2)}) collective-permute-start(bf16[64,2048]{1,0:T(8,128)(2,1)} %get-tuple-element.110), channel_id=1, source_target_pairs={{0,1},{1,4},{2,7},{3,2},{4,5},{5,0},{6,3},{7,6},{8,9},{9,12},{10,1... | collective-permute-start | bytes 786440 | tf_op jit(solution)/shard_map/ppermute | solution.py:1454
  20.6 67.0 %collective-permute-start.13 = (bf16[64,2048]{1,0:T(8,128)(2,1)}, bf16[64,2048]{1,0:T(8,128)(2,1)}, u32[]{:S(2)}, u32[]{:S(2)}) collective-permute-start(bf16[64,2048]{1,0:T(8,128)(2,1)} %get-tuple-element.109), channel_id=1, source_target_pairs={{0,2},{1,5},{2,0},{3,3},{4,6},{5,1},{6,4},{7,7},{8,10},{9,13},{10,... | collective-permute-start | bytes 786440 | tf_op jit(solution)/shard_map/ppermute | solution.py:1454
  34.5 54.5 %collective-permute-start = (bf16[128,2048]{1,0:T(8,128)(2,1)}, bf16[128,2048]{1,0:T(8,128)(2,1)S(1)}, u32[]{:S(2)}, u32[]{:S(2)}) collective-permute-start(bf16[128,2048]{1,0:T(8,128)(2,1)} %get-tuple-element.102), channel_id=1, source_target_pairs={{0,0},{1,16},{2,2},{3,18},{4,4},{5,20},{6,6},{7,22},{8,1},{9,17},{... | collective-permute-start | bytes 1572872 | tf_op jit(solution)/shard_map/ppermute | solution.py:1431
  89.0 52.5 %collective-permute-start.15 = (bf16[3,64,2048]{2,1,0:T(8,128)(2,1)S(1)}, bf16[3,64,2048]{2,1,0:T(8,128)(2,1)S(1)}, u32[]{:S(2)}, u32[]{:S(2)}) collective-permute-start(bf16[3,64,2048]{2,1,0:T(8,128)(2,1)S(1)} %get-tuple-element.104), channel_id=1, source_target_pairs={{0,16},{8,24},{16,0},{24,8},{1,17},{9,25},{17,1},{25,9},{2,18},{10... | collective-permute-start | bytes 2359304 | tf_op jit(solution)/shard_map/ppermute | solution.py:1321
  90.5 53.4 %collective-permute-start.16 = (bf16[3,64,2048]{2,1,0:T(8,128)(2,1)S(1)}, bf16[3,64,2048]{2,1,0:T(8,128)(2,1)S(1)}, u32[]{:S(2)}, u32[]{:S(2)}) collective-permute-start(bf16[3,64,2048]{2,1,0:T(8,128)(2,1)S(1)} %get-tuple-element.104), channel_id=1, source_target_pairs={{0,24},{8,16},{16,8},{24,0},{1,25},{9,17},{17,9},{25,1},{2,26},{10... | collective-permute-start | bytes 2359304 | tf_op jit(solution)/shard_map/ppermute | solution.py:1321
  106.9 56.2 %collective-permute-start.4 = (bf16[128,2048]{1,0:T(8,128)(2,1)}, bf16[128,2048]{1,0:T(8,128)(2,1)}, u32[]{:S(2)}, u32[]{:S(2)}) collective-permute-start(bf16[128,2048]{1,0:T(8,128)(2,1)} %get-tuple-element.95), channel_id=1, source_target_pairs={{0,0},{1,16},{2,2},{3,18},{4,4},{5,20},{6,6},{7,22},{8,1},{9,17},{... | collective-permute-start | bytes 1572872 | tf_op jit(solution)/shard_map/ppermute | solution.py:1431
  112.2 50.8 %collective-permute-start.5 = (bf16[128,2048]{1,0:T(8,128)(2,1)}, bf16[128,2048]{1,0:T(8,128)(2,1)}, u32[]{:S(2)}, u32[]{:S(2)}) collective-permute-start(bf16[128,2048]{1,0:T(8,128)(2,1)} %get-tuple-element.98), channel_id=1, source_target_pairs={{0,1},{1,17},{2,3},{3,19},{4,5},{5,21},{6,7},{7,23},{8,8},{9,24},{... | collective-permute-start | bytes 1572872 | tf_op jit(solution)/shard_map/ppermute | solution.py:1431
  120.9 42.2 %collective-permute-start.6 = (bf16[128,2048]{1,0:T(8,128)(2,1)}, bf16[128,2048]{1,0:T(8,128)(2,1)}, u32[]{:S(2)}, u32[]{:S(2)}) collective-permute-start(bf16[128,2048]{1,0:T(8,128)(2,1)} %get-tuple-element.97), channel_id=1, source_target_pairs={{0,8},{1,24},{2,10},{3,26},{4,12},{5,28},{6,14},{7,30},{8,9},{9,25... | collective-permute-start | bytes 1572872 | tf_op jit(solution)/shard_map/ppermute | solution.py:1431
  584.2 52.3 %collective-permute-start.22 = (bf16[512,2048]{1,0:T(8,128)(2,1)}, bf16[512,2048]{1,0:T(8,128)(2,1)}, u32[]{:S(2)}, u32[]{:S(2)}) collective-permute-start(bf16[512,2048]{1,0:T(8,128)(2,1)} %get-tuple-element.66), channel_id=1, source_target_pairs={{0,2},{1,3},{6,4},{7,5},{8,10},{9,11},{14,12},{15,13},{16,18},{17,... | collective-permute-start | bytes 6291464 | tf_op jit(solution)/shard_map/ppermute | solution.py:1279
  623.4 57.9 %collective-permute-start.21 = (bf16[512,2048]{1,0:T(8,128)(2,1)S(1)}, bf16[512,2048]{1,0:T(8,128)(2,1)}, u32[]{:S(2)}, u32[]{:S(2)}) collective-permute-start(bf16[512,2048]{1,0:T(8,128)(2,1)S(1)} %get-tuple-element.67), channel_id=1, source_target_pairs={{0,2},{1,3},{6,4},{7,5},{8,10},{9,11},{14,12},{15,13},{16,18},{17,... | collective-permute-start | bytes 6291464 | tf_op jit(solution)/shard_map/ppermute | solution.py:1279
  642.1 39.2 %collective-permute-start.23 = (bf16[512,2048]{1,0:T(8,128)(2,1)}, bf16[512,2048]{1,0:T(8,128)(2,1)}, u32[]{:S(2)}, u32[]{:S(2)}) collective-permute-start(bf16[512,2048]{1,0:T(8,128)(2,1)} %fusion.3), channel_id=1, source_target_pairs={{2,4},{3,5},{4,2},{5,3},{10,12},{11,13},{12,10},{13,11},{18,20},{1... | collective-permute-start | bytes 6291464 | tf_op jit(solution)/shard_map/ppermute | solution.py:1279
  690.8 64.0 %collective-permute-start.24 = (bf16[512,2048]{1,0:T(8,128)(2,1)}, bf16[512,2048]{1,0:T(8,128)(2,1)}, u32[]{:S(2)}, u32[]{:S(2)}) collective-permute-start(bf16[512,2048]{1,0:T(8,128)(2,1)} %get-tuple-element.64), channel_id=1, source_target_pairs={{0,2},{1,3},{2,4},{3,5},{4,6},{5,7},{8,10},{9,11},{10,12},{11,13},... | collective-permute-start | bytes 6291464 | tf_op jit(solution)/shard_map/ppermute | solution.py:1279
  710.7 49.4 %collective-permute-start.25 = (bf16[512,2048]{1,0:T(8,128)(2,1)S(1)}, bf16[512,2048]{1,0:T(8,128)(2,1)}, u32[]{:S(2)}, u32[]{:S(2)}) collective-permute-start(bf16[512,2048]{1,0:T(8,128)(2,1)S(1)} %get-tuple-element.65), channel_id=1, source_target_pairs={{2,0},{3,1},{4,2},{5,3},{6,4},{7,5},{10,8},{11,9},{12,10},{13,11},... | collective-permute-start | bytes 6291464 | tf_op jit(solution)/shard_map/ppermute | solution.py:1279
  773.5 40.1 %collective-permute-start.19 = (bf16[128,2048]{1,0:T(8,128)(2,1)S(1)}, bf16[128,2048]{1,0:T(8,128)(2,1)S(1)}, u32[]{:S(2)}, u32[]{:S(2)}) collective-permute-start(bf16[128,2048]{1,0:T(8,128)(2,1)S(1)} %get-tuple-element.93), channel_id=1, source_target_pairs={{8,0},{24,1},{10,2},{26,3},{12,4},{28,5},{14,6},{30,7},{9,8},{25,9... | collective-permute-start | bytes 1572872 | tf_op jit(solution)/shard_map/ppermute | solution.py:1439
  773.6 41.3 %collective-permute-start.20 = (bf16[128,2048]{1,0:T(8,128)(2,1)S(1)}, bf16[128,2048]{1,0:T(8,128)(2,1)S(1)}, u32[]{:S(2)}, u32[]{:S(2)}) collective-permute-start(bf16[128,2048]{1,0:T(8,128)(2,1)S(1)} %get-tuple-element.92), channel_id=1, source_target_pairs={{9,0},{25,1},{11,2},{27,3},{13,4},{29,5},{15,6},{31,7},{0,8},{16,9... | collective-permute-start | bytes 1572872 | tf_op jit(solution)/shard_map/ppermute | solution.py:1439
  777.5 37.6 %collective-permute-start.34 = (f32[2,1792]{1,0:T(2,128)S(1)}, f32[2,1792]{1,0:T(2,128)S(1)}, u32[]{:S(2)}, u32[]{:S(2)}) collective-permute-start(f32[2,1792]{1,0:T(2,128)S(1)} %broadcast_select_fusion.6), channel_id=1, source_target_pairs={{0,2},{1,3},{2,0},{3,1},{4,6},{5,7},{6,4},{7,5},{8,10},{9,11},{10,... | collective-permute-start | bytes 43016 | tf_op jit(solution)/shard_map/ppermute | solution.py:1341
  817.6 40.2 %collective-permute-start.26 = (bf16[128,2048]{1,0:T(8,128)(2,1)S(1)}, bf16[128,2048]{1,0:T(8,128)(2,1)S(1)}, u32[]{:S(2)}, u32[]{:S(2)}) collective-permute-start(bf16[128,2048]{1,0:T(8,128)(2,1)S(1)} %get-tuple-element.83), channel_id=1, source_target_pairs={{0,0},{16,1},{2,2},{18,3},{4,4},{20,5},{6,6},{22,7},{1,8},{17,9},{... | collective-permute-start | bytes 1572872 | tf_op jit(solution)/shard_map/ppermute | solution.py:1439
  818.3 39.5 %collective-permute-start.27 = (bf16[128,2048]{1,0:T(8,128)(2,1)S(1)}, bf16[128,2048]{1,0:T(8,128)(2,1)S(1)}, u32[]{:S(2)}, u32[]{:S(2)}) collective-permute-start(bf16[128,2048]{1,0:T(8,128)(2,1)S(1)} %get-tuple-element.86), channel_id=1, source_target_pairs={{1,0},{17,1},{3,2},{19,3},{5,4},{21,5},{7,6},{23,7},{8,8},{24,9},{... | collective-permute-start | bytes 1572872 | tf_op jit(solution)/shard_map/ppermute | solution.py:1439
  822.5 39.9 %collective-permute-start.28 = (bf16[128,2048]{1,0:T(8,128)(2,1)S(1)}, bf16[128,2048]{1,0:T(8,128)(2,1)S(1)}, u32[]{:S(2)}, u32[]{:S(2)}) collective-permute-start(bf16[128,2048]{1,0:T(8,128)(2,1)S(1)} %get-tuple-element.85), channel_id=1, source_target_pairs={{8,0},{24,1},{10,2},{26,3},{12,4},{28,5},{14,6},{30,7},{9,8},{25,9... | collective-permute-start | bytes 1572872 | tf_op jit(solution)/shard_map/ppermute | solution.py:1439
  823.2 45.0 %collective-permute-start.29 = (bf16[128,2048]{1,0:T(8,128)(2,1)S(1)}, bf16[128,2048]{1,0:T(8,128)(2,1)S(1)}, u32[]{:S(2)}, u32[]{:S(2)}) collective-permute-start(bf16[128,2048]{1,0:T(8,128)(2,1)S(1)} %get-tuple-element.84), channel_id=1, source_target_pairs={{9,0},{25,1},{11,2},{27,3},{13,4},{29,5},{15,6},{31,7},{0,8},{16,9... | collective-permute-start | bytes 1572872 | tf_op jit(solution)/shard_map/ppermute | solution.py:1439
  921.8 43.2 %collective-permute-start.32 = (bf16[256,2048]{1,0:T(8,128)(2,1)S(1)}, bf16[256,2048]{1,0:T(8,128)(2,1)S(1)}, u32[]{:S(2)}, u32[]{:S(2)}) collective-permute-start(bf16[256,2048]{1,0:T(8,128)(2,1)S(1)} %get-tuple-element.73), channel_id=1, source_target_pairs={{2,0},{5,1},{0,2},{3,3},{6,4},{1,5},{4,6},{7,7},{10,8},{13,9},{8,1... | collective-permute-start | bytes 3145736 | tf_op jit(solution)/shard_map/ppermute | solution.py:1523
  (38 other events, 758.4 us)
Sparse Core Ops, SparseCore 0:
  623.5 290.3 all-reduce.2

commit v3 on v2

--- a/solution.py
+++ b/solution.py
@@ -589,166 +589,6 @@
     )(gh, gq, gkv, w_up, w_qkv)
 
 
-def g2_body(acts, mixes, rights, term, acc, left, right, out, sems):
-    units = acts.shape[2]
-    rows = units + 256
-
-    def copies(k):
-        slot = k % 2
-        pairs = [
-            (acts.at[k], left.at[slot, :, pl.ds(0, units)]),
-            (mixes.at[k], left.at[slot, :, pl.ds(units, 256)]),
-            (rights.at[k], right.at[slot]),
-        ]
-        return [pltpu.make_async_copy(a, b, sems.at[slot, i]) for i, (a, b) in enumerate(pairs)]
-
-    for cp in copies(0):
-        cp.start()
-    for k in range(4):
-        if k < 3:
-            for cp in copies(k + 1):
-                cp.start()
-        for cp in copies(k):
-            cp.wait()
-        slot = k % 2
-
-        @pl.loop(0, rows // 256)
-        def _(m):
-            cols = pl.ds(pl.multiple_of(m * 256, 256), 256)
-            part = tn(left[slot, :, cols], right[slot])
-            if k == 0:
-                acc[cols, :] = part
-            elif k < 3:
-                acc[cols, :] += part
-            else:
-                out[cols, :] = (acc[cols, :] + part).astype(bf)
-    done = pltpu.make_async_copy(out, term, sems.at[0, 0])
-    done.start()
-    done.wait()
-
-
-def g2_call(acts, mixes, rights):
-    units, width = acts.shape[2], rights.shape[2]
-    rows = units + 256
-    return pl.pallas_call(
-        g2_body,
-        in_specs=[pl.BlockSpec(memory_space=pl.ANY)] * 3,
-        out_specs=pl.BlockSpec(memory_space=pl.ANY),
-        out_shape=jax.ShapeDtypeStruct((rows, width), bf),
-        scratch_shapes=[
-            pltpu.VMEM((rows, width), f32),
-            pltpu.VMEM((2, TOK, rows), bf),
-            pltpu.VMEM((2, TOK, width), bf),
-            pltpu.VMEM((rows, width), bf),
-            pltpu.SemaphoreType.DMA((2, 4)),
-        ],
-        compiler_params=pltpu.CompilerParams(vmem_limit_bytes=VM),
-        cost_estimate=cost(2 * 4096 * width * rows, 40e6),
-        name="grad_out_weights",
-    )(acts, mixes, rights)
-
-
-def g1_body(
-    ghs, gps, rights, plain, gain, shift, term, sides, sums, acc, acc_s, left, right, out, w, sems, sem_w
-):
-    units = ghs.shape[2]
-    rows = units + 768
-    tiles = rows // 256
-
-    def copies(k):
-        slot = k % 2
-        pairs = [(ghs.at[k], left.at[slot, :, pl.ds(0, units)])]
-        pairs += [(gps.at[k, i], left.at[slot, :, pl.ds(units + 256 * i, 256)]) for i in range(3)]
-        pairs += [(rights.at[k], right.at[slot])]
-        return [pltpu.make_async_copy(a, b, sems.at[slot, i]) for i, (a, b) in enumerate(pairs)]
-
-    weights = pltpu.make_async_copy(plain, w, sem_w)
-    weights.start()
-    for cp in copies(0):
-        cp.start()
-    ones = jnp.ones((TOK, 128), bf)
-    sides[...] = jnp.zeros_like(sides)
-    for k in range(4):
-        if k < 3:
-            for cp in copies(k + 1):
-                cp.start()
-        for cp in copies(k):
-            cp.wait()
-        slot = k % 2
-        if k == 3:
-            weights.wait()
-
-        @pl.loop(0, tiles)
-        def _(m):
-            cols = pl.ds(pl.multiple_of(m * 256, 256), 256)
-            piece = left[slot, :, cols]
-            part = tn(piece, right[slot])
-            part_s = tn(piece, ones)
-            if k == 0:
-                acc[cols, :] = part
-                acc_s[cols, :] = part_s
-            elif k < 3:
-                acc[cols, :] += part
-                acc_s[cols, :] += part_s
-            else:
-                raw = acc[cols, :] + part
-                total = acc_s[cols, :] + part_s
-                acc_s[cols, :] = total
-                total = total[:, 0:1]
-                which = (m >= units // 256).astype(jnp.int32)
-                g = jnp.where(which == 0, gain[0:1, :], gain[1:2, :])
-                s = jnp.where(which == 0, shift[0:1, :], shift[1:2, :])
-                out[cols, :] = (raw * g + total * s).astype(bf)
-                wt = w[cols, :].astype(f32)
-                one = jnp.sum(wt * raw, axis=0, keepdims=True)
-                two = jnp.sum(wt * total, axis=0, keepdims=True)
-
-                @pl.when(which == 0)
-                def _():
-                    sides[0:1, :] += one
-                    sides[1:2, :] += two
-
-                @pl.when(which == 1)
-                def _():
-                    sides[2:3, :] += one
-                    sides[3:4, :] += two
-
-    done = pltpu.make_async_copy(out, term, sem_w)
-    done.start()
-    sums[...] = acc_s[...]
-    done.wait()
-
-
-def g1_call(ghs, gps, rights, plain, gain, shift):
-    units, width = ghs.shape[2], rights.shape[2]
-    rows = units + 768
-    anys = pl.BlockSpec(memory_space=pl.ANY)
-    vmem = pl.BlockSpec(memory_space=pltpu.VMEM)
-    return pl.pallas_call(
-        g1_body,
-        in_specs=[anys] * 4 + [vmem] * 2,
-        out_specs=[anys, vmem, vmem],
-        out_shape=[
-            jax.ShapeDtypeStruct((rows, width), bf),
-            jax.ShapeDtypeStruct((8, width), f32),
-            jax.ShapeDtypeStruct((rows, 128), f32),
-        ],
-        scratch_shapes=[
-            pltpu.VMEM((rows, width), f32),
-            pltpu.VMEM((rows, 128), f32),
-            pltpu.VMEM((2, TOK, rows), bf),
-            pltpu.VMEM((2, TOK, width), bf),
-            pltpu.VMEM((rows, width), bf),
-            pltpu.VMEM((rows, width), bf),
-            pltpu.SemaphoreType.DMA((2, 6)),
-            pltpu.SemaphoreType.DMA,
-        ],
-        compiler_params=pltpu.CompilerParams(vmem_limit_bytes=VM),
-        cost_estimate=cost(2 * 4096 * width * rows, 50e6),
-        name="grad_in_weights",
-    )(ghs, gps, rights, plain, gain, shift)
-
-
 LANES = 128
 
 
@@ -790,6 +630,56 @@
         pl.semaphore_wait(barrier, 3)
 
 
+def near_barrier(s, f):
+    barrier = pltpu.get_barrier_semaphore()
+    c = f % 2
+    for step in range(1, 8):
+        pl.semaphore_signal(barrier, inc=1, device_id=(s, (f + step) % 8), device_id_type=MESH)
+    for step in range(1, 4):
+        for core in range(2):
+            pl.semaphore_signal(
+                barrier, inc=1, device_id=((s + step) % 4, f - c + core), device_id_type=MESH
+            )
+    pl.semaphore_wait(barrier, 13)
+
+
+class PlaneBack:
+    def __init__(self, src, dst, s, f, send, recv, own_sem):
+        c = f % 2
+        mine = 2 * (s % 2) + c
+        self.parts = []
+        for k in range(4):
+            to_s, to_f = (mine - k + 4) % 4, f - c + s // 2
+            piece = src.at[pl.ds(128 * k, 128)]
+            place = dst.at[pl.ds(pl.multiple_of(128 * mine, 128), 128)]
+            here = (to_s == s) & (to_f == f)
+            self.parts.append(
+                (
+                    here,
+                    pltpu.make_async_copy(piece, place, own_sem),
+                    remote(piece, place, send.at[k], recv.at[mine], to_s, to_f),
+                )
+            )
+        self.comes = []
+        for part in range(4):
+            from_s, from_f = 2 * c + part // 2, f - c + part % 2
+            ref = dst.at[pl.ds(128 * part, 128)]
+            away = jnp.logical_not((from_s == s) & (from_f == f))
+            self.comes.append((away, remote(ref, ref, send.at[part], recv.at[part], from_s, from_f)))
+
+    def start(self):
+        for here, local, away in self.parts:
+            pl.when(here)(local.start)
+            pl.when(jnp.logical_not(here))(away.start)
+
+    def wait(self):
+        for here, local, away in self.parts:
+            pl.when(here)(local.wait)
+            pl.when(jnp.logical_not(here))(away.wait_send)
+        for away, copy in self.comes:
+            pl.when(away)(copy.wait_recv)
+
+
 def line_step(buf, k, z, s, f, sems, held=None):
     send_up, recv_up, send_dn, recv_dn = sems
     own = pl.ds(0, HALF)
@@ -858,7 +748,7 @@
 
 def forward_body(
     own_n, own_g, w_in_h, w_out_h, bias, cos, sin, idc, idr,
-    n_all, g_all, act_o, slope_o, qkv_o, mixed_o, lse_o, own_o, sib_o,
+    n_all, g_all, a_all, slope_o, qkv_o, lse_o, own_o, sib_o,
     w_in, w_out, x, act, slope, qkv, mixed, lse, p_own, p_sib,
     load, line_n0, line_n1, line_n2, line_n3, line_g0, line_g1, line_g2, line_g3,
     core_n0, core_n1, core_p0, core_p1, out_sems,
@@ -884,19 +774,17 @@
     line_barrier(s, f, z)
 
     def outs(b):
-        return [
-            pltpu.make_async_copy(src, dst.at[b], out_sems.at[i])
-            for i, (src, dst) in enumerate(
-                [(act, act_o), (slope, slope_o), (qkv, qkv_o), (mixed, mixed_o), (lse, lse_o), (p_own, own_o)]
-            )
+        pairs = [
+            (act, a_all.at[b, :, pl.ds(0, units)]), (mixed, a_all.at[b, :, pl.ds(units, 256)]),
+            (slope, slope_o.at[b]), (qkv, qkv_o.at[b]), (lse, lse_o.at[b]), (p_own, own_o.at[b]),
         ]
+        return [pltpu.make_async_copy(src, dst, out_sems.at[i]) for i, (src, dst) in enumerate(pairs)]
 
     def send_sib(b):
         return remote(p_sib, sib_o.at[b], core_p[0].at[b], core_p[1].at[b], s, f + 1 - 2 * (f % 2))
 
     for t in range(4):
         b = line_order(z, t)
-        top = pltpu.make_async_copy(n_all.at[b, own], x.at[own], load.at[0])
         low_half = pltpu.make_async_copy(n_all.at[b, other], x.at[other], load.at[4])
         if t == 0:
             line_step(n_all, 0, z, s, f, line_n, own_n)
@@ -911,6 +799,7 @@
             else:
                 line_step(g_all, 0, z, s, f, line_g, own_g)
             new_blocks(t, z, lambda v: core_copy(n_all, v, s, f, core_n).start())
+            top = pltpu.make_async_copy(n_all.at[b, own], x.at[own], load.at[0])
             top.start()
         core_copy(n_all, b, s, f, core_n).wait_recv()
         low_half.start()
@@ -986,11 +875,11 @@
     return pl.pallas_call(
         forward_body,
         in_specs=[anys] * 4 + [vmem] * 5,
-        out_specs=[anys] * 9,
+        out_specs=[anys] * 8,
         out_shape=[
             shape((4, TOK, width), bf), shape((4, TOK, width), bf),
-            shape((4, TOK, units), bf), shape((4, TOK, units), bf), shape((4, 3, TOK, 256), bf),
-            shape((4, TOK, 256), bf), shape((4, TOK, LANES), f32),
+            shape((4, TOK, units + 256), bf), shape((4, TOK, units), bf), shape((4, 3, TOK, 256), bf),
+            shape((4, TOK, LANES), f32),
             shape((4, HALF, width), bf), shape((4, HALF, width), bf),
         ],
         scratch_shapes=[
@@ -1064,7 +953,7 @@
             remote(out.at[way], land.at[way, k], sends.at[way, k], recvs.at[way, k], s, to).start()
 
 
-def line_sum_end(z, s, f, own, sib, land, stage, out, loads, sends, recvs, result):
+def line_sum_end(z, s, f, own, sib, land, stage, out, loads, sends, recvs):
     terms = [
         pltpu.make_async_copy(own.at[z], stage.at[0], loads.at[0]),
         pltpu.make_async_copy(sib.at[z], stage.at[1], loads.at[1]),
@@ -1092,16 +981,13 @@
             sum_add(stage.at[0], [stage.at[0], stage.at[2]])
 
     sum_add(stage.at[0], [stage.at[0], stage.at[1]])
-    copy = pltpu.make_async_copy(stage.at[0], result, loads.at[0])
-    copy.start()
-    copy.wait()
 
 
 def backward_body(
     g_part, w_in_h, w_out_h, slope_h, qkv_h, lse_h, p_own, p_sib, cos, sin, idc, idr,
-    g_all, gh_o, gp_o, own_o, sib_o, branch, land, sums,
+    g_all, b_all, own_o, sib_o, branch, land, sums,
     w_in, w_out, x, slope, qkv, lse, gh, gmix, gp, acc_k, acc_v, u_own, u_sib, stage, rs_out,
-    load, l0, l1, l2, l3, core_0, core_1, core_u0, core_u1, out_sems, rs_send, rs_recv,
+    load, l0, l1, l2, l3, core_0, core_1, core_u0, core_u1, out_sems, rs_send, rs_recv, pb_send, pb_recv,
 ):
     s, f = lax.axis_index("seq"), lax.axis_index("fsdp")
     z = f // 2
@@ -1116,7 +1002,7 @@
     ]
     for copy in first:
         copy.start()
-    line_barrier(s, f, z)
+    near_barrier(s, f)
     swap = lambda b: core_copy(g_all, b, s, f, core)
     new_blocks(0, z, lambda b: swap(b).start())
     line_step(g_all, 1, z, s, f, line)
@@ -1124,6 +1010,7 @@
     reduce_args = (z, s, f, p_own, p_sib, land, stage, rs_out, load.at[pl.ds(8, 3)], rs_send, rs_recv)
     line_sum_step(0, *reduce_args)
     sums[...] = jnp.zeros_like(sums)
+    back = PlaneBack(stage.at[0], branch, s, f, pb_send, pb_recv, load.at[7])
 
     def ins(b):
         return [
@@ -1132,10 +1019,9 @@
         ]
 
     def outs(b):
-        return [
-            pltpu.make_async_copy(src, dst.at[b], out_sems.at[i])
-            for i, (src, dst) in enumerate([(gh, gh_o), (gp, gp_o), (u_own, own_o)])
-        ]
+        pairs = [(gh, b_all.at[b, :, pl.ds(0, units)]), (u_own, own_o.at[b])]
+        pairs += [(gp.at[i], b_all.at[b, :, pl.ds(units + 256 * i, 256)]) for i in range(3)]
+        return [pltpu.make_async_copy(src, dst, out_sems.at[i]) for i, (src, dst) in enumerate(pairs)]
 
     def send_sib(b):
         return remote(u_sib, sib_o.at[b], core_u0.at[b], core_u1.at[b], s, f + 1 - 2 * (f % 2))
@@ -1204,8 +1090,11 @@
             line_step(g_all, 2, z, s, f, line)
             new_blocks(2, z, lambda v: swap(v).start())
             line_sum_step(1, *reduce_args)
+        if t == 2:
+            line_sum_step(2, *reduce_args)
         if t == 3:
-            line_sum_step(2, *reduce_args)
+            line_sum_end(*reduce_args)
+            back.start()
 
         @pl.loop(0, u_own.shape[1] // 256)
         def _(j):
@@ -1220,7 +1109,6 @@
             copy.start()
         send_sib(b).start()
 
-    line_sum_end(*reduce_args, branch)
     last = line_order(z, 3)
     for copy in outs(last):
         copy.wait()
@@ -1230,6 +1118,7 @@
         send_sib(b).wait_recv()
     for k in (1, 2):
         line_sent(g_all, k, z, s, f, line)
+    back.wait()
 
 
 def backward_call(g_part, w_in, w_out, slope, qkv, lse, p_own, p_sib, cos, sin, ids_col, ids_row):
@@ -1242,9 +1131,9 @@
     return pl.pallas_call(
         backward_body,
         in_specs=[anys] * 8 + [vmem] * 4,
-        out_specs=[anys] * 7 + [vmem],
+        out_specs=[anys] * 6 + [vmem],
         out_shape=[
-            shape((4, TOK, width), bf), shape((4, TOK, units), bf), shape((4, 3, TOK, 256), bf),
+            shape((4, TOK, width), bf), shape((4, TOK, units + 768), bf),
             shape((4, HALF, width), bf), shape((4, HALF, width), bf), shape((HALF, width), bf),
             shape((2, 3, HALF, width), bf), shape((8, 256), f32),
         ],
@@ -1256,8 +1145,8 @@
             pltpu.VMEM((TOK, 256), f32), pltpu.VMEM((TOK, 256), f32),
             pltpu.VMEM((HALF, width), bf), pltpu.VMEM((HALF, width), bf),
             pltpu.VMEM((3, HALF, width), bf), pltpu.VMEM((2, HALF, width), bf),
-            dma(11), dma(3), dma(3), dma(3), dma(3), dma(4), dma(4), dma(4), dma(4), dma(3),
-            dma(2, 3), dma(2, 3),
+            dma(11), dma(3), dma(3), dma(3), dma(3), dma(4), dma(4), dma(4), dma(4), dma(5),
+            dma(2, 3), dma(2, 3), dma(4), dma(4),
         ],
         compiler_params=pltpu.CompilerParams(
             vmem_limit_bytes=62 * 1024 * 1024, collective_id=1, has_side_effects=True
@@ -1265,6 +1154,318 @@
         cost_estimate=cost(8 * TOK * width * (w_in.shape[0] + w_out.shape[0]), 200e6),
         name="backward",
     )(g_part, w_in, w_out, slope, qkv, lse, p_own, p_sib, cos, sin, ids_col, ids_row)
+
+
+PAIRS = 12
+
+
+def tail_body(
+    a_all, b_all, g_all, n_all, plain, u_own, u_sib, gain, shift, wide_in, more_in,
+    fin_up, fin_out, fin_qkv, u_o, small_o, land,
+    term, r1, r2, hop, stage, rs_out, left, right, acc, acc_s, weight, sides, wide, more, got, small,
+    load, w_sem, r1_s, r1_r, r2_s, r2_r, hop_s, hop_r, r3_s, r3_r, r4_s, r4_r,
+    rs_load, rs_send, rs_recv, pb_s, pb_r, sm_s, sm_r, sq_s, sq_r, own_sems, self_sem,
+):
+    s, f = lax.axis_index("seq"), lax.axis_index("fsdp")
+    z = f // 2
+    x, y = s % 2, s // 2
+    across = (s + 1 - 2 * x, (s + 2) % 4)
+    reduce_args = (z, s, f, u_own, u_sib, land, stage, rs_out, rs_load, rs_send, rs_recv)
+    column = [4, 5, 6, 0, 1, 2, 3, 0, 1, 2, 3, 4]
+
+    def loads(j, k):
+        rows_of, right_of = (b_all, n_all) if j < 7 else (a_all, g_all)
+        slot = k % 2
+        return (
+            pltpu.make_async_copy(rows_of.at[k, :, pl.ds(256 * column[j], 256)], left.at[slot], load.at[slot, 0]),
+            pltpu.make_async_copy(right_of.at[k], right.at[slot], load.at[slot, 1]),
+        )
+
+    def weights(j):
+        return pltpu.make_async_copy(plain.at[pl.ds(256 * column[j], 256)], weight, w_sem)
+
+    for copy in loads(0, 0):
+        copy.start()
+    near_barrier(s, f)
+    sides[...] = jnp.zeros_like(sides)
+    wide[...] = wide_in[...]
+    more[...] = more_in[...]
+
+    def compute(j):
+        if j < 7:
+            weights(j).start()
+
+        @pl.loop(0, 4)
+        def _(k):
+            slot = k % 2
+
+            @pl.when(k < 3)
+            def _():
+                for copy in loads(j, k + 1):
+                    copy.start()
+
+            if j + 1 < PAIRS:
+
+                @pl.when(k == 3)
+                def _():
+                    for copy in loads(j + 1, 0):
+                        copy.start()
+
+            for copy in loads(j, k):
+                copy.wait()
+            part = tn(left[slot], right[slot])
+
+            @pl.when(k == 0)
+            def _():
+                acc[...] = part
+
+            @pl.when(k > 0)
+            def _():
+                acc[...] += part
+
+            if j < 7:
+                part_s = tn(left[slot], jnp.ones((TOK, LANES), bf))
+
+                @pl.when(k == 0)
+                def _():
+                    acc_s[...] = part_s
+
+                @pl.when(k > 0)
+                def _():
+                    acc_s[...] += part_s
+
+        if j < 7:
+            which = 1 if j < 3 else 0
+            weights(j).wait()
+            raw, total = acc[...], acc_s[:, 0:1]
+            term[j] = (raw * gain[which : which + 1, :] + total * shift[which : which + 1, :]).astype(bf)
+            low_w = weight[...].astype(f32)
+            sides[2 * which : 2 * which + 1, :] += jnp.sum(low_w * raw, axis=0, keepdims=True)
+            sides[2 * which + 1 : 2 * which + 2, :] += jnp.sum(low_w * total, axis=0, keepdims=True)
+            if j >= 3:
+                row = jnp.transpose(acc_s[...])
+                for half in range(2):
+                    at = 2 * (j - 3) + half
+                    more[at : at + 1, :] = row[0:1, 128 * half : 128 * half + 128]
+        else:
+            term[j] = acc[...].astype(bf)
+
+    def rows(start, count):
+        return pl.ds(pl.multiple_of(start, 32), count)
+
+    ways = ((0, x, y), (1, y, x))
+
+    def base(p, a, b):
+        return 128 * p + 64 * a + 32 * b
+
+    def result(i, start, count):
+        if i < 4:
+            return fin_up.at[rows(256 * i + start, count)]
+        if i < 9:
+            return fin_out.at[rows(256 * (i - 4) + start, count)]
+        return fin_qkv.at[rows(256 * (i - 9) + start, count)]
+
+    def send1(j, p, a):
+        return remote(
+            term.at[j, rows(128 * p + 64 * (1 - a), 64)], r1.at[j, p], r1_s.at[j, p], r1_r.at[j, p], across[p], f
+        )
+
+    def send2(j, p, a, b):
+        return remote(
+            term.at[j, rows(base(p, a, 1 - b), 32)], r2.at[j, p], r2_s.at[j, p], r2_r.at[j, p], across[1 - p], f
+        )
+
+    def keep3(i, p, a, b):
+        return pltpu.make_async_copy(
+            term.at[i + 3, rows(base(p, a, b), 32)], result(i, base(p, a, b), 32), own_sems.at[i, p]
+        )
+
+    def send3(i, p, a, b):
+        ref = result(i, base(p, a, b), 32)
+        src = term.at[i + 3, rows(base(p, a, b), 32)] if i < 9 else ref
+        return remote(src, ref, r3_s.at[i, p], r3_r.at[i, p], across[1 - p], f)
+
+    def send4(i, p, a):
+        ref = result(i, 128 * p + 64 * a, 64)
+        return remote(ref, ref, r4_s.at[i, p], r4_r.at[i, p], across[p], f)
+
+    def owner(j):
+        head = 8 * j + f
+        return head // 3, head % 3
+
+    def hop_place(i, p, a, b):
+        return fin_qkv.at[rows(256 * i + base(p, a, b), 32)]
+
+    def send_hop(j, p, a, b):
+        to, i = owner(j)
+        return remote(hop.at[j, p], hop_place(i, p, a, b), hop_s.at[j, p], hop_r.at[i, p], s, to)
+
+    def keep_hop(j, p, a, b):
+        return pltpu.make_async_copy(hop.at[j, p], hop_place(owner(j)[1], p, a, b), own_sems.at[9 + j, p])
+
+    def step1(j):
+        for p, a, b in ways:
+            send1(j, p, a).start()
+
+    def step2(j):
+        for p, a, b in ways:
+            send1(j, p, a).wait_recv()
+            at = rows(128 * p + 64 * a, 64)
+            term[j, at, :] = (term[j, at, :].astype(f32) + r1[j, p].astype(f32)).astype(bf)
+            send2(j, p, a, b).start()
+
+    def step3(j):
+        for p, a, b in ways:
+            send2(j, p, a, b).wait_recv()
+            at = rows(base(p, a, b), 32)
+            total = (term[j, at, :].astype(f32) + r2[j, p].astype(f32)).astype(bf)
+            if j >= 3:
+                term[j, at, :] = total
+                send3(j - 3, p, a, b).start()
+                keep3(j - 3, p, a, b).start()
+            else:
+                hop[j, p] = total
+                here = owner(j)[0] == f
+                pl.when(here)(keep_hop(j, p, a, b).start)
+                pl.when(jnp.logical_not(here))(send_hop(j, p, a, b).start)
+
+    def step3_own(i):
+        head, kind = (3 * f + i) % 8, (3 * f + i) // 8
+        for p, a, b in ways:
+            ref = hop_place(i, p, a, b)
+            coming = remote(ref, ref, hop_s.at[i, p], hop_r.at[i, p], s, head)
+            staying = pltpu.make_async_copy(ref, ref, own_sems.at[9 + kind, p])
+            pl.when(head != f)(coming.wait_recv)
+            pl.when(head == f)(staying.wait)
+            send3(9 + i, p, a, b).start()
+
+    def step4(i):
+        for p, a, b in ways:
+            send3(i, p, a, b).wait_recv()
+            if i < 9:
+                keep3(i, p, a, b).wait()
+            send4(i, p, a).start()
+
+    def small_send(step):
+        to = (f + step) % 8
+        return remote(wide.at[to], got.at[step - 1], sm_s.at[step - 1], sm_r.at[step - 1], s, to)
+
+    def small_one():
+        for to in range(8):
+            for v in range(4):
+                for half in range(2):
+                    at = 256 * to + 128 * half
+                    wide[to, 2 * v + half : 2 * v + half + 1, :] = sides[v : v + 1, at : at + 128]
+        for step in range(1, 8):
+            small_send(step).start()
+
+    def small_two():
+        total = wide[f]
+        for step in range(1, 8):
+            small_send(step).wait_recv()
+            total = total + got[step - 1]
+        small[0, 0:16] = total
+        small[0, 16:32] = more[...]
+        small_seq(0).start()
+
+    def small_seq(way):
+        return remote(small.at[2 * way], small.at[2 * way + 1], sq_s.at[way], sq_r.at[way], across[way], f)
+
+    def small_three():
+        small_seq(0).wait_recv()
+        small[2] = small[0] + small[1]
+        small_seq(1).start()
+
+    def small_four():
+        small_seq(1).wait_recv()
+        small_o[...] = small[2] + small[3]
+
+    back = PlaneBack(stage.at[0], u_o, s, f, pb_s, pb_r, self_sem)
+    compute(0)
+    step1(0)
+    line_sum_step(0, *reduce_args)
+    compute(1)
+    step1(1)
+    for it in range(1, 16):
+        if it + 1 < PAIRS:
+            compute(it + 1)
+            step1(it + 1)
+        if it - 1 < PAIRS:
+            step2(it - 1)
+        if 0 <= it - 2 < PAIRS:
+            step3(it - 2)
+        if 5 <= it < 8:
+            step3_own(it - 5)
+        if 0 <= it - 6 < 9:
+            step4(it - 6)
+        if 6 <= it < 9:
+            step4(9 + it - 6)
+        if it == 4:
+            line_sum_step(1, *reduce_args)
+        if it == 7:
+            line_sum_step(2, *reduce_args)
+        if it == 8:
+            small_one()
+        if it == 10:
+            small_two()
+        if it == 11:
+            line_sum_end(*reduce_args)
+            back.start()
+        if it == 12:
+            small_three()
+        if it == 14:
+            small_four()
+
+    back.wait()
+    for j in range(PAIRS):
+        for p, a, b in ways:
+            send4(j, p, a).wait_recv()
+            send1(j, p, a).wait_send()
+            send2(j, p, a, b).wait_send()
+            send3(j, p, a, b).wait_send()
+            send4(j, p, a).wait_send()
+            if j < 3:
+                pl.when(owner(j)[0] != f)(send_hop(j, p, a, b).wait_send)
+
+    for step in range(1, 8):
+        small_send(step).wait_send()
+    for way in range(2):
+        small_seq(way).wait_send()
+
+
+def tail_call(a_all, b_all, g_all, n_all, plain, u_own, u_sib, gain, shift, wide, more):
+    width = plain.shape[1]
+    anys = pl.BlockSpec(memory_space=pl.ANY)
+    vmem = pl.BlockSpec(memory_space=pltpu.VMEM)
+    shape = jax.ShapeDtypeStruct
+    dma = lambda *n: pltpu.SemaphoreType.DMA(n)
+    two = [dma(PAIRS, 2)] * 2
+    return pl.pallas_call(
+        tail_body,
+        in_specs=[anys] * 7 + [vmem] * 4,
+        out_specs=[anys] * 4 + [vmem, anys],
+        out_shape=[
+            shape((1024, width), bf), shape((1280, width), bf), shape((768, width), bf),
+            shape((HALF, width), bf), shape((32, LANES), f32), shape((2, 3, HALF, width), bf),
+        ],
+        scratch_shapes=[
+            pltpu.VMEM((PAIRS, 256, width), bf), pltpu.VMEM((PAIRS, 2, 64, width), bf),
+            pltpu.VMEM((PAIRS, 2, 32, width), bf), pltpu.VMEM((3, 2, 32, width), bf),
+            pltpu.VMEM((3, HALF, width), bf), pltpu.VMEM((2, HALF, width), bf),
+            pltpu.VMEM((2, TOK, 256), bf), pltpu.VMEM((2, TOK, width), bf),
+            pltpu.VMEM((256, width), f32), pltpu.VMEM((256, LANES), f32), pltpu.VMEM((256, width), bf),
+            pltpu.VMEM((8, width), f32), pltpu.VMEM((8, 16, LANES), f32), pltpu.VMEM((16, LANES), f32),
+            pltpu.VMEM((7, 16, LANES), f32), pltpu.VMEM((4, 32, LANES), f32),
+            dma(2, 2), pltpu.SemaphoreType.DMA, *two, *two, dma(3, 2), dma(3, 2), *two, *two,
+            dma(3), dma(2, 3), dma(2, 3), dma(4), dma(4), dma(7), dma(7), dma(2), dma(2), dma(PAIRS, 2),
+            pltpu.SemaphoreType.DMA,
+        ],
+        compiler_params=pltpu.CompilerParams(
+            vmem_limit_bytes=61 * 1024 * 1024, collective_id=2, has_side_effects=True
+        ),
+        cost_estimate=cost(1e11, 600e6),
+        name="tail",
+    )(a_all, b_all, g_all, n_all, plain, u_own, u_sib, gain, shift, wide, more)
 
 
 def pick(slices, which):
@@ -1499,55 +1700,46 @@
     sine = jnp.sin(angles) * jnp.where(lane < ROT_DIM // 2, -1.0, 1.0)
     ids_col, ids_row = ids_here[:, :, None], ids_here[:, None, :]
 
-    n_all, g_part, act_all, slope_all, qkv_all, mixed_all, lse_all, p_own, p_sib = forward_call(
+    n_all, g_part, a_all, slope_all, qkv_all, lse_all, p_own, p_sib = forward_call(
         own_n, own_g, w_in, w_out, bias_in, cosine, sine, ids_col, ids_row
     )
-    g_all, gh_all, gp_all, u_own, u_sib, branch, _, col_sums = backward_call(
+    g_all, b_all, u_own, u_sib, branch, _, col_sums = backward_call(
         g_part, w_in, w_out, slope_all, qkv_all, lse_all, p_own, p_sib, cosine, sine, ids_col, ids_row
     )
-    result = flat + plane_back(branch).astype(f32) + bias_out
-    term_out = g2_call(act_all, mixed_all, g_all)
-    down_out = lax.psum(term_out, "seq").astype(f32)
-    blk = [line_order(z, t) for t in range(4)]
-    parts = [pick(u_own, q).astype(f32) + pick(u_sib, q).astype(f32) for q in blk]
-    u_sum = scatter_z(parts, z).astype(low)
-    u = plane_back(u_sum).astype(f32)
-    grad_input = grad_flat + inv * (
-        u - jnp.mean(u, axis=-1, keepdims=True) - normal * jnp.mean(u * normal, axis=-1, keepdims=True)
-    )
-    term_in, sides, sums = g1_call(gh_all, gp_all, n_all, plain_w, gain, shift)
-    qkv_sum = lax.psum(term_in[units:], "seq").reshape(3, HEAD_DIM, width)
-    up_out = lax.psum(term_in[:units], "seq").astype(f32)
-    kinds = [pick(qkv_sum, third_of(i)) for i in range(3)]
-    qkv_back = [
-        lax.ppermute(kinds[i], "fsdp", [((3 * r + i) % 8, r) for r in range(8)]) for i in range(3)
-    ]
-    qkv_out = jnp.concatenate(qkv_back).astype(f32)
+    result = flat + branch.astype(f32) + bias_out
 
     slots = jnp.zeros((16, HEAD_DIM), f32)
     slots = lax.dynamic_update_slice(slots, col_sums[0:1], (f, 0))
     slots = lax.dynamic_update_slice(slots, col_sums[1:2], (8 + f, 0))
-    spread = jnp.concatenate([sides[:4], jnp.sum(grad_flat, axis=0)[None]])
+    spread = jnp.concatenate([jnp.zeros((4, width), f32), jnp.sum(grad_flat, axis=0)[None]])
     wide = jnp.concatenate(
         [spread.reshape(5, 8, 256).transpose(1, 0, 2).reshape(8, 5 * 256), slots.reshape(8, 512)], axis=1
     )
-    wide = after(wide, u_sum)
-    mine = sum_small(jnp.concatenate([scatter_small(wide, f), sums[:units, 0], col_sums[2]]))
+    wide = jnp.pad(wide, ((0, 0), (0, 256))).reshape(8, 16, LANES)
+    more = jnp.pad(jnp.concatenate([jnp.zeros((units,), f32), col_sums[2]]), (0, 768)).reshape(16, LANES)
+    up_low, out_low, qkv_low, u, small_sum, _ = tail_call(
+        a_all, b_all, g_all, n_all, plain_w, u_own, u_sib, gain, shift, wide, more
+    )
+    u = u.astype(f32)
+    grad_input = grad_flat + inv * (
+        u - jnp.mean(u, axis=-1, keepdims=True) - normal * jnp.mean(u * normal, axis=-1, keepdims=True)
+    )
+    mine = small_sum.reshape(-1)
     vectors = [mine[i * 256 : (i + 1) * 256] for i in range(5)]
     qk_grad = mine[1280:1792]
-    up_bias_grad = mine[1792 : 1792 + units]
-    value_grad = mine[1792 + units :]
+    up_bias_grad = mine[2048 : 2048 + units]
+    value_grad = mine[2048 + units : 2304 + units]
     return (
         result.reshape(groups, piece, width),
         grad_input.reshape(groups, piece, width),
-        qkv_out,
+        qkv_low.astype(f32),
         qk_grad,
         value_grad,
-        down_out[units:],
+        out_low[units:].astype(f32),
         vectors[4],
-        up_out,
+        up_low.astype(f32),
         up_bias_grad,
-        down_out[:units],
+        out_low[:units].astype(f32),
         vectors[4],
         vectors[2],
         vectors[3],

time: 988 us -> 842 us (0.85)
  waiting for transfers between devices: 275 us -> 51.9 us
  Pallas kernels: 434 us -> 636 us
  starting transfers between devices: 104 us -> 35 us
  other arithmetic: 107 us -> 85.9 us
  local copies, waits for them, and re-layouts: 40.4 us -> 21.8 us
  between operations: 16.1 us -> 2.09 us
    pallas_call x2 -> x1, Pallas kernels: 82.4 us -> 267 us  [tail_call(): pl.pallas_call(tail_body, in_specs=[anys] * 7 + [vmem] * 4, out_specs=[an...]
    ppermute x19 -> x0, waiting for transfers between devices: 163 us -> none  [the longest x5 92.8 us: along_z(): lax.ppermute(value, 'fsdp', [(2 * a + c, 2 * b + c) for a, b in pairs for...]
    ppermute x19 -> x0, starting transfers between devices: 63.7 us -> none  [the longest x5 33.8 us: along_z(): lax.ppermute(value, 'fsdp', [(2 * a + c, 2 * b + c) for a, b in pairs for...]
    psum x1 -> x0, waiting for transfers between devices: 40.7 us -> none  [split_body(): qkv_sum = lax.psum(term_in[units:], 'seq').reshape(3, HEAD_DIM, width)]
    ppermute x5 -> x3, waiting for transfers between devices: 49.4 us -> 21.3 us  [swap_seq(): return lax.ppermute(value, 'seq', [(i, i ^ bit) for i in range(4)])]
    convert_element_type x7 -> x4, other arithmetic: 35.9 us -> 18.2 us  [the longest x1 6.81 us: split_body(): out_low[:units].astype(f32)]
    slice x10 -> x2, local copies, waits for them, and re-layouts: 18.6 us -> 1.41 us  [the longest x1 0.81 us: split_body(): col_sums[2]]
    pallas_call x1, Pallas kernels: 162 us -> 179 us  [backward_call(): pl.pallas_call(backward_body, in_specs=[anys] * 8 + [vmem] * 4, out_specs...]
  transfers between devices with their start and end apart: 39 -> 17, of which waited for: 20 -> 7; matrix products, arithmetic and copies ran while one was open for 12% -> 7% of each run, Pallas kernels for 3% -> 0%
where the time goes in v3:
time: 842 us; the launch traced here: 833 us
  Pallas kernels  636 us (76%)
  other arithmetic  85.9 us (10%)
  waiting for transfers between devices  51.9 us (6%)
  starting transfers between devices  35 us (4%)
  local copies, waits for them, and re-layouts  21.8 us (3%)
    pallas_call x1, Pallas kernels, tail_call(): pl.pallas_call(tail_body, in_specs=[anys] * 7 + [vmem] * 4, out_specs=[an...  267 us
    pallas_call x1, Pallas kernels, forward_call(): pl.pallas_call(forward_body, in_specs=[anys] * 4 + [vmem] * 5, out_specs=...  190 us
    pallas_call x1, Pallas kernels, backward_call(): pl.pallas_call(backward_body, in_specs=[anys] * 8 + [vmem] * 4, out_specs...  179 us
    ppermute x8, waiting for transfers between devices, plane_out(): lax.ppermute(pick(parts, (k + s) % 4), both_axes, spread_pairs(k))  21.6 us
    ppermute x3, waiting for transfers between devices, swap_seq(): return lax.ppermute(value, 'seq', [(i, i ^ bit) for i in range(4)])  21.3 us
    ppermute x8, starting transfers between devices, plane_out(): lax.ppermute(pick(parts, (k + s) % 4), both_axes, spread_pairs(k))  21.2 us
  transfers between devices with their start and end apart: 17, of which 7 were waited for; matrix products, arithmetic and copies ran while one was open for 7% of the time, Pallas kernels for 0%

profile of v3, /device:TPU:0, one launch (start us, length us, event | category | flops | bytes accessed | tf_op | source)
XLA Modules:
  0.0 832.6 jit_solution(4077935104130027679)
XLA Ops:
  9.2 3.6 collective-permute-start.11
  14.0 4.5 collective-permute-start.13
  32.3 4.2 convert_element_type.106
  44.1 6.6 collective-permute-done.10
  53.4 4.2 fusion.1
  57.6 3.4 fusion
  61.0 8.9 %sine_multiply_fusion = (f32[4,1024,128]{2,1,0:T(8,128)}, f32[4,1024,128]{2,1,0:T(8,128)}) fusion(f32[128]{0:T(128)S(1)} %get-tuple-element.149, f32[128]{0:T(128)S(1)} %get-tuple-element.150, f32[4,1024]{1,0:T(4,128)S(1)} %add_convert_fusion, pred[128]{0:T(512)(128)(4,1)S(1)} %iota_compare_fusion.2), kind=kLoop, calls=%fused_computation.27 | loop fusion | flops 1572864 | bytes 4211840 | tf_op jit(solution)/shard_map/mul | solution.py:1700
  75.5 3.5 collective-permute-start.3
  84.1 7.1 collective-permute-done.2
  91.3 7.6 collective-permute-done.3
  101.6 5.3 collective-permute-start.4
  109.2 6.5 collective-permute-done.14
  118.1 14.9 %collective-permute-done.15 = bf16[3,64,2048]{2,1,0:T(8,128)(2,1)S(1)} collective-permute-done((bf16[3,64,2048]{2,1,0:T(8,128)(2,1)S(1)}, bf16[3,64,2048]{2,1,0:T(8,128)(2,1)S(1)}, u32[]{:S(2)}, u32[]{:S(2)}) %collective-permute-start.15) | collective-permute-done | bytes 786464 | tf_op jit(solution)/shard_map/ppermute | solution.py:1522
  140.6 7.6 pad_maximum_fusion.w_in_h
  148.2 6.9 collective-permute-done.7
  155.1 3.1 pad_maximum_fusion.5.own_g
  158.2 190.0 %forward.1 = (bf16[4,1024,2048]{2,1,0:T(8,128)(2,1)}, bf16[4,1024,2048]{2,1,0:T(8,128)(2,1)}, bf16[4,1024,1280]{2,1,0:T(8,128)(2,1)}, bf16[4,1024,1024]{2,1,0:T(...) custom-call(bf16[512,2048]{1,0:T(8,128)(2,1)} %copy-done.9, ...), custom_call_target="tpu_custom_call" | custom-call | flops 51539607552 | bytes 200000000 | tf_op jit(solution)/shard_map/forward/pallas_call | solution.py:875
  348.2 178.7 %backward.1 = (bf16[4,1024,2048]{2,1,0:T(8,128)(2,1)}, bf16[4,1024,1792]{2,1,0:T(8,128)(2,1)}, bf16[4,512,2048]{2,1,0:T(8,128)(2,1)}, bf16[4,512,2048]{2,1,0:T(8...) custom-call(bf16[4,1024,2048]{2,1,0:T(8,128)(2,1)} %get-tuple-elemen, ...), custom_call_target="tpu_custom_call", output_to_operand_aliasing={{0}: (0, {})} | custom-call | flops 51539607552 | bytes 200000000 | tf_op jit(solution)/shard_map/backward/pallas_call | solution.py:1131
  529.0 7.6 pad_maximum_fusion.1.plain
  536.6 267.3 %tail.1 = (bf16[1024,2048]{1,0:T(8,128)(2,1)}, bf16[1280,2048]{1,0:T(8,128)(2,1)}, bf16[768,2048]{1,0:T(8,128)(2,1)}, bf16[512,2048]{1,0:T(8,128)(2,1)}, f32[32,...) custom-call(bf16[4,1024,1280]{2,1,0:T(8,128)(2,1)} %get-tuple-element.43.a_all, ...), custom_call_target="tpu_custom_call" | custom-call | flops 99999997952 | bytes 600000000 | tf_op jit(solution)/shard_map/tail/pallas_call | solution.py:1443
  803.9 6.8 slice_convert_fusion
  817.1 4.4 convert_element_type.117
  821.5 4.0 convert_element_type.115
  826.7 4.9 fusion.4
  (167 shorter events, 69.1 us)
Async XLA Ops:
  6.3 33.4 %collective-permute-start.8 = (f32[1,4112]{1,0:T(1,128)S(1)}, f32[1,4112]{1,0:T(1,128)S(1)}, u32[]{:S(2)}, u32[]{:S(2)}) collective-permute-start(f32[1,4112]{1,0:T(1,128)S(1)} %broadcast_in_dim.48), channel_id=1, source_target_pairs={{0,1},{1,0},{2,3},{3,2},{4,5},{5,4},{6,7},{7,6},{8,9},{9,8},{10,11... | collective-permute-start | bytes 49352 | tf_op jit(solution)/shard_map/ppermute | solution.py:1528
  9.2 64.6 %collective-permute-start.11 = (bf16[64,2048]{1,0:T(8,128)(2,1)}, bf16[64,2048]{1,0:T(8,128)(2,1)}, u32[]{:S(2)}, u32[]{:S(2)}) collective-permute-start(bf16[64,2048]{1,0:T(8,128)(2,1)} %get-tuple-element.82), channel_id=1, source_target_pairs={{0,0},{1,3},{2,6},{3,1},{4,4},{5,7},{6,2},{7,5},{8,8},{9,11},{10,1... | collective-permute-start | bytes 786440 | tf_op jit(solution)/shard_map/ppermute | solution.py:1655
  12.8 62.7 %collective-permute-start.12 = (bf16[64,2048]{1,0:T(8,128)(2,1)}, bf16[64,2048]{1,0:T(8,128)(2,1)}, u32[]{:S(2)}, u32[]{:S(2)}) collective-permute-start(bf16[64,2048]{1,0:T(8,128)(2,1)} %get-tuple-element.84), channel_id=1, source_target_pairs={{0,1},{1,4},{2,7},{3,2},{4,5},{5,0},{6,3},{7,6},{8,9},{9,12},{10,1... | collective-permute-start | bytes 786440 | tf_op jit(solution)/shard_map/ppermute | solution.py:1655
  14.0 65.0 %collective-permute-start.13 = (bf16[64,2048]{1,0:T(8,128)(2,1)}, bf16[64,2048]{1,0:T(8,128)(2,1)}, u32[]{:S(2)}, u32[]{:S(2)}) collective-permute-start(bf16[64,2048]{1,0:T(8,128)(2,1)} %get-tuple-element.83), channel_id=1, source_target_pairs={{0,2},{1,5},{2,0},{3,3},{4,6},{5,1},{6,4},{7,7},{8,10},{9,13},{10,... | collective-permute-start | bytes 786440 | tf_op jit(solution)/shard_map/ppermute | solution.py:1655
  27.9 53.0 %collective-permute-start = (bf16[128,2048]{1,0:T(8,128)(2,1)}, bf16[128,2048]{1,0:T(8,128)(2,1)S(1)}, u32[]{:S(2)}, u32[]{:S(2)}) collective-permute-start(bf16[128,2048]{1,0:T(8,128)(2,1)} %get-tuple-element.76), channel_id=1, source_target_pairs={{0,0},{1,16},{2,2},{3,18},{4,4},{5,20},{6,6},{7,22},{8,1},{9,17},{... | collective-permute-start | bytes 1572872 | tf_op jit(solution)/shard_map/ppermute | solution.py:1632
  39.8 4.0 collective-permute-start.9
  43.9 6.9 collective-permute-start.10
  50.7 31.2 %collective-permute-start.1 = (bf16[128,2048]{1,0:T(8,128)(2,1)}, bf16[128,2048]{1,0:T(8,128)(2,1)S(1)}, u32[]{:S(2)}, u32[]{:S(2)}) collective-permute-start(bf16[128,2048]{1,0:T(8,128)(2,1)} %get-tuple-element.75), channel_id=1, source_target_pairs={{0,1},{1,17},{2,3},{3,19},{4,5},{5,21},{6,7},{7,23},{8,8},{9,24},{... | collective-permute-start | bytes 1572872 | tf_op jit(solution)/shard_map/ppermute | solution.py:1632
  61.0 12.2 %copy-start.14 = (f32[1024]{0:T(1024)S(1)}, f32[1024]{0:T(1024)}, u32[]{:S(2)}) copy-start(f32[1024]{0:T(1024)} %param.22) | copy-start | bytes 12292
  73.8 17.4 %collective-permute-start.2 = (bf16[128,2048]{1,0:T(8,128)(2,1)}, bf16[128,2048]{1,0:T(8,128)(2,1)S(1)}, u32[]{:S(2)}, u32[]{:S(2)}) collective-permute-start(bf16[128,2048]{1,0:T(8,128)(2,1)} %get-tuple-element.74), channel_id=1, source_target_pairs={{0,8},{1,24},{2,10},{3,26},{4,12},{5,28},{6,14},{7,30},{8,9},{9,25... | collective-permute-start | bytes 1572872 | tf_op jit(solution)/shard_map/ppermute | solution.py:1632
  75.5 23.3 %collective-permute-start.3 = (bf16[128,2048]{1,0:T(8,128)(2,1)}, bf16[128,2048]{1,0:T(8,128)(2,1)S(1)}, u32[]{:S(2)}, u32[]{:S(2)}) collective-permute-start(bf16[128,2048]{1,0:T(8,128)(2,1)} %get-tuple-element.73), channel_id=1, source_target_pairs={{0,9},{1,25},{2,11},{3,27},{4,13},{5,29},{6,15},{7,31},{8,0},{9,16... | collective-permute-start | bytes 1572872 | tf_op jit(solution)/shard_map/ppermute | solution.py:1632
  80.4 35.2 %collective-permute-start.14 = (bf16[3,64,2048]{2,1,0:T(8,128)(2,1)S(1)}, bf16[3,64,2048]{2,1,0:T(8,128)(2,1)S(1)}, u32[]{:S(2)}, u32[]{:S(2)}) collective-permute-start(bf16[3,64,2048]{2,1,0:T(8,128)(2,1)S(1)} %get-tuple-element.78), channel_id=1, source_target_pairs={{0,8},{8,0},{16,24},{24,16},{1,9},{9,1},{17,25},{25,17},{2,10},{10... | collective-permute-start | bytes 2359304 | tf_op jit(solution)/shard_map/ppermute | solution.py:1522
  80.9 52.0 %collective-permute-start.15 = (bf16[3,64,2048]{2,1,0:T(8,128)(2,1)S(1)}, bf16[3,64,2048]{2,1,0:T(8,128)(2,1)S(1)}, u32[]{:S(2)}, u32[]{:S(2)}) collective-permute-start(bf16[3,64,2048]{2,1,0:T(8,128)(2,1)S(1)} %get-tuple-element.78), channel_id=1, source_target_pairs={{0,16},{8,24},{16,0},{24,8},{1,17},{9,25},{17,1},{25,9},{2,18},{10... | collective-permute-start | bytes 2359304 | tf_op jit(solution)/shard_map/ppermute | solution.py:1522
  81.9 53.4 %collective-permute-start.16 = (bf16[3,64,2048]{2,1,0:T(8,128)(2,1)S(1)}, bf16[3,64,2048]{2,1,0:T(8,128)(2,1)S(1)}, u32[]{:S(2)}, u32[]{:S(2)}) collective-permute-start(bf16[3,64,2048]{2,1,0:T(8,128)(2,1)S(1)} %get-tuple-element.78), channel_id=1, source_target_pairs={{0,24},{8,16},{16,8},{24,0},{1,25},{9,17},{17,9},{25,1},{2,26},{10... | collective-permute-start | bytes 2359304 | tf_op jit(solution)/shard_map/ppermute | solution.py:1522
  101.6 46.6 %collective-permute-start.4 = (bf16[128,2048]{1,0:T(8,128)(2,1)}, bf16[128,2048]{1,0:T(8,128)(2,1)}, u32[]{:S(2)}, u32[]{:S(2)}) collective-permute-start(bf16[128,2048]{1,0:T(8,128)(2,1)} %get-tuple-element.69), channel_id=1, source_target_pairs={{0,0},{1,16},{2,2},{3,18},{4,4},{5,20},{6,6},{7,22},{8,1},{9,17},{... | collective-permute-start | bytes 1572872 | tf_op jit(solution)/shard_map/ppermute | solution.py:1632
  107.0 41.2 %collective-permute-start.5 = (bf16[128,2048]{1,0:T(8,128)(2,1)}, bf16[128,2048]{1,0:T(8,128)(2,1)}, u32[]{:S(2)}, u32[]{:S(2)}) collective-permute-start(bf16[128,2048]{1,0:T(8,128)(2,1)} %get-tuple-element.72), channel_id=1, source_target_pairs={{0,1},{1,17},{2,3},{3,19},{4,5},{5,21},{6,7},{7,23},{8,8},{9,24},{... | collective-permute-start | bytes 1572872 | tf_op jit(solution)/shard_map/ppermute | solution.py:1632
  115.6 32.6 %collective-permute-start.6 = (bf16[128,2048]{1,0:T(8,128)(2,1)}, bf16[128,2048]{1,0:T(8,128)(2,1)}, u32[]{:S(2)}, u32[]{:S(2)}) collective-permute-start(bf16[128,2048]{1,0:T(8,128)(2,1)} %get-tuple-element.71), channel_id=1, source_target_pairs={{0,8},{1,24},{2,10},{3,26},{4,12},{5,28},{6,14},{7,30},{8,9},{9,25... | collective-permute-start | bytes 1572872 | tf_op jit(solution)/shard_map/ppermute | solution.py:1632
  132.9 22.1 %collective-permute-start.7 = (bf16[128,2048]{1,0:T(8,128)(2,1)}, bf16[128,2048]{1,0:T(8,128)(2,1)}, u32[]{:S(2)}, u32[]{:S(2)}) collective-permute-start(bf16[128,2048]{1,0:T(8,128)(2,1)} %get-tuple-element.70), channel_id=1, source_target_pairs={{0,9},{1,25},{2,11},{3,27},{4,13},{5,29},{6,15},{7,31},{8,0},{9,16... | collective-permute-start | bytes 1572872 | tf_op jit(solution)/shard_map/ppermute | solution.py:1632
  137.0 11.2 %copy-start.2 = (bf16[3,4,64,2048]{3,2,1,0:T(8,128)(2,1)}, bf16[3,4,64,2048]{3,2,1,0:T(8,128)(2,1)S(1)}, u32[]{:S(2)}) copy-start(bf16[3,4,64,2048]{3,2,1,0:T(8,128)(2,1)S(1)} %get-tuple-element.60) | copy-start | bytes 9437188
  803.9 9.8 %copy-start.13 = (f32[32,128]{1,0:T(8,128)S(1)}, f32[32,128]{1,0:T(8,128)}, u32[]{:S(2)}) copy-start(f32[32,128]{1,0:T(8,128)} %get-tuple-element.52) | copy-start | bytes 49156
  803.9 11.5 %copy-start = (f32[2,256,2048]{2,1,0:T(8,128)S(1)}, f32[2,256,2048]{2,1,0:T(8,128)}, u32[]{:S(2)}) copy-start(f32[2,256,2048]{2,1,0:T(8,128)} %param.16) | copy-start | bytes 12582916
  803.9 11.5 %copy-start.11 = (f32[1,2,2,128]{3,1,2,0:T(2,128)S(1)}, f32[1,2,2,128]{3,1,2,0:T(2,128)}, u32[]{:S(2)}) copy-start(f32[1,2,2,128]{3,1,2,0:T(2,128)} %copy.44) | copy-start | bytes 6148
  803.9 11.5 %copy-start.12 = (f32[1,2,2,128]{3,1,2,0:T(2,128)S(1)}, f32[1,2,2,128]{3,1,2,0:T(2,128)}, u32[]{:S(2)}) copy-start(f32[1,2,2,128]{3,1,2,0:T(2,128)} %copy.51) | copy-start | bytes 6148
  814.3 17.3 %copy-start.15 = (f32[256]{0:T(256)}, f32[256]{0:T(256)S(1)}, u32[]{:S(2)}) copy-start(f32[256]{0:T(256)S(1)} %get-tuple-element.178) | copy-start | bytes 3076
  (9 other events, 38.7 us)

commit v4 on v3

--- a/solution.py
+++ b/solution.py
@@ -643,6 +643,61 @@
     pl.semaphore_wait(barrier, 13)
 
 
+class PlaneOut:
+    def __init__(self, src, dst, s, f, send, recv, own_sem):
+        c = f % 2
+        mine = 2 * (s % 2) + c
+        self.parts = []
+        for j in range(4):
+            k = (j - s + 4) % 4
+            to_s, to_f = 2 * c + j // 2, f - c + j % 2
+            place = dst.at[pl.ds(pl.multiple_of(128 * k, 128), 128)]
+            here = (to_s == s) & (to_f == f)
+            self.parts.append(
+                (
+                    here,
+                    pltpu.make_async_copy(src.at[j], place, own_sem),
+                    remote(src.at[j], place, send.at[j], recv.at[k], to_s, to_f),
+                )
+            )
+        self.comes = []
+        for k in range(4):
+            from_s, from_f = (mine - k + 4) % 4, f - c + s // 2
+            ref = dst.at[pl.ds(128 * k, 128)]
+            away = jnp.logical_not((from_s == s) & (from_f == f))
+            self.comes.append((away, remote(ref, ref, send.at[k], recv.at[k], from_s, from_f)))
+
+    def start(self, j):
+        here, local, away = self.parts[j]
+        pl.when(here)(local.start)
+        pl.when(jnp.logical_not(here))(away.start)
+
+    def arrive(self):
+        for here, local, away in self.parts:
+            pl.when(here)(local.wait)
+        for away, copy in self.comes:
+            pl.when(away)(copy.wait_recv)
+
+    def sent(self):
+        for here, local, away in self.parts:
+            pl.when(jnp.logical_not(here))(away.wait_send)
+
+    def wait(self):
+        self.arrive()
+        self.sent()
+
+
+def expand_tables(cos4, sin4, b, cos, sin):
+    lane = lax.broadcasted_iota(jnp.int32, (256, LANES), 1)
+    for q in range(4):
+        at = pl.ds(256 * q, 256)
+        c, s_ = cos4[b], sin4[b]
+        if q > 0:
+            c, s_ = pltpu.roll(c, 128 - 32 * q, 1), pltpu.roll(s_, 128 - 32 * q, 1)
+        cos[at, :] = jnp.where(lane < 32, c, jnp.where(lane < 64, pltpu.roll(c, 32, 1), 1.0))
+        sin[at, :] = jnp.where(lane < 32, -s_, jnp.where(lane < 64, pltpu.roll(s_, 32, 1), 0.0))
+
+
 class PlaneBack:
     def __init__(self, src, dst, s, f, send, recv, own_sem):
         c = f % 2
@@ -747,11 +802,11 @@
 
 
 def forward_body(
-    own_n, own_g, w_in_h, w_out_h, bias, cos, sin, idc, idr,
-    n_all, g_all, a_all, slope_o, qkv_o, lse_o, own_o, sib_o,
-    w_in, w_out, x, act, slope, qkv, mixed, lse, p_own, p_sib,
-    load, line_n0, line_n1, line_n2, line_n3, line_g0, line_g1, line_g2, line_g3,
-    core_n0, core_n1, core_p0, core_p1, out_sems,
+    own_n, g_low, heads, up_h, down_h, out_h, bias, gain, shift, cos4, sin4, idc, idr,
+    n_all, g_all, w_in_o, w_out_o, a_all, slope_o, qkv_o, lse_o, own_o, sib_o,
+    w_in, w_out, x, normed, act, slope, qkv, mixed, lse, p_own, p_sib, g_out, wide, cos, sin,
+    load, w_load, w_store, line_n0, line_n1, line_n2, line_n3, line_g0, line_g1, line_g2, line_g3,
+    core_n0, core_n1, core_p0, core_p1, out_sems, po_s, po_r, h_s, h_r,
 ):
     s, f = lax.axis_index("seq"), lax.axis_index("fsdp")
     z = f // 2
@@ -759,19 +814,41 @@
     core_n, core_p = (core_n0, core_n1), (core_p0, core_p1)
     own, other = pl.ds(0, HALF), pl.ds(HALF, HALF)
     units = act.shape[1]
-    first = [
-        pltpu.make_async_copy(own_n, x.at[own], load.at[0]),
-        pltpu.make_async_copy(own_g, p_sib, load.at[3]),
-        pltpu.make_async_copy(w_in_h, w_in, load.at[1]),
-        pltpu.make_async_copy(w_out_h, w_out, load.at[2]),
+    half = (s % 2 + s // 2) % 2
+    across = (s + 1 - 2 * (s % 2), (s + 2) % 4)
+
+    def head_rows(kind, which, count, start=0):
+        return w_in.at[pl.ds(pl.multiple_of(units + 256 * kind + 128 * which + start, 64), count)]
+
+    first = [pltpu.make_async_copy(own_n, x.at[own], load.at[0])] + [
+        pltpu.make_async_copy(g_low.at[pl.ds(128 * j, 128)], g_out.at[j], load.at[1 + j]) for j in range(4)
     ]
-    keep = [
-        pltpu.make_async_copy(x.at[own], n_all.at[z, own], load.at[0]),
-        pltpu.make_async_copy(p_sib, g_all.at[z, own], load.at[3]),
-    ]
-    for copy in first:
+    held = [pltpu.make_async_copy(heads.at[i], head_rows(i, half, 128), load.at[5 + i]) for i in range(3)]
+    keep = pltpu.make_async_copy(x.at[own], n_all.at[z, own], load.at[0])
+    chunks = [(up_h, w_in, i) for i in range(units // 256)]
+    chunks += [(down_h, w_out, i) for i in range(units // 256)] + [(out_h, w_out, units // 256)]
+
+    def chunk_load(i):
+        src, dst, at = chunks[i]
+        place = at if src is not out_h else 0
+        return pltpu.make_async_copy(src.at[pl.ds(256 * place, 256)], wide.at[i % 2], w_load.at[i % 2])
+
+    def send_head(kind, way):
+        return remote(
+            heads.at[kind, pl.ds(64 * way, 64)], head_rows(kind, half, 64, 64 * way),
+            h_s.at[kind, way], h_r.at[kind, way], across[way], f,
+        )
+
+    def come_head(kind, way):
+        ref = head_rows(kind, 1 - half, 64, 64 * way)
+        return remote(ref, ref, h_s.at[kind, way], h_r.at[kind, way], across[way], f)
+
+    for copy in first + held:
         copy.start()
-    line_barrier(s, f, z)
+    chunk_load(0).start()
+    near_barrier(s, f)
+    spread = PlaneOut(g_out, g_all.at[z, own], s, f, po_s, po_r, load.at[8])
+    store = [pltpu.make_async_copy(w_in, w_in_o, w_store.at[0]), pltpu.make_async_copy(w_out, w_out_o, w_store.at[1])]
 
     def outs(b):
         pairs = [
@@ -785,27 +862,40 @@
 
     for t in range(4):
         b = line_order(z, t)
-        low_half = pltpu.make_async_copy(n_all.at[b, other], x.at[other], load.at[4])
+        low_half = pltpu.make_async_copy(n_all.at[b, other], x.at[other], load.at[9])
         if t == 0:
             line_step(n_all, 0, z, s, f, line_n, own_n)
             core_copy(n_all, z, s, f, core_n, own_n).start()
-            for copy, then in zip(first[:2], keep):
+            for kind in range(3):
+                for way in range(2):
+                    send_head(kind, way).start()
+            first[0].wait()
+            keep.start()
+            for i, (src, dst, at) in enumerate(chunks):
+                if i + 1 < len(chunks):
+                    chunk_load(i + 1).start()
+                chunk_load(i).wait()
+                dst[pl.ds(256 * at, 256), :] = wide[i % 2].astype(bf)
+            for copy in first[1:]:
                 copy.wait()
-                then.start()
         else:
             line_arrive(n_all, t - 1, z, s, f, line_n)
             if t < 3:
                 line_step(n_all, t, z, s, f, line_n)
             else:
-                line_step(g_all, 0, z, s, f, line_g, own_g)
+                spread.arrive()
+                line_step(g_all, 0, z, s, f, line_g)
             new_blocks(t, z, lambda v: core_copy(n_all, v, s, f, core_n).start())
             top = pltpu.make_async_copy(n_all.at[b, own], x.at[own], load.at[0])
             top.start()
+        if t == 1:
+            for j in range(4):
+                spread.start(j)
         core_copy(n_all, b, s, f, core_n).wait_recv()
         low_half.start()
+        expand_tables(cos4, sin4, b, cos, sin)
         if t == 0:
-            for copy in first[2:] + keep:
-                copy.wait()
+            keep.wait()
         else:
             top.wait()
             before = line_order(z, t - 1)
@@ -814,20 +904,39 @@
             send_sib(before).wait_send()
         low_half.wait()
 
+        def norm(which):
+            @pl.loop(0, TOK // 64)
+            def _(i):
+                at = pl.ds(pl.multiple_of(i * 64, 64), 64)
+                value = x[at, :].astype(f32) * gain[which : which + 1, :] + shift[which : which + 1, :]
+                normed[at, :] = value.astype(bf)
+
+        norm(0)
+
         @pl.loop(0, units // 256)
         def _(j):
             at = pl.ds(pl.multiple_of(j * 256, 256), 256)
-            h = nt(x[...], w_in[at, :]) + bias[:, at]
+            h = nt(normed[...], w_in[at, :]) + bias[:, at]
             act[:, at], slope[:, at] = gelu_pair(h)
+
+        norm(1)
+        if t == 0:
+            for copy in held:
+                copy.wait()
+            for kind in range(3):
+                for way in range(2):
+                    come_head(kind, way).wait_recv()
+            for copy in store:
+                copy.start()
 
         @pl.loop(0, 2)
         def _(j):
             at = pl.ds(pl.multiple_of(units + j * 256, 256), 256)
-            h = nt(x[...], w_in[at, :]) + bias[:, at]
-            qkv[j] = turn(h, cos[b], sin[b]).astype(bf)
+            h = nt(normed[...], w_in[at, :]) + bias[:, at]
+            qkv[j] = turn(h, cos[...], sin[...]).astype(bf)
 
         at = pl.ds(units + 512, 256)
-        qkv[2] = (nt(x[...], w_in[at, :]) + bias[:, at]).astype(bf)
+        qkv[2] = (nt(normed[...], w_in[at, :]) + bias[:, at]).astype(bf)
 
         @pl.loop(0, TOK // 256)
         def _(i):
@@ -863,39 +972,157 @@
         line_sent(n_all, k, z, s, f, line_n)
     line_arrive(g_all, 0, z, s, f, line_g)
     line_sent(g_all, 0, z, s, f, line_g)
-
-
-def forward_call(own_n, own_g, w_in, w_out, bias, cos, sin, ids_col, ids_row):
-    width = own_n.shape[1]
-    units = w_in.shape[0] - 768
+    spread.sent()
+    for copy in store:
+        copy.wait()
+    for kind in range(3):
+        for way in range(2):
+            send_head(kind, way).wait_send()
+
+
+def forward_call(own_n, g_low, heads, up, down, out, bias, gain, shift, cos4, sin4, ids_col, ids_row):
+    width, units = up.shape[1], up.shape[0]
+    anys = pl.BlockSpec(memory_space=pl.ANY)
+    vmem = pl.BlockSpec(memory_space=pltpu.VMEM)
+    shape = jax.ShapeDtypeStruct
+    dma = lambda *n: pltpu.SemaphoreType.DMA(n)
+    return pl.pallas_call(
+        forward_body,
+        in_specs=[anys] * 6 + [vmem] * 7,
+        out_specs=[anys] * 10,
+        out_shape=[
+            shape((4, TOK, width), bf), shape((4, TOK, width), bf),
+            shape((units + 768, width), bf), shape((units + 256, width), bf),
+            shape((4, TOK, units + 256), bf), shape((4, TOK, units), bf), shape((4, 3, TOK, 256), bf),
+            shape((4, TOK, LANES), f32), shape((4, HALF, width), bf), shape((4, HALF, width), bf),
+        ],
+        scratch_shapes=[
+            pltpu.VMEM((units + 768, width), bf), pltpu.VMEM((units + 256, width), bf),
+            pltpu.VMEM((TOK, width), bf), pltpu.VMEM((TOK, width), bf),
+            pltpu.VMEM((TOK, units), bf), pltpu.VMEM((TOK, units), bf), pltpu.VMEM((3, TOK, 256), bf),
+            pltpu.VMEM((TOK, 256), bf), pltpu.VMEM((TOK, LANES), f32),
+            pltpu.VMEM((HALF, width), bf), pltpu.VMEM((HALF, width), bf),
+            pltpu.VMEM((4, 128, width), bf), pltpu.VMEM((2, 256, width), f32),
+            pltpu.VMEM((TOK, LANES), f32), pltpu.VMEM((TOK, LANES), f32),
+            dma(10), dma(2), dma(2), dma(3), dma(3), dma(3), dma(3), dma(3), dma(3), dma(3), dma(3),
+            dma(4), dma(4), dma(4), dma(4), dma(6), dma(4), dma(4), dma(3, 2), dma(3, 2),
+        ],
+        compiler_params=pltpu.CompilerParams(
+            vmem_limit_bytes=60 * 1024 * 1024, collective_id=0, has_side_effects=True
+        ),
+        cost_estimate=cost(8 * TOK * width * (2 * units + 1024), 200e6),
+        name="forward",
+    )(own_n, g_low, heads, up, down, out, bias, gain, shift, cos4, sin4, ids_col, ids_row)
+
+
+def entry_body(
+    resid, grad, qkv, packed, own_n, g_low, heads, small_all,
+    x_in, g_in, q_in, n_out, g_out, q_out,
+    load, q_s, q_r, po_s, po_r, sm_s, sm_r, own_sems,
+):
+    s, f = lax.axis_index("seq"), lax.axis_index("fsdp")
+    half = (s % 2 + s // 2) % 2
+    width = resid.shape[1]
+    parts = [pltpu.make_async_copy(resid.at[pl.ds(128 * j, 128)], x_in.at[j], load.at[j]) for j in range(4)]
+    pulls = [pltpu.make_async_copy(grad.at[pl.ds(128 * j, 128)], g_in.at[j], load.at[4 + j]) for j in range(4)]
+    rows = [
+        pltpu.make_async_copy(
+            qkv.at[pl.ds(pl.multiple_of(256 * i + 128 * half, 128), 128)], q_in.at[i], load.at[8 + i]
+        )
+        for i in range(3)
+    ]
+    for copy in rows + parts + pulls:
+        copy.start()
+    near_barrier(s, f)
+    keep_small = pltpu.make_async_copy(packed, small_all.at[f], own_sems.at[0])
+    keep_small.start()
+
+    def send_small(step):
+        to = (f + step) % 8
+        return remote(packed, small_all.at[f], sm_s.at[step - 1], sm_r.at[step - 1], s, to)
+
+    for step in range(1, 8):
+        send_small(step).start()
+
+    def hop(i):
+        head = 3 * f + i
+        return remote(q_out.at[i], heads.at[head // 8], q_s.at[i], q_r.at[head // 8], s, head % 8)
+
+    def keep_hop(i):
+        return pltpu.make_async_copy(q_out.at[i], heads.at[(3 * f + i) // 8], own_sems.at[1])
+
+    for i in range(3):
+        rows[i].wait()
+        q_out[i] = q_in[i].astype(bf)
+        here = (3 * f + i) % 8 == f
+        pl.when(here)(keep_hop(i).start)
+        pl.when(jnp.logical_not(here))(hop(i).start)
+
+    out = PlaneOut(n_out, own_n, s, f, po_s, po_r, own_sems.at[2])
+    for j in range(4):
+        parts[j].wait()
+
+        @pl.loop(0, 4)
+        def _(i):
+            at = pl.ds(pl.multiple_of(32 * i, 32), 32)
+            value = x_in[j, at, :]
+            center = value - jnp.sum(value, axis=1, keepdims=True) * (1.0 / width)
+            spread = jnp.sum(center * center, axis=1, keepdims=True) * (1.0 / width)
+            n_out[j, at, :] = (center * lax.rsqrt(spread + EPS)).astype(bf)
+
+        out.start(j)
+    for j in range(4):
+        pulls[j].wait()
+        g_out[j] = g_in[j].astype(bf)
+    keep_g = [
+        pltpu.make_async_copy(g_out.at[j], g_low.at[pl.ds(128 * j, 128)], load.at[j]) for j in range(4)
+    ]
+    for copy in keep_g:
+        copy.start()
+    keep_small.wait()
+    for step in range(1, 8):
+        send_small(step).wait_send()
+        at = (f + 8 - step) % 8
+        remote(packed, small_all.at[at], sm_s.at[step - 1], sm_r.at[step - 1], s, at).wait_recv()
+    for kind in range(3):
+        frm = (8 * kind + f) // 3
+        ref = heads.at[kind]
+        away = remote(ref, ref, q_s.at[kind], q_r.at[kind], s, frm)
+        pl.when(frm != f)(away.wait_recv)
+    for i in range(3):
+        here = (3 * f + i) % 8 == f
+        pl.when(here)(keep_hop(i).wait)
+        pl.when(jnp.logical_not(here))(hop(i).wait_send)
+    out.wait()
+    for copy in keep_g:
+        copy.wait()
+
+
+def entry_call(resid, grad, qkv, packed):
+    width = resid.shape[1]
     anys = pl.BlockSpec(memory_space=pl.ANY)
     vmem = pl.BlockSpec(memory_space=pltpu.VMEM)
     shape = jax.ShapeDtypeStruct
     dma = lambda n: pltpu.SemaphoreType.DMA((n,))
     return pl.pallas_call(
-        forward_body,
-        in_specs=[anys] * 4 + [vmem] * 5,
-        out_specs=[anys] * 8,
+        entry_body,
+        in_specs=[anys] * 3 + [vmem],
+        out_specs=[anys] * 4,
         out_shape=[
-            shape((4, TOK, width), bf), shape((4, TOK, width), bf),
-            shape((4, TOK, units + 256), bf), shape((4, TOK, units), bf), shape((4, 3, TOK, 256), bf),
-            shape((4, TOK, LANES), f32),
-            shape((4, HALF, width), bf), shape((4, HALF, width), bf),
+            shape((HALF, width), bf), shape((HALF, width), bf), shape((3, 128, width), bf),
+            shape((8,) + packed.shape, f32),
         ],
         scratch_shapes=[
-            pltpu.VMEM(w_in.shape, bf), pltpu.VMEM(w_out.shape, bf), pltpu.VMEM((TOK, width), bf),
-            pltpu.VMEM((TOK, units), bf), pltpu.VMEM((TOK, units), bf), pltpu.VMEM((3, TOK, 256), bf),
-            pltpu.VMEM((TOK, 256), bf), pltpu.VMEM((TOK, LANES), f32),
-            pltpu.VMEM((HALF, width), bf), pltpu.VMEM((HALF, width), bf),
-            dma(5), dma(3), dma(3), dma(3), dma(3), dma(3), dma(3), dma(3), dma(3),
-            dma(4), dma(4), dma(4), dma(4), dma(6),
+            pltpu.VMEM((4, 128, width), f32), pltpu.VMEM((4, 128, width), f32), pltpu.VMEM((3, 128, width), f32),
+            pltpu.VMEM((4, 128, width), bf), pltpu.VMEM((4, 128, width), bf), pltpu.VMEM((3, 128, width), bf),
+            dma(11), dma(3), dma(3), dma(4), dma(4), dma(7), dma(7), dma(3),
         ],
         compiler_params=pltpu.CompilerParams(
-            vmem_limit_bytes=60 * 1024 * 1024, collective_id=0, has_side_effects=True
+            vmem_limit_bytes=40 * 1024 * 1024, collective_id=3, has_side_effects=True
         ),
-        cost_estimate=cost(8 * TOK * width * (w_in.shape[0] + w_out.shape[0]), 200e6),
-        name="forward",
-    )(own_n, own_g, w_in, w_out, bias, cos, sin, ids_col, ids_row)
+        cost_estimate=cost(1e7, 20e6),
+        name="entry",
+    )(resid, grad, qkv, packed)
 
 
 def sum_add(dst, parts):
@@ -984,9 +1211,9 @@
 
 
 def backward_body(
-    g_part, w_in_h, w_out_h, slope_h, qkv_h, lse_h, p_own, p_sib, cos, sin, idc, idr,
+    g_part, w_in_h, w_out_h, slope_h, qkv_h, lse_h, p_own, p_sib, gain, cos4, sin4, idc, idr,
     g_all, b_all, own_o, sib_o, branch, land, sums,
-    w_in, w_out, x, slope, qkv, lse, gh, gmix, gp, acc_k, acc_v, u_own, u_sib, stage, rs_out,
+    w_in, w_out, x, slope, qkv, lse, gh, gmix, gp, acc_k, acc_v, u_own, u_sib, stage, rs_out, cos, sin,
     load, l0, l1, l2, l3, core_0, core_1, core_u0, core_u1, out_sems, rs_send, rs_recv, pb_send, pb_recv,
 ):
     s, f = lax.axis_index("seq"), lax.axis_index("fsdp")
@@ -1030,6 +1257,7 @@
         b = line_order(z, t)
         for copy in ins(b):
             copy.start()
+        expand_tables(cos4, sin4, b, cos, sin)
         if t == 3:
             line_arrive(g_all, 2, z, s, f, line)
             new_blocks(3, z, lambda v: swap(v).start())
@@ -1072,14 +1300,14 @@
             inner = jnp.sum(probs * grad_probs, axis=1, keepdims=True)
             gs = (probs * (grad_probs - inner)).astype(bf)
             gq = (nn(gs, qkv[1]) * scale).astype(bf).astype(f32)
-            gq = turn(gq, cos[b, rows, :], -sin[b, rows, :])
+            gq = turn(gq, cos[rows, :], -sin[rows, :])
             sums[0:1, :] += jnp.sum(gq, axis=0, keepdims=True)
             gp[0, rows, :] = gq.astype(bf)
             acc_k[...] += tn(gs, q)
             acc_v[...] += tn(probs.astype(bf), g)
 
         gk = (acc_k[...] * scale).astype(bf).astype(f32)
-        gk = turn(gk, cos[b], -sin[b])
+        gk = turn(gk, cos[...], -sin[...])
         sums[1:2, :] += jnp.sum(gk, axis=0, keepdims=True)
         gp[1] = gk.astype(bf)
         gv = acc_v[...].astype(bf)
@@ -1099,9 +1327,11 @@
         @pl.loop(0, u_own.shape[1] // 256)
         def _(j):
             at = pl.ds(pl.multiple_of(j * 256, 256), 256)
-            out = nn(gh[...], w_in[pl.ds(0, units), at])
-            for i in range(3):
-                out = out + nn(gp[i], w_in[pl.ds(units + 256 * i, 256), at])
+            from_mlp = nn(gh[...], w_in[pl.ds(0, units), at])
+            from_attn = nn(gp[0], w_in[pl.ds(units, 256), at])
+            for i in range(1, 3):
+                from_attn = from_attn + nn(gp[i], w_in[pl.ds(units + 256 * i, 256), at])
+            out = from_mlp * gain[0:1, at] + from_attn * gain[1:2, at]
             u_own[:, at] = out[:HALF].astype(bf)
             u_sib[:, at] = out[HALF:].astype(bf)
 
@@ -1121,7 +1351,7 @@
     back.wait()
 
 
-def backward_call(g_part, w_in, w_out, slope, qkv, lse, p_own, p_sib, cos, sin, ids_col, ids_row):
+def backward_call(g_part, w_in, w_out, slope, qkv, lse, p_own, p_sib, gain, cos4, sin4, ids_col, ids_row):
     width = w_in.shape[1]
     units = w_in.shape[0] - 768
     anys = pl.BlockSpec(memory_space=pl.ANY)
@@ -1130,7 +1360,7 @@
     dma = lambda *n: pltpu.SemaphoreType.DMA(n)
     return pl.pallas_call(
         backward_body,
-        in_specs=[anys] * 8 + [vmem] * 4,
+        in_specs=[anys] * 8 + [vmem] * 5,
         out_specs=[anys] * 6 + [vmem],
         out_shape=[
             shape((4, TOK, width), bf), shape((4, TOK, units + 768), bf),
@@ -1145,6 +1375,7 @@
             pltpu.VMEM((TOK, 256), f32), pltpu.VMEM((TOK, 256), f32),
             pltpu.VMEM((HALF, width), bf), pltpu.VMEM((HALF, width), bf),
             pltpu.VMEM((3, HALF, width), bf), pltpu.VMEM((2, HALF, width), bf),
+            pltpu.VMEM((TOK, LANES), f32), pltpu.VMEM((TOK, LANES), f32),
             dma(11), dma(3), dma(3), dma(3), dma(3), dma(4), dma(4), dma(4), dma(4), dma(5),
             dma(2, 3), dma(2, 3), dma(4), dma(4),
         ],
@@ -1153,7 +1384,7 @@
         ),
         cost_estimate=cost(8 * TOK * width * (w_in.shape[0] + w_out.shape[0]), 200e6),
         name="backward",
-    )(g_part, w_in, w_out, slope, qkv, lse, p_own, p_sib, cos, sin, ids_col, ids_row)
+    )(g_part, w_in, w_out, slope, qkv, lse, p_own, p_sib, gain, cos4, sin4, ids_col, ids_row)
 
 
 PAIRS = 12
@@ -1161,7 +1392,7 @@
 
 def tail_body(
     a_all, b_all, g_all, n_all, plain, u_own, u_sib, gain, shift, wide_in, more_in,
-    fin_up, fin_out, fin_qkv, u_o, small_o, land,
+    fin_up, fin_down, fin_out, fin_qkv, u_o, small_o, land,
     term, r1, r2, hop, stage, rs_out, left, right, acc, acc_s, weight, sides, wide, more, got, small,
     load, w_sem, r1_s, r1_r, r2_s, r2_r, hop_s, hop_r, r3_s, r3_r, r4_s, r4_r,
     rs_load, rs_send, rs_recv, pb_s, pb_r, sm_s, sm_r, sq_s, sq_r, own_sems, self_sem,
@@ -1261,8 +1492,10 @@
     def result(i, start, count):
         if i < 4:
             return fin_up.at[rows(256 * i + start, count)]
+        if i < 8:
+            return fin_down.at[rows(256 * (i - 4) + start, count)]
         if i < 9:
-            return fin_out.at[rows(256 * (i - 4) + start, count)]
+            return fin_out.at[rows(start, count)]
         return fin_qkv.at[rows(256 * (i - 9) + start, count)]
 
     def send1(j, p, a):
@@ -1443,9 +1676,9 @@
     return pl.pallas_call(
         tail_body,
         in_specs=[anys] * 7 + [vmem] * 4,
-        out_specs=[anys] * 4 + [vmem, anys],
+        out_specs=[anys] * 5 + [vmem, anys],
         out_shape=[
-            shape((1024, width), bf), shape((1280, width), bf), shape((768, width), bf),
+            shape((1024, width), bf), shape((1024, width), bf), shape((256, width), bf), shape((768, width), bf),
             shape((HALF, width), bf), shape((32, LANES), f32), shape((2, 3, HALF, width), bf),
         ],
         scratch_shapes=[
@@ -1470,112 +1703,6 @@
 
 def pick(slices, which):
     return lax.dynamic_index_in_dim(slices, which, 0, keepdims=False)
-
-
-def swap_core(value):
-    return lax.ppermute(value, "fsdp", [(i, i ^ 1) for i in range(8)])
-
-
-def along_z(value, pairs):
-    return lax.ppermute(value, "fsdp", [(2 * a + c, 2 * b + c) for a, b in pairs for c in range(2)])
-
-
-def spread_pairs(step):
-    pairs = []
-    for source in range(4):
-        part = (step + source) % 4
-        for rank in range(8):
-            pairs.append((source * 8 + rank, (2 * (rank % 2) + part // 2) * 8 + rank - rank % 2 + part % 2))
-    return pairs
-
-
-def gather_z(own, z):
-    low_half = z < 2
-    edge = (z == 0) | (z == 3)
-    above = along_z(own, [(1, 0), (2, 1), (3, 2)])
-    below = along_z(own, [(0, 1), (1, 2), (2, 3)])
-    first = jnp.where(low_half, above, below)
-    outer = jnp.where(low_half, below, above)
-    inner = along_z(first, [(1, 0), (2, 3)])
-    cross = along_z(outer, [(1, 2), (2, 1)])
-    second = jnp.where(edge, inner, outer)
-    third = jnp.where(edge, along_z(cross, [(1, 0), (2, 3)]), cross)
-    return [own, first, second, third]
-
-
-def scatter_z(parts, z):
-    low = jnp.bfloat16
-    low_half = z < 2
-    far = along_z(parts[3].astype(low), [(0, 1), (3, 2)])
-    cross = along_z((parts[3] + far.astype(jnp.float32)).astype(low), [(1, 2), (2, 1)])
-    near = along_z(parts[2].astype(low), [(0, 1), (3, 2)])
-    one = parts[1] + near.astype(jnp.float32)
-    two = parts[2] + cross.astype(jnp.float32)
-    up = jnp.where(low_half, one, two).astype(low)
-    down = jnp.where(low_half, two, one).astype(low)
-    from_below = along_z(up, [(0, 1), (1, 2), (2, 3)])
-    from_above = along_z(down, [(1, 0), (2, 1), (3, 2)])
-    return parts[0] + from_below.astype(jnp.float32) + from_above.astype(jnp.float32)
-
-
-def swap_seq(value, bit):
-    return lax.ppermute(value, "seq", [(i, i ^ bit) for i in range(4)])
-
-
-def gather_small(value, f):
-    gathered = value[None]
-    for bit in (1, 2, 4):
-        other = lax.ppermute(gathered, "fsdp", [(i, i ^ bit) for i in range(8)])
-        low_side = (f // bit) % 2 == 0
-        gathered = jnp.concatenate(
-            [jnp.where(low_side, gathered, other), jnp.where(low_side, other, gathered)]
-        )
-    return gathered
-
-
-def scatter_small(value, f):
-    for bit in (4, 2, 1):
-        half = value.shape[0] // 2
-        low_side = (f // bit) % 2 == 0
-        sent = jnp.where(low_side, value[half:], value[:half])
-        kept = jnp.where(low_side, value[:half], value[half:])
-        value = kept + lax.ppermute(sent, "fsdp", [(i, i ^ bit) for i in range(8)])
-    return value[0]
-
-
-def sum_small(value):
-    for bit in (1, 2):
-        value = value + swap_seq(value, bit)
-    return value
-
-
-def after(value, other):
-    return lax.optimization_barrier((value, other))[0]
-
-
-def sum_seq(part, x, y):
-    rows, columns = part.shape
-    halves = part.reshape(2, 2, 2, rows // 8, columns)
-    low = jnp.bfloat16
-    outs = []
-    for half, (bit_a, at_a), (bit_b, at_b) in ((0, (1, x), (2, y)), (1, (2, y), (1, x))):
-        mine = halves[half]
-        sent = swap_seq(pick(mine, 1 - at_a).astype(low), bit_a)
-        kept = pick(mine, at_a) + sent.astype(jnp.float32)
-        sent = swap_seq(pick(kept, 1 - at_b).astype(low), bit_b)
-        outs.append((pick(kept, at_b) + sent.astype(jnp.float32)).astype(low))
-    return outs
-
-
-def spread_seq(pieces, x, y):
-    outs = []
-    for piece, (bit_a, at_a), (bit_b, at_b) in ((pieces[0], (1, x), (2, y)), (pieces[1], (2, y), (1, x))):
-        other = swap_seq(piece, bit_b)
-        both = jnp.where(at_b == 0, jnp.stack([piece, other]), jnp.stack([other, piece]))
-        other = swap_seq(both, bit_a)
-        outs.append(jnp.where(at_a == 0, jnp.stack([both, other]), jnp.stack([other, both])))
-    rows, columns = pieces[0].shape
-    return jnp.stack(outs).reshape(8 * rows, columns).astype(jnp.float32)
 
 
 def split_body(
@@ -1603,8 +1730,6 @@
     s = lax.axis_index("seq")
     f = lax.axis_index("fsdp")
     z, c = f // 2, f % 2
-    x, y = s % 2, s // 2
-    both_axes = ("seq", "fsdp")
     units = up_weight.shape[0]
 
     length = block_ids.shape[1]
@@ -1612,75 +1737,23 @@
     packed = jnp.concatenate(
         own_small + [block_ids.reshape(-1).astype(f32), offsets.reshape(-1).astype(f32)]
     )
+    packed = jnp.pad(packed, (0, 40 * LANES - packed.shape[0])).reshape(40, LANES)
     flat = resid_in.reshape(tokens, width)
-    center = flat - jnp.mean(flat, axis=-1, keepdims=True)
-    inv = lax.rsqrt(jnp.mean(center * center, axis=-1, keepdims=True) + EPS)
-    normal = center * inv
     grad_flat = grad_out.reshape(tokens, width)
-    small = gather_small(packed, f)
+    own_n, g_low, head_half, small = entry_call(flat, grad_flat, qkv_weight, packed)
+    small = small.reshape(8, 40 * LANES)
     gain_a, shift_a, gain_m, shift_m, bias_out = (
         small[:, i * 256 : (i + 1) * 256].reshape(width) for i in range(5)
     )
     head_bias = small[:, 1280:2048].reshape(3, HEADS, HEAD_DIM)
     head_bias = lax.dynamic_index_in_dim(head_bias, f, 1, keepdims=False).reshape(3 * HEAD_DIM)
-    ids_all = small[:, 2048 : 2048 + groups * length].astype(jnp.int32).reshape(-1, 8, LANES)
-    starts_all = small[:, 2048 + groups * length :].astype(jnp.int32).reshape(-1, offsets.shape[1])
-
-    def plane_out(value):
-        parts = value.reshape(4, tokens // 4, width)
-        got = [
-            lax.ppermute(pick(parts, (k + s) % 4), both_axes, spread_pairs(k)) for k in range(4)
-        ]
-        return jnp.concatenate(got, axis=0)
-
-    def plane_back(value):
-        parts = value.reshape(4, tokens // 4, width)
-        got = jnp.stack(
-            [
-                lax.ppermute(parts[k], both_axes, [(b, a) for a, b in spread_pairs(k)])
-                for k in range(4)
-            ]
-        )
-        return jnp.concatenate([pick(got, (j - s + 4) % 4) for j in range(4)], axis=0)
-
-    own_n = plane_out(normal.astype(low))
-    own_g = plane_out(after(grad_flat.astype(low), own_n))
-
-    quarter = HEAD_DIM // 4
-    qkv_low = lax.dynamic_slice_in_dim(
-        qkv_weight.reshape(3, HEAD_DIM, width), s * quarter, quarter, 1
-    ).astype(low)
-    came = jnp.stack(
-        [
-            lax.ppermute(qkv_low[i], "fsdp", [(r, (3 * r + i) % 8) for r in range(8)])
-            for i in range(3)
-        ]
-    )
-
-    def third_of(i):
-        return (3 * ((3 * (f - i + 8)) % 8) + i) // 8
-
-    slot_of = [
-        sum(jnp.where(third_of(i) == kind, i, 0) for i in range(3)) for kind in range(3)
-    ]
-    came = jnp.stack([pick(came, slot_of[kind]) for kind in range(3)])
-    got = jnp.stack([came] + [swap_seq(came, bit) for bit in (1, 2, 3)])
-    head_w = jnp.stack([pick(got, s ^ q) for q in range(4)], axis=1).reshape(3 * HEAD_DIM, width)
+    ids_end = 2048 + groups * length
+    ids_all = small[:, 2048:ids_end].astype(jnp.int32).reshape(-1, 8, LANES)
+    starts_all = small[:, ids_end : ids_end + groups * offsets.shape[1]].astype(jnp.int32)
+    starts_all = starts_all.reshape(-1, offsets.shape[1])
     gain = jnp.stack([gain_m, gain_a])
     shift = jnp.stack([shift_m, shift_a])
-    up_low = up_weight.astype(low).astype(f32)
-    head32 = head_w.astype(f32)
-    plain_w = jnp.concatenate([up_low, head32], axis=0).astype(low)
-    w_up = (up_low * gain_m).astype(low)
-    w_head = (head32 * gain_a).astype(low)
-    w_in = jnp.concatenate([w_up, w_head], axis=0)
-    bias_in = jnp.concatenate(
-        [
-            up_bias + jnp.sum(up_low * shift_m, axis=1),
-            head_bias + jnp.sum(head32 * shift_a, axis=1),
-        ]
-    )[None]
-    w_out = jnp.concatenate([down_weight.astype(low), out_weight.astype(low)], axis=0)
+    bias_in = jnp.concatenate([up_bias, head_bias])[None]
 
     halves = [(2 * (s % 2) + c, c), (2 * (s % 2) + 1 - c, 1 - c)]
     rows_at = [((part - k + 4) % 4) * 2 + core for part, core in halves for k in range(4)]
@@ -1692,19 +1765,19 @@
     pos = (jnp.stack(rows_at)[:, None] * LANES + jnp.arange(LANES)[None, :]).reshape(1024)
     positions = block_offset(ids_here, starts_here) + pos[None, :]
     lane = jnp.arange(LANES)
-    inverse = jnp.exp(
-        (lane % 32).astype(f32) * (-2.0 * math.log(10000.0) / ROT_DIM)
-    )
-    angles = jnp.where(lane < ROT_DIM, positions.astype(f32)[..., None] * inverse, 0.0)
-    cosine = jnp.cos(angles)
-    sine = jnp.sin(angles) * jnp.where(lane < ROT_DIM // 2, -1.0, 1.0)
+    inverse = jnp.exp((lane % 32).astype(f32) * (-2.0 * math.log(10000.0) / ROT_DIM))
+    grouped = positions.astype(f32).reshape(4, 4, 256, 1)
+    spot = sum(jnp.where(lane // 32 == q, grouped[:, q], 0.0) for q in range(4))
+    angles = spot * inverse
+    cosine, sine = jnp.cos(angles), jnp.sin(angles)
     ids_col, ids_row = ids_here[:, :, None], ids_here[:, None, :]
 
-    n_all, g_part, a_all, slope_all, qkv_all, lse_all, p_own, p_sib = forward_call(
-        own_n, own_g, w_in, w_out, bias_in, cosine, sine, ids_col, ids_row
+    n_all, g_part, w_in, w_out, a_all, slope_all, qkv_all, lse_all, p_own, p_sib = forward_call(
+        own_n, g_low, head_half, up_weight, down_weight, out_weight, bias_in, gain, shift,
+        cosine, sine, ids_col, ids_row,
     )
     g_all, b_all, u_own, u_sib, branch, _, col_sums = backward_call(
-        g_part, w_in, w_out, slope_all, qkv_all, lse_all, p_own, p_sib, cosine, sine, ids_col, ids_row
+        g_part, w_in, w_out, slope_all, qkv_all, lse_all, p_own, p_sib, gain, cosine, sine, ids_col, ids_row
     )
     result = flat + branch.astype(f32) + bias_out
 
@@ -1717,10 +1790,13 @@
     )
     wide = jnp.pad(wide, ((0, 0), (0, 256))).reshape(8, 16, LANES)
     more = jnp.pad(jnp.concatenate([jnp.zeros((units,), f32), col_sums[2]]), (0, 768)).reshape(16, LANES)
-    up_low, out_low, qkv_low, u, small_sum, _ = tail_call(
-        a_all, b_all, g_all, n_all, plain_w, u_own, u_sib, gain, shift, wide, more
+    up_low, down_low, out_low, qkv_low, u, small_sum, _ = tail_call(
+        a_all, b_all, g_all, n_all, w_in, u_own, u_sib, gain, shift, wide, more
     )
     u = u.astype(f32)
+    center = flat - jnp.mean(flat, axis=-1, keepdims=True)
+    inv = lax.rsqrt(jnp.mean(center * center, axis=-1, keepdims=True) + EPS)
+    normal = center * inv
     grad_input = grad_flat + inv * (
         u - jnp.mean(u, axis=-1, keepdims=True) - normal * jnp.mean(u * normal, axis=-1, keepdims=True)
     )
@@ -1735,11 +1811,11 @@
         qkv_low.astype(f32),
         qk_grad,
         value_grad,
-        out_low[units:].astype(f32),
+        out_low.astype(f32),
         vectors[4],
         up_low.astype(f32),
         up_bias_grad,
-        out_low[:units].astype(f32),
+        down_low.astype(f32),
         vectors[4],
         vectors[2],
         vectors[3],

time: 842 us -> 734 us (0.87)
  waiting for transfers between devices: 51.9 us -> 0 us
  other arithmetic: 85.9 us -> 34.7 us
  starting transfers between devices: 35 us -> 0 us
  Pallas kernels: 636 us -> 665 us
    ppermute x17 -> x0, waiting for transfers between devices: 51.9 us -> none  [the longest x8 21.6 us: plane_out(): lax.ppermute(pick(parts, (k + s) % 4), both_axes, spread_pairs(k))]
    ppermute x17 -> x0, starting transfers between devices: 35 us -> none  [the longest x8 21.2 us: plane_out(): lax.ppermute(pick(parts, (k + s) % 4), both_axes, spread_pairs(k))]
    pallas_call x2 -> x3, Pallas kernels: 369 us -> 398 us  [the longest x1 192 us: forward_call(): pl.pallas_call(forward_body, in_specs=[anys] * 6 + [vmem] * 7, out_specs=...]
    concatenate x7 -> x1, other arithmetic: 21.3 us -> 0.01 us  [split_body(): bias_in = jnp.concatenate([up_bias, head_bias])[None]]
    convert_element_type x10 -> x5, other arithmetic: 22.9 us -> 6.03 us  [the longest x1 4.45 us: split_body(): down_low.astype(f32)]
    mul x1 -> x0, other arithmetic: 8.89 us -> none  [split_body(): sine = jnp.sin(angles) * jnp.where(lane < ROT_DIM // 2, -1.0, 1.0)]
  transfers between devices with their start and end apart: 17 -> 0, of which waited for: 7 -> 0; matrix products, arithmetic and copies ran while one was open for 7% -> 0% of each run, Pallas kernels for 0% -> 0%
where the time goes in v4:
time: 734 us; the launch traced here: 724 us
  Pallas kernels  665 us (91%)
  other arithmetic  34.7 us (5%)
  local copies, waits for them, and re-layouts  22 us (3%)
    pallas_call x1, Pallas kernels, tail_call(): pl.pallas_call(tail_body, in_specs=[anys] * 7 + [vmem] * 4, out_specs=[an...  268 us
    pallas_call x1, Pallas kernels, forward_call(): pl.pallas_call(forward_body, in_specs=[anys] * 6 + [vmem] * 7, out_specs=...  192 us
    pallas_call x1, Pallas kernels, backward_call(): pl.pallas_call(backward_body, in_specs=[anys] * 8 + [vmem] * 5, out_specs...  174 us
    pallas_call x1, Pallas kernels, entry_call(): pl.pallas_call(entry_body, in_specs=[anys] * 3 + [vmem], out_specs=[anys]...  31.9 us
    unnamed x60, local copies, waits for them, and re-layouts  15 us

profile of v4, /device:TPU:0, one launch (start us, length us, event | category | flops | bytes accessed | tf_op | source)
XLA Modules:
  0.0 723.9 jit_solution(18297415292243012469)
XLA Ops:
  3.6 0.7 constant_dynamic-update-slice_fusion.38
  4.3 0.7 constant_dynamic-update-slice_fusion.37
  5.0 0.7 convert_bitcast_fusion
  6.5 2.2 copy-done
  8.7 2.2 copy-done.2
  10.9 31.9 %entry.1 = (bf16[512,2048]{1,0:T(8,128)(2,1)S(1)}, bf16[512,2048]{1,0:T(8,128)(2,1)S(1)}, bf16[3,128,2048]{2,1,0:T(8,128)(2,1)S(1)}, f32[8,40,128]{2,1,0:T(8,128)S(1)}) custom-call(f32[512,2048]{1,0:T(8,128)S(1)} %bitcast.230, f32[512,2048]{1,0:T(8,128)S(1)} %bitcast.231, f32[768,2048]{1,0:T(8,128)} %qkv.1, f32[40,128]{1,0:T(8,128)S(1)} %pad_bitcast_fusion.packed), custom_call_target="tpu_custom_call" | custom-call | flops 10000000 | bytes 20000000 | tf_op jit(solution)/shard_map/entry/pallas_call | solution.py:1107
  42.7 1.3 copy-done.4
  44.0 1.3 copy-done.5
  45.4 1.1 copy-done.6
  46.9 2.0 copy.37.idc
  49.4 3.4 fusion.4
  55.4 191.7 %forward.1 = (bf16[4,1024,2048]{2,1,0:T(8,128)(2,1)}, bf16[4,1024,2048]{2,1,0:T(8,128)(2,1)}, bf16[1792,2048]{1,0:T(8,128)(2,1)}, bf16[1280,2048]{1,0:T(8,128)(2...) custom-call(bf16[512,2048]{1,0:T(8,128)(2,1)} %copy-done.4, ...), custom_call_target="tpu_custom_call" | custom-call | flops 51539607552 | bytes 200000000 | tf_op jit(solution)/shard_map/forward/pallas_call | solution.py:989
  247.1 174.2 %backward.1 = (bf16[4,1024,2048]{2,1,0:T(8,128)(2,1)}, bf16[4,1024,1792]{2,1,0:T(8,128)(2,1)}, bf16[4,512,2048]{2,1,0:T(8,128)(2,1)}, bf16[4,512,2048]{2,1,0:T(8...) custom-call(bf16[4,1024,2048]{2,1,0:T(8,128)(2,1)} %get-tuple-elemen, ...), custom_call_target="tpu_custom_call", output_to_operand_aliasing={{0}: (0, {})} | custom-call | flops 51539607552 | bytes 200000000 | tf_op jit(solution)/shard_map/backward/pallas_call | solution.py:1361
  421.3 0.8 fusion.45
  422.4 2.4 reduce_sum.60
  426.1 267.7 %tail.1 = (bf16[1024,2048]{1,0:T(8,128)(2,1)}, bf16[1024,2048]{1,0:T(8,128)(2,1)}, bf16[256,2048]{1,0:T(8,128)(2,1)}, bf16[768,2048]{1,0:T(8,128)(2,1)}, bf16[51...) custom-call(bf16[4,1024,1280]{2,1,0:T(8,128)(2,1)} %get-tuple-element.54.a_all, ...), custom_call_target="tpu_custom_call" | custom-call | flops 99999997952 | bytes 600000000 | tf_op jit(solution)/shard_map/tail/pallas_call | solution.py:1676
  693.8 2.6 reduce_sum.58
  696.4 2.9 multiply_reduce_fusion
  699.9 1.6 convert_reduce_fusion
  702.3 4.9 fusion.2
  707.2 4.4 convert_element_type.72
  711.6 4.4 convert_element_type.73
  716.1 3.5 convert_element_type.70
  719.6 1.6 convert_element_type.71
  (105 shorter events, 12.0 us)
Async XLA Ops:
  6.5 2.2 copy-start
  8.7 2.2 copy-start.2
  42.7 1.3 copy-start.4
  44.0 1.3 copy-start.5
  45.4 1.1 copy-start.6
  46.5 8.2 %copy-start.16 = (f32[1024]{0:T(1024)S(1)}, f32[1024]{0:T(1024)}, u32[]{:S(2)}) copy-start(f32[1024]{0:T(1024)} %param.22) | copy-start | bytes 12292
  693.8 5.6 copy-start.7
  696.4 3.5 copy-start.1
  699.3 2.2 copy-start.13
  699.3 2.3 copy-start.3
  699.3 2.9 copy-start.11
  702.3 4.9 copy-start.9
  707.2 4.4 copy-start.8
  711.6 4.5 copy-start.10
  716.1 3.6 copy-start.12
  716.1 5.1 copy-start.14
  721.8 1.7 copy-start.15

commit v5 on v4

--- a/solution.py
+++ b/solution.py
@@ -1016,7 +1016,7 @@
 
 
 def entry_body(
-    resid, grad, qkv, packed, own_n, g_low, heads, small_all,
+    resid, grad, qkv, packed, own_n, g_low, heads, small_all, bias_sum,
     x_in, g_in, q_in, n_out, g_out, q_out,
     load, q_s, q_r, po_s, po_r, sm_s, sm_r, own_sems,
 ):
@@ -1066,14 +1066,18 @@
         def _(i):
             at = pl.ds(pl.multiple_of(32 * i, 32), 32)
             value = x_in[j, at, :]
-            center = value - jnp.sum(value, axis=1, keepdims=True) * (1.0 / width)
+            mean = jnp.sum(value, axis=1, keepdims=True) * (1.0 / width)
+            center = value - mean
             spread = jnp.sum(center * center, axis=1, keepdims=True) * (1.0 / width)
-            n_out[j, at, :] = (center * lax.rsqrt(spread + EPS)).astype(bf)
+            inv = lax.rsqrt(spread + EPS)
+            n_out[j, at, :] = (center * inv).astype(bf)
 
         out.start(j)
     for j in range(4):
         pulls[j].wait()
         g_out[j] = g_in[j].astype(bf)
+        part = jnp.sum(g_in[j], axis=0, keepdims=True)
+        bias_sum[...] = part if j == 0 else bias_sum[...] + part
     keep_g = [
         pltpu.make_async_copy(g_out.at[j], g_low.at[pl.ds(128 * j, 128)], load.at[j]) for j in range(4)
     ]
@@ -1107,10 +1111,10 @@
     return pl.pallas_call(
         entry_body,
         in_specs=[anys] * 3 + [vmem],
-        out_specs=[anys] * 4,
+        out_specs=[anys] * 4 + [vmem],
         out_shape=[
             shape((HALF, width), bf), shape((HALF, width), bf), shape((3, 128, width), bf),
-            shape((8,) + packed.shape, f32),
+            shape((8,) + packed.shape, f32), shape((1, width), f32),
         ],
         scratch_shapes=[
             pltpu.VMEM((4, 128, width), f32), pltpu.VMEM((4, 128, width), f32), pltpu.VMEM((3, 128, width), f32),
@@ -1118,11 +1122,89 @@
             dma(11), dma(3), dma(3), dma(4), dma(4), dma(7), dma(7), dma(3),
         ],
         compiler_params=pltpu.CompilerParams(
-            vmem_limit_bytes=40 * 1024 * 1024, collective_id=3, has_side_effects=True
+            vmem_limit_bytes=60 * 1024 * 1024, collective_id=3, has_side_effects=True
         ),
         cost_estimate=cost(1e7, 20e6),
         name="entry",
     )(resid, grad, qkv, packed)
+
+
+class SeqSum:
+    def __init__(self, term, r1, r2, sems, own_sems, result, s, f):
+        self.term, self.r1, self.r2, self.own_sems, self.result, self.f = term, r1, r2, own_sems, result, f
+        self.sems = sems
+        x, y = s % 2, s // 2
+        self.across = (s + 1 - 2 * x, (s + 2) % 4)
+        self.ways = ((0, x, y), (1, y, x))
+
+    @staticmethod
+    def rows(start, count):
+        return pl.ds(pl.multiple_of(start, 32), count)
+
+    @staticmethod
+    def base(p, a, b):
+        return 128 * p + 64 * a + 32 * b
+
+    def copy(self, step, src, dst, j, p):
+        to = self.across[p if step in (1, 4) else 1 - p]
+        send, recv = self.sems[2 * step - 2 : 2 * step]
+        return remote(src, dst, send.at[j, p], recv.at[j, p], to, self.f)
+
+    def send1(self, j, p, a):
+        return self.copy(1, self.term.at[j, self.rows(128 * p + 64 * (1 - a), 64)], self.r1.at[j, p], j, p)
+
+    def send2(self, j, p, a, b):
+        return self.copy(2, self.term.at[j, self.rows(self.base(p, a, 1 - b), 32)], self.r2.at[j, p], j, p)
+
+    def keep3(self, j, p, a, b):
+        at = self.base(p, a, b)
+        return pltpu.make_async_copy(self.term.at[j, self.rows(at, 32)], self.result(j, at, 32), self.own_sems.at[j, p])
+
+    def send3(self, j, p, a, b, held=True):
+        at = self.base(p, a, b)
+        ref = self.result(j, at, 32)
+        return self.copy(3, self.term.at[j, self.rows(at, 32)] if held else ref, ref, j, p)
+
+    def send4(self, j, p, a):
+        ref = self.result(j, 128 * p + 64 * a, 64)
+        return self.copy(4, ref, ref, j, p)
+
+    def step1(self, j):
+        for p, a, b in self.ways:
+            self.send1(j, p, a).start()
+
+    def step2(self, j):
+        for p, a, b in self.ways:
+            self.send1(j, p, a).wait_recv()
+            at = self.rows(128 * p + 64 * a, 64)
+            self.term[j, at, :] = (self.term[j, at, :].astype(f32) + self.r1[j, p].astype(f32)).astype(bf)
+            self.send2(j, p, a, b).start()
+
+    def total(self, j, p, a, b):
+        self.send2(j, p, a, b).wait_recv()
+        at = self.rows(self.base(p, a, b), 32)
+        return (self.term[j, at, :].astype(f32) + self.r2[j, p].astype(f32)).astype(bf)
+
+    def step3(self, j):
+        for p, a, b in self.ways:
+            self.term[j, self.rows(self.base(p, a, b), 32), :] = self.total(j, p, a, b)
+            self.send3(j, p, a, b).start()
+            self.keep3(j, p, a, b).start()
+
+    def step4(self, j, held=True):
+        for p, a, b in self.ways:
+            self.send3(j, p, a, b, held).wait_recv()
+            if held:
+                self.keep3(j, p, a, b).wait()
+            self.send4(j, p, a).start()
+
+    def finish(self, j):
+        for p, a, b in self.ways:
+            self.send4(j, p, a).wait_recv()
+            self.send1(j, p, a).wait_send()
+            self.send2(j, p, a, b).wait_send()
+            self.send3(j, p, a, b).wait_send()
+            self.send4(j, p, a).wait_send()
 
 
 def sum_add(dst, parts):
@@ -1135,7 +1217,7 @@
         dst[rows, :] = total.astype(bf)
 
 
-def line_sum_step(k, z, s, f, own, sib, land, stage, out, loads, sends, recvs):
+def line_sum_step(k, z, s, f, own, sib, land, stage, out, loads, sends, recvs, early=None):
     for way in range(2):
         d = z - 3 + k if way == 0 else z + 3 - k
         valid = d >= 0 if way == 0 else d <= 3
@@ -1151,7 +1233,15 @@
             ]
             for copy in terms:
                 copy.start()
-            if k > 0:
+            if k == 1 and early is not None:
+
+                @pl.when(inner)
+                def _():
+                    came = pltpu.make_async_copy(early.at[way], stage.at[2], loads.at[2])
+                    came.start()
+                    came.wait()
+
+            elif k > 0:
 
                 @pl.when(was)
                 def _():
@@ -1207,14 +1297,15 @@
             came.wait()
             sum_add(stage.at[0], [stage.at[0], stage.at[2]])
 
-    sum_add(stage.at[0], [stage.at[0], stage.at[1]])
+    sum_add(stage.at[2], [stage.at[0], stage.at[1]])
 
 
 def backward_body(
-    g_part, w_in_h, w_out_h, slope_h, qkv_h, lse_h, p_own, p_sib, gain, cos4, sin4, idc, idr,
-    g_all, b_all, own_o, sib_o, branch, land, sums,
-    w_in, w_out, x, slope, qkv, lse, gh, gmix, gp, acc_k, acc_v, u_own, u_sib, stage, rs_out, cos, sin,
+    g_part, a_all, w_in_h, w_out_h, slope_h, qkv_h, lse_h, p_own, p_sib, gain, cos4, sin4, idc, idr,
+    g_all, b_all, own_o, sib_o, branch, land, land_u, fin_down, fin_out, sums,
+    w_in, w_out, x, slope, qkv, lse, gh, gmix, gp, acc_k, acc_v, u_own, u_sib, stage, rs_out, cos, sin, term, r1, r2, left, acc,
     load, l0, l1, l2, l3, core_0, core_1, core_u0, core_u1, out_sems, rs_send, rs_recv, pb_send, pb_recv,
+    t_load, r1_s, r1_r, r2_s, r2_r, r3_s, r3_r, r4_s, r4_r, own_sems, u_send, u_recv,
 ):
     s, f = lax.axis_index("seq"), lax.axis_index("fsdp")
     z = f // 2
@@ -1237,13 +1328,11 @@
     reduce_args = (z, s, f, p_own, p_sib, land, stage, rs_out, load.at[pl.ds(8, 3)], rs_send, rs_recv)
     line_sum_step(0, *reduce_args)
     sums[...] = jnp.zeros_like(sums)
-    back = PlaneBack(stage.at[0], branch, s, f, pb_send, pb_recv, load.at[7])
-
-    def ins(b):
-        return [
-            pltpu.make_async_copy(src.at[b], dst, load.at[2 + i])
-            for i, (src, dst) in enumerate([(slope_h, slope), (qkv_h, qkv), (lse_h, lse)])
-        ]
+    back = PlaneBack(stage.at[2], branch, s, f, pb_send, pb_recv, load.at[7])
+
+    def ins(b, which=(0, 1, 2)):
+        pairs = [(slope_h, slope), (qkv_h, qkv), (lse_h, lse)]
+        return [pltpu.make_async_copy(pairs[i][0].at[b], pairs[i][1], load.at[2 + i]) for i in which]
 
     def outs(b):
         pairs = [(gh, b_all.at[b, :, pl.ds(0, units)]), (u_own, own_o.at[b])]
@@ -1253,31 +1342,93 @@
     def send_sib(b):
         return remote(u_sib, sib_o.at[b], core_u0.at[b], core_u1.at[b], s, f + 1 - 2 * (f % 2))
 
+    def result(j, start, count):
+        if j < 4:
+            return fin_down.at[SeqSum.rows(256 * j + start, count)]
+        return fin_out.at[SeqSum.rows(start, count)]
+
+    row_sums = SeqSum(
+        term, r1, r2, (r1_s, r1_r, r2_s, r2_r, r3_s, r3_r, r4_s, r4_r), own_sems, result, s, f
+    )
+
+    def term_loads(j, k):
+        slot = (8 * j + k) % 3
+        at = pl.ds(pl.multiple_of(HALF * (k % 2), HALF), HALF)
+        return (
+            pltpu.make_async_copy(a_all.at[k // 2, at, pl.ds(256 * j, 256)], left.at[slot], t_load.at[slot, 0]),
+            pltpu.make_async_copy(g_all.at[k // 2, at], stage.at[slot], t_load.at[slot, 1]),
+        )
+
+    def compute_term(j):
+        @pl.loop(0, 8)
+        def _(k):
+            @pl.when(k < 6)
+            def _():
+                for copy in term_loads(j, k + 2):
+                    copy.start()
+
+            if j < 4:
+
+                @pl.when(k >= 6)
+                def _():
+                    for copy in term_loads(j + 1, k - 6):
+                        copy.start()
+
+            for copy in term_loads(j, k):
+                copy.wait()
+            slot = (8 * j + k) % 3
+            part = tn(left[slot], stage[slot])
+
+            @pl.when(k == 0)
+            def _():
+                acc[...] = part
+
+            @pl.when((k > 0) & (k < 7))
+            def _():
+                acc[...] += part
+
+            @pl.when(k == 7)
+            def _():
+                term[j] = (acc[...] + part).astype(bf)
+
+    def load_x(b):
+        return [
+            pltpu.make_async_copy(g_all.at[b, own], x.at[own], load.at[5]),
+            pltpu.make_async_copy(g_all.at[b, other], x.at[other], load.at[6]),
+        ]
+
+    for copy in ins(z):
+        copy.start()
+    swap(z).wait_recv()
+    for copy in load_x(z):
+        copy.start()
+    for copy in first:
+        copy.wait()
+
     for t in range(4):
         b = line_order(z, t)
-        for copy in ins(b):
-            copy.start()
         expand_tables(cos4, sin4, b, cos, sin)
         if t == 3:
             line_arrive(g_all, 2, z, s, f, line)
             new_blocks(3, z, lambda v: swap(v).start())
-        top = pltpu.make_async_copy(g_all.at[b, own], x.at[own], load.at[5])
-        top.start()
-        swap(b).wait_recv()
-        low_half = pltpu.make_async_copy(g_all.at[b, other], x.at[other], load.at[6])
-        low_half.start()
-        if t == 0:
-            for copy in first:
-                copy.wait()
-        else:
+            line_sum_step(2, *reduce_args)
+            swap(b).wait_recv()
+            for copy in term_loads(0, 0) + term_loads(0, 1) + tuple(load_x(b)):
+                copy.start()
+            for j in range(5):
+                compute_term(j)
+                row_sums.step1(j)
+                if j >= 2:
+                    row_sums.step2(j - 2)
+                if j >= 3:
+                    row_sums.step3(j - 3)
+        if t > 0:
             before = line_order(z, t - 1)
             for copy in outs(before):
                 copy.wait()
             send_sib(before).wait_send()
-        for copy in ins(b):
+        for copy in ins(b) + load_x(b):
             copy.wait()
-        top.wait()
-        low_half.wait()
 
         @pl.loop(0, units // 256)
         def _(j):
@@ -1286,6 +1437,13 @@
             gh[:, at] = (ga.astype(f32) * slope[:, at].astype(f32)).astype(bf)
 
         gmix[...] = nt(x[...], w_out[pl.ds(units, 256), :]).astype(bf)
+        after = line_order(z, t + 1)
+        if t < 3:
+            ins(after, (0,))[0].start()
+        else:
+            row_sums.step2(3)
+            row_sums.step3(2)
+            row_sums.step4(0)
         acc_k[...] = jnp.zeros_like(acc_k)
         acc_v[...] = jnp.zeros_like(acc_v)
 
@@ -1313,14 +1471,23 @@
         gv = acc_v[...].astype(bf)
         sums[2:3, :] += jnp.sum(gv.astype(f32), axis=0, keepdims=True)
         gp[2] = gv
+        if t < 3:
+            for copy in ins(after, (1, 2)):
+                copy.start()
         if t == 1:
             line_arrive(g_all, 1, z, s, f, line)
             line_step(g_all, 2, z, s, f, line)
             new_blocks(2, z, lambda v: swap(v).start())
+        if t < 2:
+            swap(after).wait_recv()
+            for copy in load_x(after):
+                copy.start()
+        if t == 1:
             line_sum_step(1, *reduce_args)
-        if t == 2:
-            line_sum_step(2, *reduce_args)
         if t == 3:
+            row_sums.step2(4)
+            row_sums.step3(3)
+            row_sums.step4(1)
             line_sum_end(*reduce_args)
             back.start()
 
@@ -1346,12 +1513,24 @@
     for b in range(4):
         swap(b).wait_send()
         send_sib(b).wait_recv()
+    line_sum_step(0, z, s, f, own_o, sib_o, land_u, stage, rs_out, load.at[pl.ds(8, 3)], u_send, u_recv)
+    row_sums.step3(4)
+    row_sums.step4(2)
+    row_sums.step4(3)
+    row_sums.step4(4)
+    back.wait()
     for k in (1, 2):
         line_sent(g_all, k, z, s, f, line)
-    back.wait()
-
-
-def backward_call(g_part, w_in, w_out, slope, qkv, lse, p_own, p_sib, gain, cos4, sin4, ids_col, ids_row):
+    for j in range(5):
+        row_sums.finish(j)
+    for way in range(2):
+        to = f - 2 if way == 0 else f + 2
+        copy = remote(rs_out.at[way], land_u.at[way, 0], u_send.at[way, 0], u_recv.at[way, 0], s, to)
+        pl.when(z == (3 if way == 0 else 0))(copy.wait_send)
+        pl.when(z == (2 if way == 0 else 1))(copy.wait_recv)
+
+
+def backward_call(g_part, a_all, w_in, w_out, slope, qkv, lse, p_own, p_sib, gain, cos4, sin4, ids_col, ids_row):
     width = w_in.shape[1]
     units = w_in.shape[0] - 768
     anys = pl.BlockSpec(memory_space=pl.ANY)
@@ -1360,12 +1539,13 @@
     dma = lambda *n: pltpu.SemaphoreType.DMA(n)
     return pl.pallas_call(
         backward_body,
-        in_specs=[anys] * 8 + [vmem] * 5,
-        out_specs=[anys] * 6 + [vmem],
+        in_specs=[anys] * 9 + [vmem] * 5,
+        out_specs=[anys] * 9 + [vmem],
         out_shape=[
             shape((4, TOK, width), bf), shape((4, TOK, units + 768), bf),
             shape((4, HALF, width), bf), shape((4, HALF, width), bf), shape((HALF, width), bf),
-            shape((2, 3, HALF, width), bf), shape((8, 256), f32),
+            shape((2, 3, HALF, width), bf), shape((2, 1, HALF, width), bf), shape((1024, width), bf),
+            shape((256, width), bf), shape((8, 256), f32),
         ],
         input_output_aliases={0: 0},
         scratch_shapes=[
@@ -1376,40 +1556,49 @@
             pltpu.VMEM((HALF, width), bf), pltpu.VMEM((HALF, width), bf),
             pltpu.VMEM((3, HALF, width), bf), pltpu.VMEM((2, HALF, width), bf),
             pltpu.VMEM((TOK, LANES), f32), pltpu.VMEM((TOK, LANES), f32),
+            pltpu.VMEM((5, 256, width), bf), pltpu.VMEM((5, 2, 64, width), bf), pltpu.VMEM((5, 2, 32, width), bf),
+            pltpu.VMEM((3, HALF, 256), bf), pltpu.VMEM((256, width), f32),
             dma(11), dma(3), dma(3), dma(3), dma(3), dma(4), dma(4), dma(4), dma(4), dma(5),
-            dma(2, 3), dma(2, 3), dma(4), dma(4),
+            dma(2, 3), dma(2, 3), dma(4), dma(4), dma(3, 2), *[dma(5, 2)] * 9, dma(2, 3), dma(2, 3),
         ],
         compiler_params=pltpu.CompilerParams(
-            vmem_limit_bytes=62 * 1024 * 1024, collective_id=1, has_side_effects=True
+            vmem_limit_bytes=63 * 1024 * 1024, collective_id=1, has_side_effects=True
         ),
         cost_estimate=cost(8 * TOK * width * (w_in.shape[0] + w_out.shape[0]), 200e6),
         name="backward",
-    )(g_part, w_in, w_out, slope, qkv, lse, p_own, p_sib, gain, cos4, sin4, ids_col, ids_row)
-
-
-PAIRS = 12
+    )(g_part, a_all, w_in, w_out, slope, qkv, lse, p_own, p_sib, gain, cos4, sin4, ids_col, ids_row)
+
+
+PAIRS = 7
 
 
 def tail_body(
-    a_all, b_all, g_all, n_all, plain, u_own, u_sib, gain, shift, wide_in, more_in,
-    fin_up, fin_down, fin_out, fin_qkv, u_o, small_o, land,
+    b_all, n_all, plain, u_own, u_sib, early, gain, shift, wide_in, more_in,
+    fin_up, fin_qkv, u_o, small_o, land,
     term, r1, r2, hop, stage, rs_out, left, right, acc, acc_s, weight, sides, wide, more, got, small,
     load, w_sem, r1_s, r1_r, r2_s, r2_r, hop_s, hop_r, r3_s, r3_r, r4_s, r4_r,
     rs_load, rs_send, rs_recv, pb_s, pb_r, sm_s, sm_r, sq_s, sq_r, own_sems, self_sem,
 ):
     s, f = lax.axis_index("seq"), lax.axis_index("fsdp")
     z = f // 2
-    x, y = s % 2, s // 2
-    across = (s + 1 - 2 * x, (s + 2) % 4)
     reduce_args = (z, s, f, u_own, u_sib, land, stage, rs_out, rs_load, rs_send, rs_recv)
-    column = [4, 5, 6, 0, 1, 2, 3, 0, 1, 2, 3, 4]
+    column = [4, 5, 6, 0, 1, 2, 3]
+
+    def result(j, start, count):
+        if j < 3:
+            return fin_qkv.at[SeqSum.rows(256 * j + start, count)]
+        return fin_up.at[SeqSum.rows(256 * (j - 3) + start, count)]
+
+    sums = SeqSum(
+        term, r1, r2, (r1_s, r1_r, r2_s, r2_r, r3_s, r3_r, r4_s, r4_r), own_sems, result, s, f
+    )
+    across = sums.across
 
     def loads(j, k):
-        rows_of, right_of = (b_all, n_all) if j < 7 else (a_all, g_all)
         slot = k % 2
         return (
-            pltpu.make_async_copy(rows_of.at[k, :, pl.ds(256 * column[j], 256)], left.at[slot], load.at[slot, 0]),
-            pltpu.make_async_copy(right_of.at[k], right.at[slot], load.at[slot, 1]),
+            pltpu.make_async_copy(b_all.at[k, :, pl.ds(256 * column[j], 256)], left.at[slot], load.at[slot, 0]),
+            pltpu.make_async_copy(n_all.at[k], right.at[slot], load.at[slot, 1]),
         )
 
     def weights(j):
@@ -1423,8 +1612,7 @@
     more[...] = more_in[...]
 
     def compute(j):
-        if j < 7:
-            weights(j).start()
+        weights(j).start()
 
         @pl.loop(0, 4)
         def _(k):
@@ -1445,139 +1633,64 @@
             for copy in loads(j, k):
                 copy.wait()
             part = tn(left[slot], right[slot])
+            part_s = tn(left[slot], jnp.ones((TOK, LANES), bf))
 
             @pl.when(k == 0)
             def _():
                 acc[...] = part
+                acc_s[...] = part_s
 
             @pl.when(k > 0)
             def _():
                 acc[...] += part
-
-            if j < 7:
-                part_s = tn(left[slot], jnp.ones((TOK, LANES), bf))
-
-                @pl.when(k == 0)
-                def _():
-                    acc_s[...] = part_s
-
-                @pl.when(k > 0)
-                def _():
-                    acc_s[...] += part_s
-
-        if j < 7:
-            which = 1 if j < 3 else 0
-            weights(j).wait()
-            raw, total = acc[...], acc_s[:, 0:1]
-            term[j] = (raw * gain[which : which + 1, :] + total * shift[which : which + 1, :]).astype(bf)
-            low_w = weight[...].astype(f32)
-            sides[2 * which : 2 * which + 1, :] += jnp.sum(low_w * raw, axis=0, keepdims=True)
-            sides[2 * which + 1 : 2 * which + 2, :] += jnp.sum(low_w * total, axis=0, keepdims=True)
-            if j >= 3:
-                row = jnp.transpose(acc_s[...])
-                for half in range(2):
-                    at = 2 * (j - 3) + half
-                    more[at : at + 1, :] = row[0:1, 128 * half : 128 * half + 128]
-        else:
-            term[j] = acc[...].astype(bf)
-
-    def rows(start, count):
-        return pl.ds(pl.multiple_of(start, 32), count)
-
-    ways = ((0, x, y), (1, y, x))
-
-    def base(p, a, b):
-        return 128 * p + 64 * a + 32 * b
-
-    def result(i, start, count):
-        if i < 4:
-            return fin_up.at[rows(256 * i + start, count)]
-        if i < 8:
-            return fin_down.at[rows(256 * (i - 4) + start, count)]
-        if i < 9:
-            return fin_out.at[rows(start, count)]
-        return fin_qkv.at[rows(256 * (i - 9) + start, count)]
-
-    def send1(j, p, a):
-        return remote(
-            term.at[j, rows(128 * p + 64 * (1 - a), 64)], r1.at[j, p], r1_s.at[j, p], r1_r.at[j, p], across[p], f
-        )
-
-    def send2(j, p, a, b):
-        return remote(
-            term.at[j, rows(base(p, a, 1 - b), 32)], r2.at[j, p], r2_s.at[j, p], r2_r.at[j, p], across[1 - p], f
-        )
-
-    def keep3(i, p, a, b):
-        return pltpu.make_async_copy(
-            term.at[i + 3, rows(base(p, a, b), 32)], result(i, base(p, a, b), 32), own_sems.at[i, p]
-        )
-
-    def send3(i, p, a, b):
-        ref = result(i, base(p, a, b), 32)
-        src = term.at[i + 3, rows(base(p, a, b), 32)] if i < 9 else ref
-        return remote(src, ref, r3_s.at[i, p], r3_r.at[i, p], across[1 - p], f)
-
-    def send4(i, p, a):
-        ref = result(i, 128 * p + 64 * a, 64)
-        return remote(ref, ref, r4_s.at[i, p], r4_r.at[i, p], across[p], f)
+                acc_s[...] += part_s
+
+        which = 1 if j < 3 else 0
+        weights(j).wait()
+        raw, total = acc[...], acc_s[:, 0:1]
+        term[j] = (raw * gain[which : which + 1, :] + total * shift[which : which + 1, :]).astype(bf)
+        low_w = weight[...].astype(f32)
+        sides[2 * which : 2 * which + 1, :] += jnp.sum(low_w * raw, axis=0, keepdims=True)
+        sides[2 * which + 1 : 2 * which + 2, :] += jnp.sum(low_w * total, axis=0, keepdims=True)
+        if j >= 3:
+            row = jnp.transpose(acc_s[...])
+            for half in range(2):
+                at = 2 * (j - 3) + half
+                more[at : at + 1, :] = row[0:1, 128 * half : 128 * half + 128]
 
     def owner(j):
         head = 8 * j + f
         return head // 3, head % 3
 
     def hop_place(i, p, a, b):
-        return fin_qkv.at[rows(256 * i + base(p, a, b), 32)]
+        return fin_qkv.at[SeqSum.rows(256 * i + SeqSum.base(p, a, b), 32)]
 
     def send_hop(j, p, a, b):
         to, i = owner(j)
         return remote(hop.at[j, p], hop_place(i, p, a, b), hop_s.at[j, p], hop_r.at[i, p], s, to)
 
     def keep_hop(j, p, a, b):
-        return pltpu.make_async_copy(hop.at[j, p], hop_place(owner(j)[1], p, a, b), own_sems.at[9 + j, p])
-
-    def step1(j):
-        for p, a, b in ways:
-            send1(j, p, a).start()
-
-    def step2(j):
-        for p, a, b in ways:
-            send1(j, p, a).wait_recv()
-            at = rows(128 * p + 64 * a, 64)
-            term[j, at, :] = (term[j, at, :].astype(f32) + r1[j, p].astype(f32)).astype(bf)
-            send2(j, p, a, b).start()
+        return pltpu.make_async_copy(hop.at[j, p], hop_place(owner(j)[1], p, a, b), own_sems.at[j, p])
 
     def step3(j):
-        for p, a, b in ways:
-            send2(j, p, a, b).wait_recv()
-            at = rows(base(p, a, b), 32)
-            total = (term[j, at, :].astype(f32) + r2[j, p].astype(f32)).astype(bf)
-            if j >= 3:
-                term[j, at, :] = total
-                send3(j - 3, p, a, b).start()
-                keep3(j - 3, p, a, b).start()
-            else:
-                hop[j, p] = total
-                here = owner(j)[0] == f
-                pl.when(here)(keep_hop(j, p, a, b).start)
-                pl.when(jnp.logical_not(here))(send_hop(j, p, a, b).start)
+        if j >= 3:
+            sums.step3(j)
+            return
+        for p, a, b in sums.ways:
+            hop[j, p] = sums.total(j, p, a, b)
+            here = owner(j)[0] == f
+            pl.when(here)(keep_hop(j, p, a, b).start)
+            pl.when(jnp.logical_not(here))(send_hop(j, p, a, b).start)
 
     def step3_own(i):
         head, kind = (3 * f + i) % 8, (3 * f + i) // 8
-        for p, a, b in ways:
+        for p, a, b in sums.ways:
             ref = hop_place(i, p, a, b)
             coming = remote(ref, ref, hop_s.at[i, p], hop_r.at[i, p], s, head)
-            staying = pltpu.make_async_copy(ref, ref, own_sems.at[9 + kind, p])
+            staying = pltpu.make_async_copy(ref, ref, own_sems.at[kind, p])
             pl.when(head != f)(coming.wait_recv)
             pl.when(head == f)(staying.wait)
-            send3(9 + i, p, a, b).start()
-
-    def step4(i):
-        for p, a, b in ways:
-            send3(i, p, a, b).wait_recv()
-            if i < 9:
-                keep3(i, p, a, b).wait()
-            send4(i, p, a).start()
+            sums.send3(i, p, a, b, False).start()
 
     def small_send(step):
         to = (f + step) % 8
@@ -1613,60 +1726,52 @@
         small_seq(1).wait_recv()
         small_o[...] = small[2] + small[3]
 
-    back = PlaneBack(stage.at[0], u_o, s, f, pb_s, pb_r, self_sem)
+    back = PlaneBack(stage.at[2], u_o, s, f, pb_s, pb_r, self_sem)
+    line_sum_step(1, *reduce_args, early.at[:, 0])
     compute(0)
-    step1(0)
-    line_sum_step(0, *reduce_args)
+    sums.step1(0)
     compute(1)
-    step1(1)
-    for it in range(1, 16):
+    sums.step1(1)
+    for it in range(1, 10):
         if it + 1 < PAIRS:
             compute(it + 1)
-            step1(it + 1)
+            sums.step1(it + 1)
         if it - 1 < PAIRS:
-            step2(it - 1)
+            sums.step2(it - 1)
         if 0 <= it - 2 < PAIRS:
             step3(it - 2)
+        if it == 4:
+            line_sum_step(2, *reduce_args)
         if 5 <= it < 8:
             step3_own(it - 5)
-        if 0 <= it - 6 < 9:
-            step4(it - 6)
+        if 3 <= it - 3 < PAIRS:
+            sums.step4(it - 3)
         if 6 <= it < 9:
-            step4(9 + it - 6)
-        if it == 4:
-            line_sum_step(1, *reduce_args)
+            sums.step4(it - 6, False)
+        if it == 6:
+            small_one()
         if it == 7:
-            line_sum_step(2, *reduce_args)
+            small_two()
         if it == 8:
-            small_one()
-        if it == 10:
-            small_two()
-        if it == 11:
+            small_three()
             line_sum_end(*reduce_args)
             back.start()
-        if it == 12:
-            small_three()
-        if it == 14:
-            small_four()
-
-    back.wait()
+
+    small_four()
     for j in range(PAIRS):
-        for p, a, b in ways:
-            send4(j, p, a).wait_recv()
-            send1(j, p, a).wait_send()
-            send2(j, p, a, b).wait_send()
-            send3(j, p, a, b).wait_send()
-            send4(j, p, a).wait_send()
-            if j < 3:
-                pl.when(owner(j)[0] != f)(send_hop(j, p, a, b).wait_send)
+        sums.finish(j)
+    for j in range(3):
+        for p, a, b in sums.ways:
+            pl.when(owner(j)[0] != f)(send_hop(j, p, a, b).wait_send)
 
     for step in range(1, 8):
         small_send(step).wait_send()
     for way in range(2):
         small_seq(way).wait_send()
-
-
-def tail_call(a_all, b_all, g_all, n_all, plain, u_own, u_sib, gain, shift, wide, more):
+    back.wait()
+
+
+def tail_call(b_all, n_all, plain, u_own, u_sib, early, gain, shift, wide, more):
     width = plain.shape[1]
     anys = pl.BlockSpec(memory_space=pl.ANY)
     vmem = pl.BlockSpec(memory_space=pltpu.VMEM)
@@ -1675,10 +1780,10 @@
     two = [dma(PAIRS, 2)] * 2
     return pl.pallas_call(
         tail_body,
-        in_specs=[anys] * 7 + [vmem] * 4,
-        out_specs=[anys] * 5 + [vmem, anys],
+        in_specs=[anys] * 6 + [vmem] * 4,
+        out_specs=[anys] * 3 + [vmem, anys],
         out_shape=[
-            shape((1024, width), bf), shape((1024, width), bf), shape((256, width), bf), shape((768, width), bf),
+            shape((1024, width), bf), shape((768, width), bf),
             shape((HALF, width), bf), shape((32, LANES), f32), shape((2, 3, HALF, width), bf),
         ],
         scratch_shapes=[
@@ -1698,7 +1803,7 @@
         ),
         cost_estimate=cost(1e11, 600e6),
         name="tail",
-    )(a_all, b_all, g_all, n_all, plain, u_own, u_sib, gain, shift, wide, more)
+    )(b_all, n_all, plain, u_own, u_sib, early, gain, shift, wide, more)
 
 
 def pick(slices, which):
@@ -1740,7 +1845,7 @@
     packed = jnp.pad(packed, (0, 40 * LANES - packed.shape[0])).reshape(40, LANES)
     flat = resid_in.reshape(tokens, width)
     grad_flat = grad_out.reshape(tokens, width)
-    own_n, g_low, head_half, small = entry_call(flat, grad_flat, qkv_weight, packed)
+    own_n, g_low, head_half, small, bias_sum = entry_call(flat, grad_flat, qkv_weight, packed)
     small = small.reshape(8, 40 * LANES)
     gain_a, shift_a, gain_m, shift_m, bias_out = (
         small[:, i * 256 : (i + 1) * 256].reshape(width) for i in range(5)
@@ -1776,22 +1881,22 @@
         own_n, g_low, head_half, up_weight, down_weight, out_weight, bias_in, gain, shift,
         cosine, sine, ids_col, ids_row,
     )
-    g_all, b_all, u_own, u_sib, branch, _, col_sums = backward_call(
-        g_part, w_in, w_out, slope_all, qkv_all, lse_all, p_own, p_sib, gain, cosine, sine, ids_col, ids_row
+    _, b_all, u_own, u_sib, branch, _, early, down_low, out_low, col_sums = backward_call(
+        g_part, a_all, w_in, w_out, slope_all, qkv_all, lse_all, p_own, p_sib, gain, cosine, sine, ids_col, ids_row
     )
     result = flat + branch.astype(f32) + bias_out
 
     slots = jnp.zeros((16, HEAD_DIM), f32)
     slots = lax.dynamic_update_slice(slots, col_sums[0:1], (f, 0))
     slots = lax.dynamic_update_slice(slots, col_sums[1:2], (8 + f, 0))
-    spread = jnp.concatenate([jnp.zeros((4, width), f32), jnp.sum(grad_flat, axis=0)[None]])
+    spread = jnp.concatenate([jnp.zeros((4, width), f32), bias_sum])
     wide = jnp.concatenate(
         [spread.reshape(5, 8, 256).transpose(1, 0, 2).reshape(8, 5 * 256), slots.reshape(8, 512)], axis=1
     )
     wide = jnp.pad(wide, ((0, 0), (0, 256))).reshape(8, 16, LANES)
     more = jnp.pad(jnp.concatenate([jnp.zeros((units,), f32), col_sums[2]]), (0, 768)).reshape(16, LANES)
-    up_low, down_low, out_low, qkv_low, u, small_sum, _ = tail_call(
-        a_all, b_all, g_all, n_all, w_in, u_own, u_sib, gain, shift, wide, more
+    up_low, qkv_low, u, small_sum, _ = tail_call(
+        b_all, n_all, w_in, u_own, u_sib, early, gain, shift, wide, more
     )
     u = u.astype(f32)
     center = flat - jnp.mean(flat, axis=-1, keepdims=True)

time: 734 us -> 702 us (0.956)
  Pallas kernels: 665 us -> 640 us
    pallas_call x2, Pallas kernels: 442 us -> 413 us  [the longest x1 235 us: backward_call(): pl.pallas_call(backward_body, in_specs=[anys] * 9 + [vmem] * 5, out_specs...]
    unnamed x60 -> x52, local copies, waits for them, and re-layouts: 15 us -> 7.78 us
where the time goes in v5:
time: 702 us; the launch traced here: 690 us
  Pallas kernels  640 us (91%)
  other arithmetic  32.3 us (5%)
  local copies, waits for them, and re-layouts  15.4 us (2%)
    pallas_call x1, Pallas kernels, backward_call(): pl.pallas_call(backward_body, in_specs=[anys] * 9 + [vmem] * 5, out_specs...  235 us
    pallas_call x1, Pallas kernels, forward_call(): pl.pallas_call(forward_body, in_specs=[anys] * 6 + [vmem] * 7, out_specs=...  195 us
    pallas_call x1, Pallas kernels, tail_call(): pl.pallas_call(tail_body, in_specs=[anys] * 6 + [vmem] * 4, out_specs=[an...  177 us
    pallas_call x1, Pallas kernels, entry_call(): pl.pallas_call(entry_body, in_specs=[anys] * 3 + [vmem], out_specs=[anys]...  32.5 us

profile of v5, /device:TPU:0, one launch (start us, length us, event | category | flops | bytes accessed | tf_op | source)
XLA Modules:
  0.0 689.9 jit_solution(14628465128410339972)
XLA Ops:
  0.9 0.7 constant_dynamic-update-slice_fusion.15
  1.6 0.7 constant_dynamic-update-slice_fusion.10
  2.2 0.7 constant_dynamic-update-slice_fusion.5
  2.9 0.7 constant_dynamic-update-slice_fusion
  3.6 0.7 constant_dynamic-update-slice_fusion.38
  4.3 0.7 constant_dynamic-update-slice_fusion.37
  5.0 0.7 convert_bitcast_fusion
  5.7 0.7 convert_element_type.62
  7.1 32.5 %entry.1 = (bf16[512,2048]{1,0:T(8,128)(2,1)}, bf16[512,2048]{1,0:T(8,128)(2,1)}, bf16[3,128,2048]{2,1,0:T(8,128)(2,1)}, f32[8,40,128]{2,1,0:T(8,128)}, f32[1,2048]{1,0:T(1,128)}) custom-call(f32[512,2048]{1,0:T(8,128)} %bitcast.229, f32[512,2048]{1,0:T(8,128)} %bitcast.230, f32[768,2048]{1,0:T(8,128)} %qkv.1, f32[40,128]{1,0:T(8,128)} %pad_bitcast_fusion.packed), custom_call_target="tpu_custom_call" | custom-call | flops 10000000 | bytes 20000000 | tf_op jit(solution)/shard_map/entry/pallas_call | solution.py:1111
  39.6 1.0 copy.56
  40.9 2.0 copy.37.idc
  43.5 3.4 fusion.4
  49.4 195.2 %forward.1 = (bf16[4,1024,2048]{2,1,0:T(8,128)(2,1)}, bf16[4,1024,2048]{2,1,0:T(8,128)(2,1)}, bf16[1792,2048]{1,0:T(8,128)(2,1)}, bf16[1280,2048]{1,0:T(8,128)(2...) custom-call(bf16[512,2048]{1,0:T(8,128)(2,1)} %get-tuple-element.42., ...), custom_call_target="tpu_custom_call" | custom-call | flops 51539607552 | bytes 200000000 | tf_op jit(solution)/shard_map/forward/pallas_call | solution.py:989
  244.7 235.2 %backward.1 = (bf16[4,1024,2048]{2,1,0:T(8,128)(2,1)}, bf16[4,1024,1792]{2,1,0:T(8,128)(2,1)}, bf16[4,512,2048]{2,1,0:T(8,128)(2,1)}, bf16[4,512,2048]{2,1,0:T(8...) custom-call(bf16[4,1024,2048]{2,1,0:T(8,128)(2,1)} %get-tuple-elemen, ...), custom_call_target="tpu_custom_call", output_to_operand_aliasing={{0}: (0, {})} | custom-call | flops 51539607552 | bytes 200000000 | tf_op jit(solution)/shard_map/backward/pallas_call | solution.py:1540
  479.9 0.8 fusion.45
  482.3 177.5 %tail.1 = (bf16[1024,2048]{1,0:T(8,128)(2,1)}, bf16[768,2048]{1,0:T(8,128)(2,1)}, bf16[512,2048]{1,0:T(8,128)(2,1)}, f32[32,128]{1,0:T(8,128)}, bf16[2,3,512,2048]{3,2,1,0:T(8,128)(2,1)}) custom-call(bf16[4,1024,1792]{2,1,0:T(8,128)(2,1)} %get-tuple-element.56.b_all, bf16[4,1024,2048]{2,1,0:T(8,128)(2,1)} %get-tuple-element.57.n_all, ...), custom_call_target="tpu_custom_call" | custom-call | flops 99999997952 | bytes 600000000 | tf_op jit(solution)/shard_map/tail/pallas_call | solution.py:1781
  659.8 2.6 reduce_sum.49
  662.4 2.9 multiply_reduce_fusion
  665.9 1.6 convert_reduce_fusion
  668.2 4.9 fusion.2
  673.1 4.4 convert_element_type.72
  677.6 3.5 convert_element_type.70
  682.9 4.4 convert_element_type.73
  687.3 1.5 convert_element_type.71
  (96 shorter events, 9.2 us)
Async XLA Ops:
  39.6 9.2 %copy-start.12 = (f32[1024]{0:T(1024)S(1)}, f32[1024]{0:T(1024)}, u32[]{:S(2)}) copy-start(f32[1024]{0:T(1024)} %param.22) | copy-start | bytes 12292
  244.7 236.3 %copy-start.10 = (f32[1,2048]{1,0:T(1,128)S(1)}, f32[1,2048]{1,0:T(1,128)}, u32[]{:S(2)}) copy-start(f32[1,2048]{1,0:T(1,128)} %get-tuple-element.61) | copy-start | bytes 24580
  659.7 5.6 copy-start.2
  662.4 3.5 copy-start
  665.3 2.2 copy-start.8
  665.3 2.3 copy-start.1
  665.3 2.9 copy-start.6
  668.2 4.9 copy-start.4
  673.1 4.4 copy-start.5
  677.6 3.5 copy-start.9
  677.6 5.3 copy-start.3
  681.7 7.2 %copy-start.11 = (f32[256]{0:T(256)}, f32[256]{0:T(256)S(1)}, u32[]{:S(2)}) copy-start(f32[256]{0:T(256)S(1)} %get-tuple-element.164) | copy-start | bytes 3076
  682.9 4.5 copy-start.7

commit v6 on v5

--- a/solution.py
+++ b/solution.py
@@ -860,6 +860,15 @@
     def send_sib(b):
         return remote(p_sib, sib_o.at[b], core_p[0].at[b], core_p[1].at[b], s, f + 1 - 2 * (f % 2))
 
+    def pass_on(t):
+        line_arrive(n_all, t - 1, z, s, f, line_n)
+        if t < 3:
+            line_step(n_all, t, z, s, f, line_n)
+        else:
+            spread.arrive()
+            line_step(g_all, 0, z, s, f, line_g)
+        new_blocks(t, z, lambda v: core_copy(n_all, v, s, f, core_n).start())
+
     for t in range(4):
         b = line_order(z, t)
         low_half = pltpu.make_async_copy(n_all.at[b, other], x.at[other], load.at[9])
@@ -879,13 +888,8 @@
             for copy in first[1:]:
                 copy.wait()
         else:
-            line_arrive(n_all, t - 1, z, s, f, line_n)
-            if t < 3:
-                line_step(n_all, t, z, s, f, line_n)
-            else:
-                spread.arrive()
-                line_step(g_all, 0, z, s, f, line_g)
-            new_blocks(t, z, lambda v: core_copy(n_all, v, s, f, core_n).start())
+            if t > 1:
+                pass_on(t)
             top = pltpu.make_async_copy(n_all.at[b, own], x.at[own], load.at[0])
             top.start()
         if t == 1:
@@ -949,6 +953,9 @@
             probs = (weights / total).astype(bf)
             mixed[rows, :] = nn(probs, qkv[2]).astype(bf)
             lse[rows, :] = jnp.broadcast_to(top_score + jnp.log(total), (256, LANES))
+
+        if t == 0:
+            pass_on(1)
 
         @pl.loop(0, p_own.shape[1] // 256)
         def _(j):

time: 702 us -> 702 us (level)
  no operation moved by 1% of the time
where the time goes in v6:
time: 702 us; the launch traced here: 690 us
  Pallas kernels  640 us (91%)
  other arithmetic  32.3 us (5%)
  local copies, waits for them, and re-layouts  15.4 us (2%)
    pallas_call x1, Pallas kernels, backward_call(): pl.pallas_call(backward_body, in_specs=[anys] * 9 + [vmem] * 5, out_specs...  235 us
    pallas_call x1, Pallas kernels, forward_call(): pl.pallas_call(forward_body, in_specs=[anys] * 6 + [vmem] * 7, out_specs=...  195 us
    pallas_call x1, Pallas kernels, tail_call(): pl.pallas_call(tail_body, in_specs=[anys] * 6 + [vmem] * 4, out_specs=[an...  177 us
    pallas_call x1, Pallas kernels, entry_call(): pl.pallas_call(entry_body, in_specs=[anys] * 3 + [vmem], out_specs=[anys]...  32.5 us

profile of v6, /device:TPU:0, one launch (start us, length us, event | category | flops | bytes accessed | tf_op | source)
XLA Modules:
  0.0 689.9 jit_solution(2716939856495087578)
XLA Ops:
  0.9 0.7 constant_dynamic-update-slice_fusion.15
  1.6 0.7 constant_dynamic-update-slice_fusion.10
  2.2 0.7 constant_dynamic-update-slice_fusion.5
  2.9 0.7 constant_dynamic-update-slice_fusion
  3.6 0.7 constant_dynamic-update-slice_fusion.38
  4.3 0.7 constant_dynamic-update-slice_fusion.37
  5.0 0.7 convert_bitcast_fusion
  5.7 0.7 convert_element_type.62
  7.1 32.5 %entry.1 = (bf16[512,2048]{1,0:T(8,128)(2,1)}, bf16[512,2048]{1,0:T(8,128)(2,1)}, bf16[3,128,2048]{2,1,0:T(8,128)(2,1)}, f32[8,40,128]{2,1,0:T(8,128)}, f32[1,2048]{1,0:T(1,128)}) custom-call(f32[512,2048]{1,0:T(8,128)} %bitcast.229, f32[512,2048]{1,0:T(8,128)} %bitcast.230, f32[768,2048]{1,0:T(8,128)} %qkv.1, f32[40,128]{1,0:T(8,128)} %pad_bitcast_fusion.packed), custom_call_target="tpu_custom_call" | custom-call | flops 10000000 | bytes 20000000 | tf_op jit(solution)/shard_map/entry/pallas_call | solution.py:1118
  39.6 1.0 copy.56
  40.9 2.0 copy.37.idc
  43.5 3.4 fusion.4
  49.4 195.2 %forward.1 = (bf16[4,1024,2048]{2,1,0:T(8,128)(2,1)}, bf16[4,1024,2048]{2,1,0:T(8,128)(2,1)}, bf16[1792,2048]{1,0:T(8,128)(2,1)}, bf16[1280,2048]{1,0:T(8,128)(2...) custom-call(bf16[512,2048]{1,0:T(8,128)(2,1)} %get-tuple-element.42., ...), custom_call_target="tpu_custom_call" | custom-call | flops 51539607552 | bytes 200000000 | tf_op jit(solution)/shard_map/forward/pallas_call | solution.py:996
  244.7 235.2 %backward.1 = (bf16[4,1024,2048]{2,1,0:T(8,128)(2,1)}, bf16[4,1024,1792]{2,1,0:T(8,128)(2,1)}, bf16[4,512,2048]{2,1,0:T(8,128)(2,1)}, bf16[4,512,2048]{2,1,0:T(8...) custom-call(bf16[4,1024,2048]{2,1,0:T(8,128)(2,1)} %get-tuple-elemen, ...), custom_call_target="tpu_custom_call", output_to_operand_aliasing={{0}: (0, {})} | custom-call | flops 51539607552 | bytes 200000000 | tf_op jit(solution)/shard_map/backward/pallas_call | solution.py:1547
  479.9 0.8 fusion.45
  482.3 177.5 %tail.1 = (bf16[1024,2048]{1,0:T(8,128)(2,1)}, bf16[768,2048]{1,0:T(8,128)(2,1)}, bf16[512,2048]{1,0:T(8,128)(2,1)}, f32[32,128]{1,0:T(8,128)}, bf16[2,3,512,2048]{3,2,1,0:T(8,128)(2,1)}) custom-call(bf16[4,1024,1792]{2,1,0:T(8,128)(2,1)} %get-tuple-element.56.b_all, bf16[4,1024,2048]{2,1,0:T(8,128)(2,1)} %get-tuple-element.57.n_all, ...), custom_call_target="tpu_custom_call" | custom-call | flops 99999997952 | bytes 600000000 | tf_op jit(solution)/shard_map/tail/pallas_call | solution.py:1788
  659.8 2.6 reduce_sum.49
  662.4 2.9 multiply_reduce_fusion
  665.9 1.6 convert_reduce_fusion
  668.2 4.9 fusion.2
  673.1 4.4 convert_element_type.72
  677.6 3.5 convert_element_type.70
  682.9 4.4 convert_element_type.73
  687.3 1.5 convert_element_type.71
  (96 shorter events, 9.2 us)
Async XLA Ops:
  39.6 9.2 %copy-start.12 = (f32[1024]{0:T(1024)S(1)}, f32[1024]{0:T(1024)}, u32[]{:S(2)}) copy-start(f32[1024]{0:T(1024)} %param.22) | copy-start | bytes 12292
  244.7 236.3 %copy-start.10 = (f32[1,2048]{1,0:T(1,128)S(1)}, f32[1,2048]{1,0:T(1,128)}, u32[]{:S(2)}) copy-start(f32[1,2048]{1,0:T(1,128)} %get-tuple-element.61) | copy-start | bytes 24580
  659.7 5.6 copy-start.2
  662.4 3.5 copy-start
  665.3 2.2 copy-start.8
  665.3 2.3 copy-start.1
  665.3 2.9 copy-start.6
  668.2 4.9 copy-start.4
  673.1 4.4 copy-start.5
  677.6 3.5 copy-start.9
  677.6 5.3 copy-start.3
  681.7 7.2 %copy-start.11 = (f32[256]{0:T(256)}, f32[256]{0:T(256)S(1)}, u32[]{:S(2)}) copy-start(f32[256]{0:T(256)S(1)} %get-tuple-element.164) | copy-start | bytes 3076
  682.9 4.5 copy-start.7
